TPU v7x, 32 devices: a whole 2x2x4 slice. The times are simulated.
32 devices in a mesh: grp: 4 (over x, core), hub: 8 (over z, y).
Axes of the slice: x: 2, y: 2, z: 4, core: 2. Of those that a mesh axis runs over, the one named last changes fastest.
Arguments:
- embed: bfloat16 [262144, 128], P(('grp', 'hub')), may hold values from -6 to 6
- hub_ids: int32 [32, 4], P(('grp', 'hub')), may hold values from 0 to 63
- send_ids: int32 [32, 4, 4], P(('grp', 'hub')), may hold values from 0 to 63
- tile_row: int32 [32, 192], P(('grp', 'hub')), may hold values from 0 to 63
- tile_col: int32 [32, 192], P(('grp', 'hub')), may hold values from 0 to 111
- tile_val: bfloat16 [6144, 128, 128], P(('grp', 'hub')), may hold values from -0.3125 to 0.3125
- tile_count: int32 [32], P(('grp', 'hub')), may hold values from 96 to 192, as said below
Outputs:
- spectral: float32 [262144, 128], P(('grp', 'hub'))
Inputs may be any that keep to these rules, and one draw needn't show every extreme that they name: `tile_count`: each device has at least 96 live tile slots and some device has all 192 live; slots at or past a device's count are ignored.
All inputs are finite; a program needn't handle non-finite values.
Results may differ from a plain program's by a relative error of at most 0.0051.
Values may be sent and summed in bfloat16 or wider, within the bound.
No kernel may reach another device: no remote copies, remote signals or barrier semaphores. Data moves between devices by JAX's collectives and lax.ppermute only.
A program may use at most 128 MiB of HBM per device.

v0:
```python
import math

import jax
import jax.numpy as jnp
from jax import lax
from jax.sharding import PartitionSpec as P

ORDER = 4


SHIFT = 0.2
THETA = 3.0


def bessel_scaled(order_index):
    total = 0.0
    for term in range(40):
        total += (THETA / 2.0) ** (2 * term + order_index) / (
            math.factorial(term) * math.factorial(term + order_index)
        )
    return math.exp(-THETA) * total


def coefficients():
    values = [bessel_scaled(0)]
    for order_index in range(1, ORDER + 1):
        values.append(2.0 * (-1.0) ** order_index * bessel_scaled(order_index))
    return values


def shards(embed, hub_ids, send_ids, tile_row, tile_col, tile_val, tile_count):
    width = embed.shape[1]
    tile_size = tile_val.shape[1]
    nblocks = embed.shape[0] // tile_size
    slots = tile_val.shape[0]
    live = (jnp.arange(slots, dtype=jnp.int32) < tile_count[0]).astype(jnp.float32)
    row_list = tile_row[0]
    hub_list = hub_ids[0]
    send_list = send_ids[0].reshape(-1)
    col_list = tile_col[0]

    def apply(field):
        blocks = field.reshape(nblocks, tile_size, width)
        hub_local = blocks[hub_list].reshape(-1, width)
        hub_all = lax.all_gather(hub_local, "hub", axis=0, tiled=True)
        outgoing = blocks[send_list].reshape(-1, width)
        tail = lax.all_to_all(outgoing, "grp", split_axis=0, concat_axis=0, tiled=True)
        space = jnp.concatenate([field, hub_all, tail], axis=0).reshape(-1, tile_size, width)
        picked = space[col_list]
        prod = jnp.einsum("tij,tjk->tik", tile_val, picked, preferred_element_type=jnp.float32)
        masked = prod * live[:, None, None]
        summed = jax.ops.segment_sum(masked, row_list, num_segments=nblocks)
        return summed.reshape(nblocks * tile_size, width) - SHIFT * field.astype(jnp.float32)

    weights = coefficients()
    previous = embed
    spectral = weights[0] * previous.astype(jnp.float32)
    current = apply(previous).astype(jnp.bfloat16)
    spectral = spectral + weights[1] * current.astype(jnp.float32)
    for order_index in range(2, ORDER + 1):
        following = (2.0 * apply(current) - previous.astype(jnp.float32)).astype(jnp.bfloat16)
        spectral = spectral + weights[order_index] * following.astype(jnp.float32)
        previous, current = (current, following)
    return spectral


def solution(mesh):
    return jax.shard_map(
        shards,
        mesh=mesh,
        in_specs=(
            P(("grp", "hub"), None),
            P(("grp", "hub"), None),
            P(("grp", "hub"), None, None),
            P(("grp", "hub"), None),
            P(("grp", "hub"), None),
            P(("grp", "hub"), None, None),
            P(("grp", "hub")),
        ),
        out_specs=P(("grp", "hub"), None),
        check_vma=False,
    )
```

profile of v0, /device:TPU:0, one launch (start us, length us, event | category | flops | bytes accessed | tf_op | source)
XLA Modules:
  0.0 562.8 jit_solution(9080844696432089606)
XLA Ops:
  6.5 0.0 all-gather.5.cloned.1.call-start
  6.5 0.7 fusion.15
  7.2 2.8 gather_fusion
  10.0 0.0 all-gather.5.cloned.1.call-update
  10.0 0.8 reshape_squeeze.3
  10.8 3.0 gather_fusion.1
  13.8 4.2 all-to-all-start
  18.0 0.0 all-gather.7.cloned.1.call-start
  18.7 0.7 compare_select_fusion
  19.4 7.5 %all-to-all-done = bf16[4,512,128]{2,1,0:T(8,128)(2,1)S(1)} async-done(((bf16[4,512,128]{2,1,0:T(8,128)(2,1)}), bf16[4,512,128]{2,1,0:T(8,128)(2,1)S(1)}, u32[]{:S(2)}, u32[]{:S(2)}) %all-to-all-start) | async-done | bytes 524320 | tf_op jit(solution)/shard_map/all_to_all | solution.py:47
  26.9 26.1 %all-gather.5.cloned.1.call-done = bf16[4096,128]{1,0:T(8,128)(2,1)} async-done(((bf16[512,128]{1,0:T(8,128)(2,1)}), bf16[4096,128]{1,0:T(8,128)(2,1)}) %all-gather.5.cloned.1.call-update) | async-done | bytes 1048592 | tf_op jit(solution)/shard_map/all_gather | solution.py:45
  53.0 10.8 %pad_maximum_fusion = bf16[14336,128]{1,0:T(8,128)(2,1)} fusion(bf16[2048,128]{1,0:T(8,128)(2,1)S(1)} %bitcast.70, bf16[4096,128]{1,0:T(8,128)(2,1)} %all-gather.5.cloned.1.call-done, bf16[8192,128]{1,0:T(8,128)(2,1)} %param.7), kind=kLoop, calls=%fused_computation.46 | loop fusion | flops 11010048 | bytes 7340032 | tf_op jit(solution)/shard_map/concatenate | solution.py:48
  63.7 10.0 %gather_fusion.2 = bf16[192,128,128]{2,1,0:T(8,128)(2,1)} fusion(bf16[112,128,128]{2,1,0:T(8,128)(2,1)} %bitcast.65, s32[1024]{0:T(1024)S(1)} %pad_clamp_fusion), kind=kCustom, calls=%fused_computation.2 | custom fusion | bytes 12583680 | tf_op jit(solution)/shard_map/gather | solution.py:49
  73.7 13.8 %multiply_bitcast_fusion.3 = f32[192,128,128]{1,2,0:T(8,128)} fusion(f32[192]{0:T(256)S(1)} %compare_convert_fusion, bf16[192,128,128]{2,1,0:T(8,128)(2,1)} %gather_fusion.2, bf16[192,128,128]{2,1,0:T(8,128)(2,1)} %param.12), kind=kOutput, calls=%fused_computation.19 | convolution fusion | flops 808452096 | bytes 25166592 | tf_op jit(solution)/shard_map/tij,tjk->tik/dot_general | solution.py:50
  87.5 12.6 %copy.13 = f32[192,128,128]{2,1,0:T(8,128)} copy(f32[192,128,128]{1,2,0:T(8,128)} %multiply_bitcast_fusion.3) | data formatting | bytes 25165824 | tf_op jit(solution)/shard_map/mul | solution.py:51
  100.1 0.0 copy-start
  100.1 2.5 broadcast.77.clone
  102.6 0.0 copy-done
  102.6 39.1 %scatter_fusion = f32[64,128,128]{2,1,0:T(8,128)} fusion(f32[64,128,128]{2,1,0:T(8,128)} %broadcast.77.clone, s32[192]{0:T(256)S(1)} %bitcast.81, f32[192,128,128]{2,1,0:T(8,128)} %copy.13), kind=kCustom, calls=%fused_computation.12 | custom fusion | flops 3145728 | bytes 37749504 | tf_op jit(solution)/shard_map/scatter-add | solution.py:52
  141.8 3.4 fusion.7
  145.1 1.2 gather_fusion.3
  146.4 0.0 all-gather.7.cloned.1.call-update
  146.4 0.0 all-gather.9.cloned.1.call-start
  146.4 0.6 gather_fusion.4
  147.1 11.6 %all_to_all.48 = bf16[4,512,128]{2,1,0:T(8,128)(2,1)S(1)} all-to-all(bf16[4,512,128]{2,1,0:T(8,128)(2,1)S(1)} %bitcast.75), channel_id=1, replica_groups=mesh['grp'=4,'hub'=8] {'grp'}, dimensions={0} | all-to-all | bytes 1048576 | tf_op jit(solution)/shard_map/all_to_all | solution.py:47
  158.6 26.9 %all-gather.7.cloned.1.call-done = bf16[4096,128]{1,0:T(8,128)(2,1)} async-done(((bf16[512,128]{1,0:T(8,128)(2,1)}), bf16[4096,128]{1,0:T(8,128)(2,1)}) %all-gather.7.cloned.1.call-update) | async-done | bytes 1048592 | tf_op jit(solution)/shard_map/all_gather | solution.py:45
  185.6 14.1 %pad_maximum_fusion.1 = bf16[14336,128]{1,0:T(8,128)(2,1)} fusion(bf16[2048,128]{1,0:T(8,128)(2,1)S(1)} %bitcast.71, bf16[4096,128]{1,0:T(8,128)(2,1)} %all-gather.7.cloned.1.call-done, bf16[8192,128]{1,0:T(8,128)(2,1)S(1)} %fusion.7), kind=kLoop, calls=%fused_computation.47 | loop fusion | flops 11010048 | bytes 7340032 | tf_op jit(solution)/shard_map/concatenate | solution.py:48
  199.7 10.0 %gather_fusion.5 = bf16[192,128,128]{2,1,0:T(8,128)(2,1)} fusion(bf16[112,128,128]{2,1,0:T(8,128)(2,1)} %bitcast.66, s32[1024]{0:T(1024)S(1)} %pad_clamp_fusion), kind=kCustom, calls=%fused_computation.5 | custom fusion | bytes 12583680 | tf_op jit(solution)/shard_map/gather | solution.py:49
  209.7 13.8 %multiply_bitcast_fusion.2 = f32[192,128,128]{1,2,0:T(8,128)} fusion(f32[192]{0:T(256)S(1)} %compare_convert_fusion, bf16[192,128,128]{2,1,0:T(8,128)(2,1)} %gather_fusion.5, bf16[192,128,128]{2,1,0:T(8,128)(2,1)} %param.12), kind=kOutput, calls=%fused_computation.18 | convolution fusion | flops 808452096 | bytes 25166592 | tf_op jit(solution)/shard_map/tij,tjk->tik/dot_general | solution.py:50
  223.4 12.6 %copy.15 = f32[192,128,128]{2,1,0:T(8,128)} copy(f32[192,128,128]{1,2,0:T(8,128)} %multiply_bitcast_fusion.2) | data formatting | bytes 25165824 | tf_op jit(solution)/shard_map/mul | solution.py:51
  236.0 2.5 broadcast.77.clone.1
  238.6 38.9 %scatter_fusion.1 = f32[64,128,128]{2,1,0:T(8,128)} fusion(f32[64,128,128]{2,1,0:T(8,128)} %broadcast.77.clone.1, s32[192]{0:T(256)S(1)} %bitcast.82, f32[192,128,128]{2,1,0:T(8,128)} %copy.15), kind=kCustom, calls=%fused_computation.13 | custom fusion | flops 3145728 | bytes 37749504 | tf_op jit(solution)/shard_map/scatter-add | solution.py:52
  277.5 5.1 fusion.8
  282.6 2.8 gather_fusion.6
  285.4 0.0 all-gather.9.cloned.1.call-update
  285.4 0.0 all-gather.11.cloned.1.call-start
  285.5 2.2 gather_fusion.7
  287.7 20.8 %all_to_all.49 = bf16[4,512,128]{2,1,0:T(8,128)(2,1)S(1)} all-to-all(bf16[4,512,128]{2,1,0:T(8,128)(2,1)S(1)} %bitcast.76), channel_id=1, replica_groups=mesh['grp'=4,'hub'=8] {'grp'}, dimensions={0} | all-to-all | bytes 1048576 | tf_op jit(solution)/shard_map/all_to_all | solution.py:47
  308.5 16.1 %all-gather.9.cloned.1.call-done = bf16[4096,128]{1,0:T(8,128)(2,1)} async-done(((bf16[512,128]{1,0:T(8,128)(2,1)}), bf16[4096,128]{1,0:T(8,128)(2,1)}) %all-gather.9.cloned.1.call-update) | async-done | bytes 1048592 | tf_op jit(solution)/shard_map/all_gather | solution.py:45
  324.6 10.8 %pad_maximum_fusion.2 = bf16[14336,128]{1,0:T(8,128)(2,1)} fusion(bf16[2048,128]{1,0:T(8,128)(2,1)S(1)} %bitcast.72, bf16[4096,128]{1,0:T(8,128)(2,1)} %all-gather.9.cloned.1.call-done, bf16[8192,128]{1,0:T(8,128)(2,1)} %fusion.8), kind=kLoop, calls=%fused_computation.48 | loop fusion | flops 11010048 | bytes 7340032 | tf_op jit(solution)/shard_map/concatenate | solution.py:48
  335.4 10.0 %gather_fusion.8 = bf16[192,128,128]{2,1,0:T(8,128)(2,1)} fusion(bf16[112,128,128]{2,1,0:T(8,128)(2,1)} %bitcast.67, s32[1024]{0:T(1024)S(1)} %pad_clamp_fusion), kind=kCustom, calls=%fused_computation.8 | custom fusion | bytes 12583680 | tf_op jit(solution)/shard_map/gather | solution.py:49
  345.4 13.8 %multiply_bitcast_fusion.1 = f32[192,128,128]{1,2,0:T(8,128)} fusion(f32[192]{0:T(256)S(1)} %compare_convert_fusion, bf16[192,128,128]{2,1,0:T(8,128)(2,1)} %gather_fusion.8, bf16[192,128,128]{2,1,0:T(8,128)(2,1)} %param.12), kind=kOutput, calls=%fused_computation.17 | convolution fusion | flops 808452096 | bytes 25166592 | tf_op jit(solution)/shard_map/tij,tjk->tik/dot_general | solution.py:50
  359.1 12.6 %copy.17 = f32[192,128,128]{2,1,0:T(8,128)} copy(f32[192,128,128]{1,2,0:T(8,128)} %multiply_bitcast_fusion.1) | data formatting | bytes 25165824 | tf_op jit(solution)/shard_map/mul | solution.py:51
  371.7 2.5 broadcast.77.clone.2
  374.3 38.9 %scatter_fusion.2 = f32[64,128,128]{2,1,0:T(8,128)} fusion(f32[64,128,128]{2,1,0:T(8,128)} %broadcast.77.clone.2, s32[192]{0:T(256)S(1)} %bitcast.83, f32[192,128,128]{2,1,0:T(8,128)} %copy.17), kind=kCustom, calls=%fused_computation.14 | custom fusion | flops 3145728 | bytes 37749504 | tf_op jit(solution)/shard_map/scatter-add | solution.py:52
  413.2 5.1 fusion.11
  418.2 2.8 gather_fusion.9
  421.0 0.0 all-gather.11.cloned.1.call-update
  421.1 2.2 gather_fusion.10
  423.3 11.8 %all_to_all.50 = bf16[4,512,128]{2,1,0:T(8,128)(2,1)S(1)} all-to-all(bf16[4,512,128]{2,1,0:T(8,128)(2,1)S(1)} %bitcast.74), channel_id=1, replica_groups=mesh['grp'=4,'hub'=8] {'grp'}, dimensions={0} | all-to-all | bytes 1048576 | tf_op jit(solution)/shard_map/all_to_all | solution.py:47
  435.1 25.2 %all-gather.11.cloned.1.call-done = bf16[4096,128]{1,0:T(8,128)(2,1)} async-done(((bf16[512,128]{1,0:T(8,128)(2,1)}), bf16[4096,128]{1,0:T(8,128)(2,1)}) %all-gather.11.cloned.1.call-update) | async-done | bytes 1048592 | tf_op jit(solution)/shard_map/all_gather | solution.py:45
  460.3 10.8 %pad_maximum_fusion.3 = bf16[14336,128]{1,0:T(8,128)(2,1)} fusion(bf16[2048,128]{1,0:T(8,128)(2,1)S(1)} %bitcast.73, bf16[4096,128]{1,0:T(8,128)(2,1)} %all-gather.11.cloned.1.call-done, bf16[8192,128]{1,0:T(8,128)(2,1)} %fusion.11), kind=kLoop, calls=%fused_computation.49 | loop fusion | flops 11010048 | bytes 7340032 | tf_op jit(solution)/shard_map/concatenate | solution.py:48
  471.1 10.1 %gather_fusion.11 = bf16[192,128,128]{2,1,0:T(8,128)(2,1)} fusion(bf16[112,128,128]{2,1,0:T(8,128)(2,1)} %bitcast.64, s32[1024]{0:T(1024)S(1)} %pad_clamp_fusion), kind=kCustom, calls=%fused_computation.11 | custom fusion | bytes 12583680 | tf_op jit(solution)/shard_map/gather | solution.py:49
  481.1 13.7 %multiply_bitcast_fusion = f32[192,128,128]{1,2,0:T(8,128)} fusion(f32[192]{0:T(256)S(1)} %compare_convert_fusion, bf16[192,128,128]{2,1,0:T(8,128)(2,1)} %gather_fusion.11, bf16[192,128,128]{2,1,0:T(8,128)(2,1)} %param.12), kind=kOutput, calls=%fused_computation.16 | convolution fusion | flops 808452096 | bytes 25166592 | tf_op jit(solution)/shard_map/tij,tjk->tik/dot_general | solution.py:50
  494.8 12.6 %copy.19 = f32[192,128,128]{2,1,0:T(8,128)} copy(f32[192,128,128]{1,2,0:T(8,128)} %multiply_bitcast_fusion) | data formatting | bytes 25165824 | tf_op jit(solution)/shard_map/mul | solution.py:51
  507.4 2.5 broadcast.77
  509.8 39.5 %scatter_fusion.3 = f32[64,128,128]{2,1,0:T(8,128)} fusion(f32[64,128,128]{2,1,0:T(8,128)} %broadcast.77, s32[192]{0:T(256)S(1)} %bitcast.84, f32[192,128,128]{2,1,0:T(8,128)} %copy.19), kind=kCustom, calls=%fused_computation.15 | custom fusion | flops 3145728 | bytes 37749504 | tf_op jit(solution)/shard_map/scatter-add | solution.py:52
  549.3 6.6 %fusion.1 = f32[8192,128]{1,0:T(8,128)} fusion(bf16[8192,128]{1,0:T(8,128)(2,1)} %fusion.11, bf16[8192,128]{1,0:T(8,128)(2,1)} %param.7, bf16[8192,128]{1,0:T(8,128)(2,1)S(1)} %fusion.7, bf16[8192,128]{1,0:T(8,128)(2,1)} %fusion.8, f32[64,128,128]{2,1,0:T(8,128)} %scatter_fusion.3), kind=kLoop, calls=%fused_computation.32 | loop fusion | flops 19922944 | bytes 16777216 | tf_op jit(solution)/shard_map/add | solution.py:62
  (5 shorter events, 0.0 us)
Async XLA Ops:
  6.5 46.4 %all-gather.5.cloned.1.call-start = ((), (), s32[]{:S(2)}) async-start(), calls=%async_computation.4 | async-start | bytes 1179648 | tf_op jit(solution)/shard_map/all_gather | solution.py:45
  13.8 13.1 %all-to-all-start = ((bf16[4,512,128]{2,1,0:T(8,128)(2,1)}), bf16[4,512,128]{2,1,0:T(8,128)(2,1)S(1)}, u32[]{:S(2)}, u32[]{:S(2)}) async-start(bf16[4,512,128]{2,1,0:T(8,128)(2,1)} %bitcast.6), calls=%async_computation | async-start | bytes 1048576 | tf_op jit(solution)/shard_map/all_to_all | solution.py:47
  18.0 167.5 %all-gather.7.cloned.1.call-start = ((), (), s32[]{:S(2)}) async-start(), calls=%async_computation.5 | async-start | bytes 1179648 | tf_op jit(solution)/shard_map/all_gather | solution.py:45
  100.1 2.5 copy-start
  146.4 178.2 %all-gather.9.cloned.1.call-start = ((), (), s32[]{:S(2)}) async-start(), calls=%async_computation.6 | async-start | bytes 1179648 | tf_op jit(solution)/shard_map/all_gather | solution.py:45
  285.4 174.9 %all-gather.11.cloned.1.call-start = ((), (), s32[]{:S(2)}) async-start(), calls=%async_computation.7 | async-start | bytes 1179648 | tf_op jit(solution)/shard_map/all_gather | solution.py:45
Sparse Core Ops, SparseCore 0:
  10.1 42.7 all-gather.4
  146.5 38.9 all-gather.6
  285.5 38.9 all-gather.8
  421.2 39.0 all-gather.10
where the time goes:
time: 574 us; the launch traced here: 563 us
  other arithmetic  224 us (39%)
  local copies, waits for them, and re-layouts  119 us (21%)
  waiting for transfers between devices  102 us (18%)
  matrix products  55 us (10%)
  blocking collectives  44.1 us (8%)
  between operations  14.2 us (2%)
    scatter-add x4, other arithmetic, apply(): summed = jax.ops.segment_sum(masked, row_list, num_segments=nblocks)  156 us
    all_gather x4, waiting for transfers between devices, apply(): hub_all = lax.all_gather(hub_local, 'hub', axis=0, tiled=True)  94.3 us
    dot_general x4, matrix products, apply(): jnp.einsum('tij,tjk->tik', tile_val, picked, preferred_element_type=jnp.f...  55 us
    mul x4, local copies, waits for them, and re-layouts, apply(): masked = prod * live[:, None, None]  50.3 us
    concatenate x4, other arithmetic, apply(): jnp.concatenate([field, hub_all, tail], axis=0)  46.5 us
    all_to_all x3, blocking collectives, apply(): lax.all_to_all(outgoing, 'grp', split_axis=0, concat_axis=0, tiled=True)  44.1 us
    gather x4, local copies, waits for them, and re-layouts, apply(): picked = space[col_list]  40.1 us
  transfers between devices with their start and end apart: 5, of which 5 were waited for; matrix products, arithmetic and copies ran while one was open for 2% of the time, Pallas kernels for 0%

commit v1 on v0

v1 whole, which is shorter than its diff:
```python
import functools
import math

import jax
import jax.numpy as jnp
from jax import lax
from jax.experimental import pallas as pl
from jax.experimental.pallas import tpu as pltpu
from jax.sharding import PartitionSpec as P

ORDER = 4
SHIFT = 0.2
THETA = 3.0

UNROLL = 8
BITS = 10
MASK = (1 << BITS) - 1
F32 = jnp.float32
BF16 = jnp.bfloat16


def bessel_scaled(order_index):
    total = 0.0
    for term in range(40):
        total += (THETA / 2.0) ** (2 * term + order_index) / (
            math.factorial(term) * math.factorial(term + order_index)
        )
    return math.exp(-THETA) * total


def coefficients():
    values = [bessel_scaled(0)]
    for order_index in range(1, ORDER + 1):
        values.append(2.0 * (-1.0) ** order_index * bessel_scaled(order_index))
    return values


WEIGHTS = coefficients()


def ring_order(n):
    return [i for i in range(n) if i % 2 == 0] + [i for i in range(n - 1, -1, -1) if i % 2 == 1]


def ring_position(i, n):
    return jnp.where(i % 2 == 0, i // 2, n - 1 - i // 2)


def ring_send(x, n, step):
    order = ring_order(n)
    return lax.ppermute(x, "hub", [(order[p], order[(p + step) % n]) for p in range(n)])


def grp_source(g, e, n):
    return g ^ e if n & (n - 1) == 0 else (g - e) % n


def grp_target(g, e, n):
    return g ^ e if n & (n - 1) == 0 else (g + e) % n


def vmem(x):
    return pltpu.with_memory_space_constraint(x, pltpu.VMEM)


VMEM_SPEC = pl.BlockSpec(memory_space=pltpu.VMEM)
SMEM_SPEC = pl.BlockSpec(memory_space=pltpu.SMEM)
ANY_SPEC = pl.BlockSpec(memory_space=pl.ANY)
PARAMS = pltpu.CompilerParams(vmem_limit_bytes=8 * 1024 * 1024)


class Sizes:
    def __init__(self, mesh_shape, embed, hub_ids, send_ids, tile_val):
        self.n_grp, self.n_hub = mesh_shape["grp"], mesh_shape["hub"]
        self.blk, self.emb = tile_val.shape[1], embed.shape[1]
        self.nb = embed.shape[0] // self.blk
        self.slots = tile_val.shape[0]
        self.hub = hub_ids.shape[1]
        self.tail = send_ids.shape[2]
        self.half = self.hub // 2
        self.hub_slots = (self.n_hub - 1) * self.hub
        self.rem = self.hub_slots + (self.n_grp - 1) * self.tail
        self.cap = self.slots + UNROLL
        self.off_local, self.off_first, self.off_rest = 0, self.cap, 2 * self.cap
        self.off_len = 3 * self.cap
        self.list_len = 3 * self.cap + 3
        assert max(self.slots, self.nb + 1, self.nb + self.rem) <= MASK

    def block(self, n, dtype):
        return jax.ShapeDtypeStruct((n, self.blk, self.emb), dtype)

    def block_vmem(self, n, dtype):
        return pltpu.VMEM((n, self.blk, self.emb), dtype)


def gather_kernel(z, hub_ids, send_ids, field, hub_out, *rest):
    tails, sem = rest[:-1], rest[-1]
    g = lax.axis_index("grp")
    copies = []
    for j in range(z.hub):
        copies.append((field.at[hub_ids[0, j]], hub_out.at[j]))
    for e in range(1, z.n_grp):
        for k in range(z.tail):
            copies.append((field.at[send_ids[0, grp_target(g, e, z.n_grp), k]], tails[e - 1].at[k]))
    copies = [pltpu.make_async_copy(s, d, sem.at[i]) for i, (s, d) in enumerate(copies)]
    for c in copies:
        c.start()
    for c in copies:
        c.wait()


def bin_kernel(z, hub_ids, send_ids, tile_row, tile_col, tile_count, lists, colmap, sent):
    g = lax.axis_index("grp")
    mine = ring_position(lax.axis_index("hub"), z.n_hub)

    def clear(i, c):
        sent[i] = 0
        return c

    lax.fori_loop(0, z.nb, clear, 0)

    def local_cols(i, c):
        colmap[i] = i
        return c

    lax.fori_loop(0, z.nb, local_cols, 0)
    for j in range(z.hub):
        sent[hub_ids[0, j]] = 1

    def hub_cols(h, c):
        d = mine - ring_position(h, z.n_hub)
        d = jnp.where(d < 0, d + z.n_hub, d)
        for j in range(z.hub):
            colmap[z.nb + h * z.hub + j] = jnp.where(
                d == 0, hub_ids[0, j], z.nb + (d - 1) * z.hub + j
            )
        return c

    lax.fori_loop(0, z.n_hub, hub_cols, 0)
    base = z.nb + z.n_hub * z.hub
    for e in range(z.n_grp):
        src = grp_source(g, e, z.n_grp)
        dst = grp_target(g, e, z.n_grp)
        for k in range(z.tail):
            if e == 0:
                colmap[base + src * z.tail + k] = send_ids[0, g, k]
            else:
                colmap[base + src * z.tail + k] = z.nb + z.hub_slots + (e - 1) * z.tail + k
                sent[send_ids[0, dst, k]] = 1

    def place(t, counts):
        n0, n1, n2 = counts
        row = tile_row[0, t]
        spot = colmap[tile_col[0, t]]
        local = spot < z.nb
        first = jnp.logical_and(jnp.logical_not(local), sent[row] == 1)
        rest = jnp.logical_not(jnp.logical_or(local, first))
        where = jnp.where(local, z.off_local + n0, jnp.where(first, z.off_first + n1, z.off_rest + n2))
        spot = jnp.where(local, spot, spot - z.nb)
        lists[where] = t + (row << BITS) + (spot << (2 * BITS))
        return (n0 + local.astype(jnp.int32), n1 + first.astype(jnp.int32), n2 + rest.astype(jnp.int32))

    zero = jnp.int32(0)
    counts = lax.fori_loop(0, tile_count[0], place, (zero, zero, zero))
    for n, (off, length) in enumerate(zip((z.off_local, z.off_first, z.off_rest), counts)):
        for u in range(UNROLL):
            lists[off + length + u] = z.nb << BITS
        lists[z.off_len + n] = length


def accumulate(z, lists, which, vals, source, acc):
    off = (z.off_local, z.off_first, z.off_rest)[which]
    length = lists[z.off_len + which]

    def body(i, c):
        entries = [lists[off + i * UNROLL + u] for u in range(UNROLL)]
        prods = [
            jnp.dot(vals[e & MASK], source[e >> (2 * BITS)], preferred_element_type=F32)
            for e in entries
        ]
        for e, p in zip(entries, prods):
            row = (e >> BITS) & MASK
            acc[row] = acc[row] + p
        return c

    lax.fori_loop(0, (length + UNROLL - 1) // UNROLL, body, 0)


def fetch(parts, refs, rem, sems):
    copies = []
    for i, ((slot, n), ref) in enumerate(zip(parts, refs)):
        copies.append(pltpu.make_async_copy(ref, rem.at[pl.ds(slot, n)], sems.at[i]))
    for c in copies:
        c.start()
    return copies


def start_kernel(z, lists, embed, vals, acc, spec):
    def body(r, c):
        t = embed[r].astype(F32)
        acc[r] = -SHIFT * t
        spec[r] = WEIGHTS[0] * t
        return c

    lax.fori_loop(0, z.nb, body, 0)
    accumulate(z, lists, 0, vals, embed, acc)


def edge_kernel(z, parts, step, lists, hub_ids, send_ids, vals, prev, acc_in, *rest):
    n = len(parts)
    refs, rest = rest[:n], rest[n:]
    acc, hub_out = rest[0], rest[1]
    tails = rest[2 : 2 + z.n_grp - 1]
    rem, sems = rest[-2:]
    for c in fetch(parts, refs, rem, sems):
        c.wait()
    accumulate(z, lists, 1, vals, rem, acc)
    g = lax.axis_index("grp")

    def value(row):
        if step == 1:
            return acc[row].astype(BF16)
        return (2.0 * acc[row] - prev[row].astype(F32)).astype(BF16)

    for j in range(z.hub):
        hub_out[j] = value(hub_ids[0, j])
    for e in range(1, z.n_grp):
        for k in range(z.tail):
            tails[e - 1][k] = value(send_ids[0, grp_target(g, e, z.n_grp), k])


def inner_kernel(z, parts, step, lists, vals, prev, acc_in, spec_in, *rest):
    n = len(parts)
    refs, rest = rest[:n], rest[n:]
    acc, spec, field, rem, sems = rest
    for c in fetch(parts, refs, rem, sems):
        c.wait()
    accumulate(z, lists, 2, vals, rem, acc)

    def body(r, c):
        if step == 1:
            t = acc[r].astype(BF16)
        else:
            t = (2.0 * acc[r] - prev[r].astype(F32)).astype(BF16)
        field[r] = t
        t = t.astype(F32)
        acc[r] = -SHIFT * t
        spec[r] = spec[r] + WEIGHTS[step] * t
        return c

    lax.fori_loop(0, z.nb, body, 0)
    accumulate(z, lists, 0, vals, field, acc)


def last_kernel(z, parts, lists, vals, prev, acc_in, spec_in, *rest):
    n = len(parts)
    refs, rest = rest[:n], rest[n:]
    acc, out, stage, rem, sems, out_sem = rest
    for c in fetch(parts, refs, rem, sems):
        c.wait()
    accumulate(z, lists, 1, vals, rem, acc)
    accumulate(z, lists, 2, vals, rem, acc)
    chunks = 8 if z.nb % 8 == 0 else 1
    size = z.nb // chunks
    copies = []
    for q in range(chunks):

        def body(i, c):
            r = q * size + i
            t = (2.0 * acc[r] - prev[r].astype(F32)).astype(BF16).astype(F32)
            stage[r] = spec_in[r] + WEIGHTS[ORDER] * t
            return c

        lax.fori_loop(0, size, body, 0)
        part = pl.ds(q * size, size)
        copies.append(pltpu.make_async_copy(stage.at[part], out.at[part], out_sem.at[q]))
        copies[-1].start()
    for c in copies:
        c.wait()


def exchange(z, hub, tails):
    arrays, parts = [], []
    for e in range(1, z.n_grp):
        arrays.append(
            lax.ppermute(tails[e - 1], "grp", [(i, grp_target(i, e, z.n_grp)) for i in range(z.n_grp)])
        )
        parts.append((z.hub_slots + (e - 1) * z.tail, z.tail))
    up = down = hub
    for s in range(1, (z.n_hub + 1) // 2):
        up, down = ring_send(up, z.n_hub, 1), ring_send(down, z.n_hub, -1)
        arrays += [up, down]
        parts += [((s - 1) * z.hub, z.hub), ((z.n_hub - s - 1) * z.hub, z.hub)]
    if z.n_hub % 2 == 0:
        far = (z.n_hub // 2 - 1) * z.hub
        if z.half:
            arrays.append(ring_send(up[: z.half], z.n_hub, 1))
            parts.append((far, z.half))
        arrays.append(ring_send(down[z.half :], z.n_hub, -1))
        parts.append((far + z.half, z.hub - z.half))
    return arrays, tuple(parts)


def shards(mesh_shape, embed, hub_ids, send_ids, tile_row, tile_col, tile_val, tile_count):
    z = Sizes(mesh_shape, embed, hub_ids, send_ids, tile_val)
    ngt = z.n_grp - 1
    field0 = embed.reshape(z.nb, z.blk, z.emb)
    sent_shapes = [z.block(z.hub, BF16)] + [z.block(z.tail, BF16)] * ngt

    hub, *tails = pl.pallas_call(
        functools.partial(gather_kernel, z),
        out_shape=sent_shapes,
        in_specs=[SMEM_SPEC, SMEM_SPEC, ANY_SPEC],
        out_specs=[ANY_SPEC] * (1 + ngt),
        scratch_shapes=[pltpu.SemaphoreType.DMA((z.hub + ngt * z.tail,))],
        compiler_params=PARAMS,
        name="gather",
    )(hub_ids, send_ids, field0)
    arrays, parts = exchange(z, hub, tails)

    lists = pl.pallas_call(
        functools.partial(bin_kernel, z),
        out_shape=jax.ShapeDtypeStruct((z.list_len,), jnp.int32),
        in_specs=[SMEM_SPEC] * 5,
        out_specs=SMEM_SPEC,
        scratch_shapes=[
            pltpu.SMEM((z.nb + z.n_hub * z.hub + z.n_grp * z.tail,), jnp.int32),
            pltpu.SMEM((z.nb,), jnp.int32),
        ],
        compiler_params=PARAMS,
        name="binning",
    )(hub_ids, send_ids, tile_row, tile_col, tile_count)

    vals = vmem(tile_val)
    cur = vmem(field0)
    acc, spec = pl.pallas_call(
        functools.partial(start_kernel, z),
        out_shape=[z.block_vmem(z.nb + 1, F32), z.block_vmem(z.nb, F32)],
        in_specs=[SMEM_SPEC, VMEM_SPEC, VMEM_SPEC],
        out_specs=[VMEM_SPEC] * 2,
        compiler_params=PARAMS,
        name="start",
    )(lists, cur, vals)

    prev = cur
    scratch = [
        pltpu.VMEM((z.rem, z.blk, z.emb), BF16),
        pltpu.SemaphoreType.DMA((len(parts),)),
    ]
    for step in range(1, ORDER):
        acc, hub, *tails = pl.pallas_call(
            functools.partial(edge_kernel, z, parts, step),
            out_shape=[z.block_vmem(z.nb + 1, F32)] + sent_shapes,
            in_specs=[SMEM_SPEC] * 3 + [VMEM_SPEC] * 3 + [ANY_SPEC] * len(parts),
            out_specs=[VMEM_SPEC] * (2 + ngt),
            input_output_aliases={5: 0},
            scratch_shapes=scratch,
            compiler_params=PARAMS,
            name="edge",
        )(lists, hub_ids, send_ids, vals, vmem(prev), vmem(acc), *arrays)
        new_arrays, _ = exchange(z, hub, tails)
        acc, spec, new = pl.pallas_call(
            functools.partial(inner_kernel, z, parts, step),
            out_shape=[
                z.block_vmem(z.nb + 1, F32),
                z.block_vmem(z.nb, F32),
                z.block_vmem(z.nb, BF16),
            ],
            in_specs=[SMEM_SPEC] + [VMEM_SPEC] * 4 + [ANY_SPEC] * len(parts),
            out_specs=[VMEM_SPEC] * 3,
            input_output_aliases={3: 0, 4: 1},
            scratch_shapes=scratch,
            compiler_params=PARAMS,
            name="inner",
        )(lists, vals, vmem(prev), vmem(acc), vmem(spec), *arrays)
        arrays = new_arrays
        prev, cur = cur, new

    _, out = pl.pallas_call(
        functools.partial(last_kernel, z, parts),
        out_shape=[z.block_vmem(z.nb + 1, F32), z.block(z.nb, F32)],
        in_specs=[SMEM_SPEC] + [VMEM_SPEC] * 4 + [ANY_SPEC] * len(parts),
        out_specs=[VMEM_SPEC, ANY_SPEC],
        input_output_aliases={3: 0},
        scratch_shapes=[pltpu.VMEM((z.nb, z.blk, z.emb), F32)]
        + scratch
        + [pltpu.SemaphoreType.DMA((8,))],
        compiler_params=PARAMS,
        name="last",
    )(lists, vals, vmem(prev), vmem(acc), vmem(spec), *arrays)
    return out.reshape(embed.shape[0], z.emb)


def solution(mesh):
    return jax.shard_map(
        functools.partial(shards, dict(mesh.shape)),
        mesh=mesh,
        in_specs=(
            P(("grp", "hub"), None),
            P(("grp", "hub"), None),
            P(("grp", "hub"), None, None),
            P(("grp", "hub"), None),
            P(("grp", "hub"), None),
            P(("grp", "hub"), None, None),
            P(("grp", "hub")),
        ),
        out_specs=P(("grp", "hub"), None),
        check_vma=False,
    )
```

time: 574 us -> 141 us (0.25); the launches traced: 563 us -> 141 us
  other arithmetic: 224 us -> 0 us
  local copies, waits for them, and re-layouts: 119 us -> 10 us
  waiting for transfers between devices: 102 us -> 33.5 us
  matrix products: 55 us -> 0 us
  Pallas kernels: 0 us -> 52.2 us
  blocking collectives: 44.1 us -> 0 us
  starting transfers between devices: 4.3 us -> 44.2 us
  between operations: 14.2 us -> 0.99 us
    scatter-add x4 -> x0, other arithmetic: 156 us -> none  [apply(): summed = jax.ops.segment_sum(masked, row_list, num_segments=nblocks)]
    all_gather x4 -> x0, waiting for transfers between devices: 94.3 us -> none  [apply(): hub_all = lax.all_gather(hub_local, 'hub', axis=0, tiled=True)]
    gather x12 -> x0, local copies, waits for them, and re-layouts: 57.8 us -> none  [the longest x4 40.1 us: apply(): picked = space[col_list]]
    dot_general x4 -> x0, matrix products: 55 us -> none  [apply(): jnp.einsum('tij,tjk->tik', tile_val, picked, preferred_element_type=jnp.f...]
    pallas_call x0 -> x10, Pallas kernels: none -> 52.2 us  [the longest x3 25.2 us: shards(): pl.pallas_call(functools.partial(inner_kernel, z, parts, step), out_shape...]
    mul x4 -> x0, local copies, waits for them, and re-layouts: 50.3 us -> none  [apply(): masked = prod * live[:, None, None]]
    concatenate x4 -> x0, other arithmetic: 46.5 us -> none  [apply(): jnp.concatenate([field, hub_all, tail], axis=0)]
    ppermute x0 -> x44, starting transfers between devices: none -> 44.2 us  [the longest x32 36.8 us: ring_send(): lax.ppermute(x, 'hub', [(order[p], order[(p + step) % n]) for p in range(...]
  transfers between devices with their start and end apart: 5 -> 44, of which waited for: 5 -> 14; matrix products, arithmetic and copies ran while one was open for 2% -> 0% of each run, Pallas kernels for 0% -> 24%
where the time goes in v1:
time: 141 us
  Pallas kernels  52.2 us (37%)
  starting transfers between devices  44.2 us (31%)
  waiting for transfers between devices  33.5 us (24%)
  local copies, waits for them, and re-layouts  10 us (7%)
    ppermute x32, starting transfers between devices, ring_send(): lax.ppermute(x, 'hub', [(order[p], order[(p + step) % n]) for p in range(...  36.8 us
    ppermute x32, waiting for transfers between devices, ring_send(): lax.ppermute(x, 'hub', [(order[p], order[(p + step) % n]) for p in range(...  33.5 us
    pallas_call x3, Pallas kernels, shards(): pl.pallas_call(functools.partial(inner_kernel, z, parts, step), out_shape...  25.2 us
    unnamed x26, local copies, waits for them, and re-layouts  10 us
    pallas_call x3, Pallas kernels, shards(): pl.pallas_call(functools.partial(edge_kernel, z, parts, step), out_shape=...  9.71 us
    ppermute x12, starting transfers between devices, exchange(): lax.ppermute(tails[e - 1], 'grp', [(i, grp_target(i, e, z.n_grp)) for i i...  7.44 us
    pallas_call x1, Pallas kernels, shards(): pl.pallas_call(functools.partial(last_kernel, z, parts), out_shape=[z.blo...  6.97 us
    pallas_call x1, Pallas kernels, shards(): pl.pallas_call(functools.partial(bin_kernel, z), out_shape=jax.ShapeDtype...  4.7 us
  transfers between devices with their start and end apart: 44, of which 14 were waited for; matrix products, arithmetic and copies ran while one was open for 0% of the time, Pallas kernels for 24%

profile of v1, /device:TPU:0, one launch (start us, length us, event | category | flops | bytes accessed | tf_op | source)
XLA Modules:
  0.0 141.0 jit_solution(11118463253803747745)
XLA Ops:
  0.0 1.6 %copy-done.2 = bf16[8192,128]{1,0:T(8,128)(2,1)S(1)} copy-done((bf16[8192,128]{1,0:T(8,128)(2,1)S(1)}, bf16[8192,128]{1,0:T(8,128)(2,1)}, u32[]{:S(2)}) %copy-start.2) | copy-done | bytes 2097176
  1.6 0.7 copy-done.5
  2.3 0.7 copy-done.8
  2.9 1.5 %gather.1 = (bf16[4,128,128]{2,1,0:T(8,128)(2,1)S(1)}, bf16[4,128,128]{2,1,0:T(8,128)(2,1)S(1)}, bf16[4,128,128]{2,1,0:T(8,128)(2,1)S(1)}, bf16[4,128,128]{2,1,0:T(8,128)(2,1)S(1)}) custom-call(s32[1,4]{1,0:T(1,128)S(1)} %copy-done.8, s32[1,4,4]{2,1,0:T(4,128)S(1)} %copy-done.5, bf16[64,128,128]{2,1,0:T(8,128)(2,1)S(1)} %bitcast.2), custom_call_target="tpu_custom_call" | custom-call | tf_op jit(solution)/shard_map/gather/pallas_call | solution.py:310
  4.4 3.0 %collective-permute-start.4 = (bf16[4,128,128]{2,1,0:T(8,128)(2,1)S(1)}, bf16[4,128,128]{2,1,0:T(8,128)(2,1)S(1)}, u32[]{:S(2)}, u32[]{:S(2)}) collective-permute-start(bf16[4,128,128]{2,1,0:T(8,128)(2,1)S(1)} %get-tuple-element.39), channel_id=1, source_target_pairs={{0,1},{2,0},{4,2},{6,4},{7,6},{5,7},{3,5},{1,3},{8,9},{10,8},{12,1... | collective-permute-start | bytes 393224 | tf_op jit(solution)/shard_map/ppermute | solution.py:51
  7.6 3.4 %collective-permute-done.4.rest_4_ = bf16[4,128,128]{2,1,0:T(8,128)(2,1)S(1)} collective-permute-done((bf16[4,128,128]{2,1,0:T(8,128)(2,1)S(1)}, bf16[4,128,128]{2,1,0:T(8,128)(2,1)S(1)}, u32[]{:S(2)}, u32[]{:S(2)}) %collective-permute-start.4) | collective-permute-done | bytes 131104 | tf_op jit(solution)/shard_map/ppermute | solution.py:51
  11.0 1.7 %collective-permute-start.6 = (bf16[4,128,128]{2,1,0:T(8,128)(2,1)S(1)}, bf16[4,128,128]{2,1,0:T(8,128)(2,1)S(1)}, u32[]{:S(2)}, u32[]{:S(2)}) collective-permute-start(bf16[4,128,128]{2,1,0:T(8,128)(2,1)S(1)} %collective-permute-done.4.rest_4_), channel_id=1, source_target_pairs={{0,1},{2,0},{4,2},{6,4},{7,6},{5,7},{3,5},{1,3},{8,9},{10,8},{12,1... | collective-permute-start | bytes 393224 | tf_op jit(solution)/shard_map/ppermute | solution.py:51
  13.0 2.9 %collective-permute-done.6.rest_6_ = bf16[4,128,128]{2,1,0:T(8,128)(2,1)S(1)} collective-permute-done((bf16[4,128,128]{2,1,0:T(8,128)(2,1)S(1)}, bf16[4,128,128]{2,1,0:T(8,128)(2,1)S(1)}, u32[]{:S(2)}, u32[]{:S(2)}) %collective-permute-start.6) | collective-permute-done | bytes 131104 | tf_op jit(solution)/shard_map/ppermute | solution.py:51
  16.0 1.7 %collective-permute-start.8 = (bf16[4,128,128]{2,1,0:T(8,128)(2,1)S(1)}, bf16[4,128,128]{2,1,0:T(8,128)(2,1)S(1)}, u32[]{:S(2)}, u32[]{:S(2)}) collective-permute-start(bf16[4,128,128]{2,1,0:T(8,128)(2,1)S(1)} %collective-permute-done.6.rest_6_), channel_id=1, source_target_pairs={{0,1},{2,0},{4,2},{6,4},{7,6},{5,7},{3,5},{1,3},{8,9},{10,8},{12,1... | collective-permute-start | bytes 393224 | tf_op jit(solution)/shard_map/ppermute | solution.py:51
  18.0 1.7 %collective-permute-start.1 = (bf16[4,128,128]{2,1,0:T(8,128)(2,1)S(1)}, bf16[4,128,128]{2,1,0:T(8,128)(2,1)S(1)}, u32[]{:S(2)}, u32[]{:S(2)}) collective-permute-start(bf16[4,128,128]{2,1,0:T(8,128)(2,1)S(1)} %get-tuple-element.37), channel_id=1, source_target_pairs={{0,16},{8,24},{16,0},{24,8},{1,17},{9,25},{17,1},{25,9},{2,18},{10... | collective-permute-start | bytes 393224 | tf_op jit(solution)/shard_map/ppermute | solution.py:286
  19.9 1.1 collective-permute-done.8.rest_8_
  20.9 1.7 %collective-permute-start.10 = (bf16[2,128,128]{2,1,0:T(8,128)(2,1)S(1)}, bf16[2,128,128]{2,1,0:T(8,128)(2,1)S(1)}, u32[]{:S(2)}, u32[]{:S(2)}) collective-permute-start(bf16[2,128,128]{2,1,0:T(8,128)(2,1)S(1)} %slice.33), channel_id=1, source_target_pairs={{0,1},{2,0},{4,2},{6,4},{7,6},{5,7},{3,5},{1,3},{8,9},{10,8},{12,1... | collective-permute-start | bytes 196616 | tf_op jit(solution)/shard_map/ppermute | solution.py:51
  22.7 0.4 collective-permute-start.9
  23.7 0.7 copy-done.6
  24.4 0.7 copy-done.9
  25.1 0.7 copy-done.11
  25.8 0.7 copy-done.12
  26.4 4.7 %binning.1.lists = s32[603]{0:T(1024)S(1)} custom-call(s32[1,4]{1,0:T(1,128)S(1)} %copy-done.9, s32[1,4,4]{2,1,0:T(4,128)S(1)} %copy-done.6, s32[1,192]{1,0:T(1,128)S(1)} %copy-done.11, s32[1,192]{1,0:T(1,128)S(1)} %copy-done.12, s32[1]{0:T(128)S(6)} %copy.28.tile_count), custom_call_target="tpu_custom_call" | custom-call | tf_op jit(solution)/shard_map/binning/pallas_call | solution.py:321
  31.2 2.8 %copy-done = bf16[192,128,128]{2,1,0:T(8,128)(2,1)S(1)} copy-done((bf16[192,128,128]{2,1,0:T(8,128)(2,1)S(1)}, bf16[192,128,128]{2,1,0:T(8,128)(2,1)}, u32[]{:S(2)}) %copy-start) | copy-done | bytes 6291480
  33.9 1.6 %copy-done.3 = bf16[8192,128]{1,0:T(8,128)(2,1)S(1)} copy-done((bf16[8192,128]{1,0:T(8,128)(2,1)S(1)}, bf16[8192,128]{1,0:T(8,128)(2,1)}, u32[]{:S(2)}) %copy-start.3) | copy-done | bytes 2097176
  35.5 4.1 %start.1 = (f32[65,128,128]{2,1,0:T(8,128)S(1)}, f32[64,128,128]{2,1,0:T(8,128)S(1)}) custom-call(s32[603]{0:T(1024)S(1)} %binning.1.lists, bf16[64,128,128]{2,1,0:T(8,128)(2,1)S(1)} %bitcast.3, bf16[192,128,128]{2,1,0:T(8,128)(2,1)S(1)} %copy-done), custom_call_target="tpu_custom_call" | custom-call | tf_op jit(solution)/shard_map/start/pallas_call | solution.py:336
  39.7 3.2 %edge.3 = (f32[65,128,128]{2,1,0:T(8,128)S(1)}, bf16[4,128,128]{2,1,0:T(8,128)(2,1)S(1)}, bf16[4,128,128]{2,1,0:T(8,128)(2,1)S(1)}, bf16[4,128,128]{2,1,0:T(8,128)(2,1)S(1)}, bf16[4,128,128]{2,1,0:T(8,128)(2,1)S(1)}) custom-call(s32[603]{0:T(1024)S(1)} %binning.1.lists, s32[1,4]{1,0:T(1,128)S(1)} %copy-done.9, ...), custom_call_target="tpu_custom_call", output_to_operand_aliasing={{0}: (5, {})} | custom-call | tf_op jit(solution)/shard_map/edge/pallas_call | solution.py:351
  42.9 2.1 %collective-permute-start.15 = (bf16[4,128,128]{2,1,0:T(8,128)(2,1)S(1)}, bf16[4,128,128]{2,1,0:T(8,128)(2,1)S(1)}, u32[]{:S(2)}, u32[]{:S(2)}) collective-permute-start(bf16[4,128,128]{2,1,0:T(8,128)(2,1)S(1)} %get-tuple-element.46), channel_id=1, source_target_pairs={{0,1},{2,0},{4,2},{6,4},{7,6},{5,7},{3,5},{1,3},{8,9},{10,8},{12,1... | collective-permute-start | bytes 393224 | tf_op jit(solution)/shard_map/ppermute | solution.py:51
  45.0 0.8 collective-permute-start.14
  45.9 3.2 %collective-permute-done.15.rest_4_ = bf16[4,128,128]{2,1,0:T(8,128)(2,1)S(1)} collective-permute-done((bf16[4,128,128]{2,1,0:T(8,128)(2,1)S(1)}, bf16[4,128,128]{2,1,0:T(8,128)(2,1)S(1)}, u32[]{:S(2)}, u32[]{:S(2)}) %collective-permute-start.15) | collective-permute-done | bytes 131104 | tf_op jit(solution)/shard_map/ppermute | solution.py:51
  49.1 2.2 %collective-permute-start.17 = (bf16[4,128,128]{2,1,0:T(8,128)(2,1)S(1)}, bf16[4,128,128]{2,1,0:T(8,128)(2,1)S(1)}, u32[]{:S(2)}, u32[]{:S(2)}) collective-permute-start(bf16[4,128,128]{2,1,0:T(8,128)(2,1)S(1)} %collective-permute-done.15.rest_4_), channel_id=1, source_target_pairs={{0,1},{2,0},{4,2},{6,4},{7,6},{5,7},{3,5},{1,3},{8,9},{10,8},{12,1... | collective-permute-start | bytes 393224 | tf_op jit(solution)/shard_map/ppermute | solution.py:51
  51.5 4.2 %collective-permute-done.17.rest_6_ = bf16[4,128,128]{2,1,0:T(8,128)(2,1)S(1)} collective-permute-done((bf16[4,128,128]{2,1,0:T(8,128)(2,1)S(1)}, bf16[4,128,128]{2,1,0:T(8,128)(2,1)S(1)}, u32[]{:S(2)}, u32[]{:S(2)}) %collective-permute-start.17) | collective-permute-done | bytes 131104 | tf_op jit(solution)/shard_map/ppermute | solution.py:51
  55.7 1.1 collective-permute-start.19
  57.1 0.6 collective-permute-start.18
  57.7 1.1 collective-permute-start.12
  58.8 0.8 collective-permute-start.13
  59.6 1.1 collective-permute-done.19.rest_8_
  60.6 1.1 collective-permute-start.21
  62.1 0.6 collective-permute-start.20
  62.7 7.7 %inner.3 = (f32[65,128,128]{2,1,0:T(8,128)S(1)}, f32[64,128,128]{2,1,0:T(8,128)S(1)}, bf16[64,128,128]{2,1,0:T(8,128)(2,1)S(1)}) custom-call(s32[603]{0:T(1024)S(1)} %binning.1.lists, bf16[192,128,128]{2,1,0:T(8,128)(2,1)S(1)} %copy-done.1, bf16[64,128,128]{2,1,0:T(8,128)(2,1)S(1)} %bitcast.5, ...), custom_call_target="tpu_custom_call", output_to_operand_aliasing={{0}: (3, {}), {1}: (4, {})} | custom-call | tf_op jit(solution)/shard_map/inner/pallas_call | solution.py:362
  70.5 3.3 %edge.4 = (f32[65,128,128]{2,1,0:T(8,128)S(1)}, bf16[4,128,128]{2,1,0:T(8,128)(2,1)S(1)}, bf16[4,128,128]{2,1,0:T(8,128)(2,1)S(1)}, bf16[4,128,128]{2,1,0:T(8,128)(2,1)S(1)}, bf16[4,128,128]{2,1,0:T(8,128)(2,1)S(1)}) custom-call(s32[603]{0:T(1024)S(1)} %binning.1.lists, s32[1,4]{1,0:T(1,128)S(1)} %copy-done.10, ...), custom_call_target="tpu_custom_call", output_to_operand_aliasing={{0}: (5, {})} | custom-call | tf_op jit(solution)/shard_map/edge/pallas_call | solution.py:351
  73.8 1.7 %collective-permute-start.26 = (bf16[4,128,128]{2,1,0:T(8,128)(2,1)S(1)}, bf16[4,128,128]{2,1,0:T(8,128)(2,1)S(1)}, u32[]{:S(2)}, u32[]{:S(2)}) collective-permute-start(bf16[4,128,128]{2,1,0:T(8,128)(2,1)S(1)} %get-tuple-element.55), channel_id=1, source_target_pairs={{0,1},{2,0},{4,2},{6,4},{7,6},{5,7},{3,5},{1,3},{8,9},{10,8},{12,1... | collective-permute-start | bytes 393224 | tf_op jit(solution)/shard_map/ppermute | solution.py:51
  75.4 1.1 collective-permute-start.25
  76.5 3.1 %collective-permute-done.26.rest_4_ = bf16[4,128,128]{2,1,0:T(8,128)(2,1)S(1)} collective-permute-done((bf16[4,128,128]{2,1,0:T(8,128)(2,1)S(1)}, bf16[4,128,128]{2,1,0:T(8,128)(2,1)S(1)}, u32[]{:S(2)}, u32[]{:S(2)}) %collective-permute-start.26) | collective-permute-done | bytes 131104 | tf_op jit(solution)/shard_map/ppermute | solution.py:51
  79.7 1.8 %collective-permute-start.28 = (bf16[4,128,128]{2,1,0:T(8,128)(2,1)S(1)}, bf16[4,128,128]{2,1,0:T(8,128)(2,1)S(1)}, u32[]{:S(2)}, u32[]{:S(2)}) collective-permute-start(bf16[4,128,128]{2,1,0:T(8,128)(2,1)S(1)} %collective-permute-done.26.rest_4_), channel_id=1, source_target_pairs={{0,1},{2,0},{4,2},{6,4},{7,6},{5,7},{3,5},{1,3},{8,9},{10,8},{12,1... | collective-permute-start | bytes 393224 | tf_op jit(solution)/shard_map/ppermute | solution.py:51
  81.5 0.6 collective-permute-start.27
  82.1 4.3 %collective-permute-done.28.rest_6_ = bf16[4,128,128]{2,1,0:T(8,128)(2,1)S(1)} collective-permute-done((bf16[4,128,128]{2,1,0:T(8,128)(2,1)S(1)}, bf16[4,128,128]{2,1,0:T(8,128)(2,1)S(1)}, u32[]{:S(2)}, u32[]{:S(2)}) %collective-permute-start.28) | collective-permute-done | bytes 131104 | tf_op jit(solution)/shard_map/ppermute | solution.py:51
  86.3 0.7 collective-permute-start.30
  87.0 1.3 collective-permute-start.29
  88.4 1.3 collective-permute-start.23
  89.7 0.5 collective-permute-start.24
  90.2 1.1 collective-permute-done.30.rest_8_
  91.3 0.7 collective-permute-start.32
  92.0 1.4 collective-permute-start.31
  93.4 8.2 %inner.4 = (f32[65,128,128]{2,1,0:T(8,128)S(1)}, f32[64,128,128]{2,1,0:T(8,128)S(1)}, bf16[64,128,128]{2,1,0:T(8,128)(2,1)S(1)}) custom-call(s32[603]{0:T(1024)S(1)} %binning.1.lists, bf16[192,128,128]{2,1,0:T(8,128)(2,1)S(1)} %copy-done.1, bf16[64,128,128]{2,1,0:T(8,128)(2,1)S(1)} %bitcast.7, ...), custom_call_target="tpu_custom_call", output_to_operand_aliasing={{0}: (3, {}), {1}: (4, {})} | custom-call | tf_op jit(solution)/shard_map/inner/pallas_call | solution.py:362
  101.6 3.3 %edge.5 = (f32[65,128,128]{2,1,0:T(8,128)S(1)}, bf16[4,128,128]{2,1,0:T(8,128)(2,1)S(1)}, bf16[4,128,128]{2,1,0:T(8,128)(2,1)S(1)}, bf16[4,128,128]{2,1,0:T(8,128)(2,1)S(1)}, bf16[4,128,128]{2,1,0:T(8,128)(2,1)S(1)}) custom-call(s32[603]{0:T(1024)S(1)} %binning.1.lists, s32[1,4]{1,0:T(1,128)S(1)} %copy-done.10, ...), custom_call_target="tpu_custom_call", output_to_operand_aliasing={{0}: (5, {})} | custom-call | tf_op jit(solution)/shard_map/edge/pallas_call | solution.py:351
  104.9 1.0 collective-permute-start.37
  105.9 1.8 %collective-permute-start.36 = (bf16[4,128,128]{2,1,0:T(8,128)(2,1)S(1)}, bf16[4,128,128]{2,1,0:T(8,128)(2,1)S(1)}, u32[]{:S(2)}, u32[]{:S(2)}) collective-permute-start(bf16[4,128,128]{2,1,0:T(8,128)(2,1)S(1)} %get-tuple-element.63), channel_id=1, source_target_pairs={{0,2},{2,4},{4,6},{6,7},{7,5},{5,3},{3,1},{1,0},{8,10},{10,12},{12... | collective-permute-start | bytes 393224 | tf_op jit(solution)/shard_map/ppermute | solution.py:51
  107.7 3.2 %collective-permute-done.37.rest_4_ = bf16[4,128,128]{2,1,0:T(8,128)(2,1)S(1)} collective-permute-done((bf16[4,128,128]{2,1,0:T(8,128)(2,1)S(1)}, bf16[4,128,128]{2,1,0:T(8,128)(2,1)S(1)}, u32[]{:S(2)}, u32[]{:S(2)}) %collective-permute-start.37) | collective-permute-done | bytes 131104 | tf_op jit(solution)/shard_map/ppermute | solution.py:51
  110.9 2.4 %collective-permute-start.38 = (bf16[4,128,128]{2,1,0:T(8,128)(2,1)S(1)}, bf16[4,128,128]{2,1,0:T(8,128)(2,1)S(1)}, u32[]{:S(2)}, u32[]{:S(2)}) collective-permute-start(bf16[4,128,128]{2,1,0:T(8,128)(2,1)S(1)} %collective-permute-done.36.rest_3_), channel_id=1, source_target_pairs={{0,2},{2,4},{4,6},{6,7},{7,5},{5,3},{3,1},{1,0},{8,10},{10,12},{12... | collective-permute-start | bytes 393224 | tf_op jit(solution)/shard_map/ppermute | solution.py:51
  113.3 4.2 %collective-permute-done.39.rest_6_ = bf16[4,128,128]{2,1,0:T(8,128)(2,1)S(1)} collective-permute-done((bf16[4,128,128]{2,1,0:T(8,128)(2,1)S(1)}, bf16[4,128,128]{2,1,0:T(8,128)(2,1)S(1)}, u32[]{:S(2)}, u32[]{:S(2)}) %collective-permute-start.39) | collective-permute-done | bytes 131104 | tf_op jit(solution)/shard_map/ppermute | solution.py:51
  117.5 2.0 %collective-permute-start.40 = (bf16[4,128,128]{2,1,0:T(8,128)(2,1)S(1)}, bf16[4,128,128]{2,1,0:T(8,128)(2,1)S(1)}, u32[]{:S(2)}, u32[]{:S(2)}) collective-permute-start(bf16[4,128,128]{2,1,0:T(8,128)(2,1)S(1)} %collective-permute-done.38.rest_5_), channel_id=1, source_target_pairs={{0,2},{2,4},{4,6},{6,7},{7,5},{5,3},{3,1},{1,0},{8,10},{10,12},{12... | collective-permute-start | bytes 393224 | tf_op jit(solution)/shard_map/ppermute | solution.py:51
  119.5 1.5 %collective-permute-start.34 = (bf16[4,128,128]{2,1,0:T(8,128)(2,1)S(1)}, bf16[4,128,128]{2,1,0:T(8,128)(2,1)S(1)}, u32[]{:S(2)}, u32[]{:S(2)}) collective-permute-start(bf16[4,128,128]{2,1,0:T(8,128)(2,1)S(1)} %get-tuple-element.61), channel_id=1, source_target_pairs={{0,16},{8,24},{16,0},{24,8},{1,17},{9,25},{17,1},{25,9},{2,18},{10... | collective-permute-start | bytes 393224 | tf_op jit(solution)/shard_map/ppermute | solution.py:286
  121.0 0.4 collective-permute-start.35
  121.4 1.1 collective-permute-done.41.rest_8_
  122.5 0.8 collective-permute-start.43
  123.3 1.3 collective-permute-start.42
  124.6 9.4 %inner.5 = (f32[65,128,128]{2,1,0:T(8,128)S(1)}, f32[64,128,128]{2,1,0:T(8,128)S(1)}, bf16[64,128,128]{2,1,0:T(8,128)(2,1)}) custom-call(s32[603]{0:T(1024)S(1)} %binning.1.lists, bf16[192,128,128]{2,1,0:T(8,128)(2,1)S(1)} %copy-done.1, bf16[64,128,128]{2,1,0:T(8,128)(2,1)S(1)} %get-tuple-element.50.prev, ...), custom_call_target="tpu_custom_call", output_to_operand_aliasing={{0}: (3, {}), {1}: (4, {})} | custom-call | tf_op jit(solution)/shard_map/inner/pallas_call | solution.py:362
  134.0 7.0 %last.1 = (f32[65,128,128]{2,1,0:T(8,128)S(1)}, f32[64,128,128]{2,1,0:T(8,128)}) custom-call(s32[603]{0:T(1024)S(1)} %binning.1.lists, bf16[192,128,128]{2,1,0:T(8,128)(2,1)S(1)} %copy-done.1, bf16[64,128,128]{2,1,0:T(8,128)(2,1)S(1)} %get-tuple-element.49.prev, f32[65,128,128]{2,1,0:T(8,128)S(1)} %get-tuple-element.58.acc_in, ...), custom_call_target="tpu_custom_call", output_to_operand_aliasing={{0}: (3, {})} | custom-call | tf_op jit(solution)/shard_map/last/pallas_call | solution.py:379
  (68 shorter events, 2.0 us)
Async XLA Ops:
  0.0 1.6 %copy-start.2 = (bf16[8192,128]{1,0:T(8,128)(2,1)S(1)}, bf16[8192,128]{1,0:T(8,128)(2,1)}, u32[]{:S(2)}) copy-start(bf16[8192,128]{1,0:T(8,128)(2,1)} %param.7) | copy-start | bytes 6291460
  1.6 0.7 copy-start.5
  2.3 0.7 copy-start.8
  4.4 6.6 %collective-permute-start.4 = (bf16[4,128,128]{2,1,0:T(8,128)(2,1)S(1)}, bf16[4,128,128]{2,1,0:T(8,128)(2,1)S(1)}, u32[]{:S(2)}, u32[]{:S(2)}) collective-permute-start(bf16[4,128,128]{2,1,0:T(8,128)(2,1)S(1)} %get-tuple-element.39), channel_id=1, source_target_pairs={{0,1},{2,0},{4,2},{6,4},{7,6},{5,7},{3,5},{1,3},{8,9},{10,8},{12,1... | collective-permute-start | bytes 393224 | tf_op jit(solution)/shard_map/ppermute | solution.py:51
  7.4 5.2 %collective-permute-start.3 = (bf16[4,128,128]{2,1,0:T(8,128)(2,1)S(1)}, bf16[4,128,128]{2,1,0:T(8,128)(2,1)S(1)}, u32[]{:S(2)}, u32[]{:S(2)}) collective-permute-start(bf16[4,128,128]{2,1,0:T(8,128)(2,1)S(1)} %get-tuple-element.39), channel_id=1, source_target_pairs={{0,2},{2,4},{4,6},{6,7},{7,5},{5,3},{3,1},{1,0},{8,10},{10,12},{12... | collective-permute-start | bytes 393224 | tf_op jit(solution)/shard_map/ppermute | solution.py:51
  11.0 5.0 %collective-permute-start.6 = (bf16[4,128,128]{2,1,0:T(8,128)(2,1)S(1)}, bf16[4,128,128]{2,1,0:T(8,128)(2,1)S(1)}, u32[]{:S(2)}, u32[]{:S(2)}) collective-permute-start(bf16[4,128,128]{2,1,0:T(8,128)(2,1)S(1)} %collective-permute-done.4.rest_4_), channel_id=1, source_target_pairs={{0,1},{2,0},{4,2},{6,4},{7,6},{5,7},{3,5},{1,3},{8,9},{10,8},{12,1... | collective-permute-start | bytes 393224 | tf_op jit(solution)/shard_map/ppermute | solution.py:51
  12.7 5.0 %collective-permute-start.5 = (bf16[4,128,128]{2,1,0:T(8,128)(2,1)S(1)}, bf16[4,128,128]{2,1,0:T(8,128)(2,1)S(1)}, u32[]{:S(2)}, u32[]{:S(2)}) collective-permute-start(bf16[4,128,128]{2,1,0:T(8,128)(2,1)S(1)} %collective-permute-done.3.rest_3_), channel_id=1, source_target_pairs={{0,2},{2,4},{4,6},{6,7},{7,5},{5,3},{3,1},{1,0},{8,10},{10,12},{12... | collective-permute-start | bytes 393224 | tf_op jit(solution)/shard_map/ppermute | solution.py:51
  16.0 5.0 %collective-permute-start.8 = (bf16[4,128,128]{2,1,0:T(8,128)(2,1)S(1)}, bf16[4,128,128]{2,1,0:T(8,128)(2,1)S(1)}, u32[]{:S(2)}, u32[]{:S(2)}) collective-permute-start(bf16[4,128,128]{2,1,0:T(8,128)(2,1)S(1)} %collective-permute-done.6.rest_6_), channel_id=1, source_target_pairs={{0,1},{2,0},{4,2},{6,4},{7,6},{5,7},{3,5},{1,3},{8,9},{10,8},{12,1... | collective-permute-start | bytes 393224 | tf_op jit(solution)/shard_map/ppermute | solution.py:51
  17.6 5.0 %collective-permute-start.7 = (bf16[4,128,128]{2,1,0:T(8,128)(2,1)S(1)}, bf16[4,128,128]{2,1,0:T(8,128)(2,1)S(1)}, u32[]{:S(2)}, u32[]{:S(2)}) collective-permute-start(bf16[4,128,128]{2,1,0:T(8,128)(2,1)S(1)} %collective-permute-done.5.rest_5_), channel_id=1, source_target_pairs={{0,2},{2,4},{4,6},{6,7},{7,5},{5,3},{3,1},{1,0},{8,10},{10,12},{12... | collective-permute-start | bytes 393224 | tf_op jit(solution)/shard_map/ppermute | solution.py:51
  18.0 21.6 %collective-permute-start = (bf16[4,128,128]{2,1,0:T(8,128)(2,1)S(1)}, bf16[4,128,128]{2,1,0:T(8,128)(2,1)S(1)}, u32[]{:S(2)}, u32[]{:S(2)}) collective-permute-start(bf16[4,128,128]{2,1,0:T(8,128)(2,1)S(1)} %get-tuple-element.36), channel_id=1, source_target_pairs={{0,8},{8,0},{16,24},{24,16},{1,9},{9,1},{17,25},{25,17},{2,10},{10... | collective-permute-start | bytes 393224 | tf_op jit(solution)/shard_map/ppermute | solution.py:286
  18.0 21.6 %collective-permute-start.1 = (bf16[4,128,128]{2,1,0:T(8,128)(2,1)S(1)}, bf16[4,128,128]{2,1,0:T(8,128)(2,1)S(1)}, u32[]{:S(2)}, u32[]{:S(2)}) collective-permute-start(bf16[4,128,128]{2,1,0:T(8,128)(2,1)S(1)} %get-tuple-element.37), channel_id=1, source_target_pairs={{0,16},{8,24},{16,0},{24,8},{1,17},{9,25},{17,1},{25,9},{2,18},{10... | collective-permute-start | bytes 393224 | tf_op jit(solution)/shard_map/ppermute | solution.py:286
  19.7 20.0 %collective-permute-start.2 = (bf16[4,128,128]{2,1,0:T(8,128)(2,1)S(1)}, bf16[4,128,128]{2,1,0:T(8,128)(2,1)S(1)}, u32[]{:S(2)}, u32[]{:S(2)}) collective-permute-start(bf16[4,128,128]{2,1,0:T(8,128)(2,1)S(1)} %get-tuple-element.38), channel_id=1, source_target_pairs={{0,24},{8,16},{16,8},{24,0},{1,25},{9,17},{17,9},{25,1},{2,26},{10... | collective-permute-start | bytes 393224 | tf_op jit(solution)/shard_map/ppermute | solution.py:286
  20.9 18.7 %copy-start.7 = (s32[1,4,4]{2,1,0:T(4,128)S(1)}, s32[1,4,4]{2,1,0:T(4,128)}, u32[]{:S(2)}) copy-start(s32[1,4,4]{2,1,0:T(4,128)} %send_ids.9) | copy-start | bytes 196
  20.9 18.7 %collective-permute-start.10 = (bf16[2,128,128]{2,1,0:T(8,128)(2,1)S(1)}, bf16[2,128,128]{2,1,0:T(8,128)(2,1)S(1)}, u32[]{:S(2)}, u32[]{:S(2)}) collective-permute-start(bf16[2,128,128]{2,1,0:T(8,128)(2,1)S(1)} %slice.33), channel_id=1, source_target_pairs={{0,1},{2,0},{4,2},{6,4},{7,6},{5,7},{3,5},{1,3},{8,9},{10,8},{12,1... | collective-permute-start | bytes 196616 | tf_op jit(solution)/shard_map/ppermute | solution.py:51
  22.7 17.0 %collective-permute-start.9 = (bf16[2,128,128]{2,1,0:T(8,128)(2,1)S(1)}, bf16[2,128,128]{2,1,0:T(8,128)(2,1)S(1)}, u32[]{:S(2)}, u32[]{:S(2)}) collective-permute-start(bf16[2,128,128]{2,1,0:T(8,128)(2,1)S(1)} %slice.32), channel_id=1, source_target_pairs={{0,2},{2,4},{4,6},{6,7},{7,5},{5,3},{3,1},{1,0},{8,10},{10,12},{12... | collective-permute-start | bytes 196616 | tf_op jit(solution)/shard_map/ppermute | solution.py:51
  23.7 0.7 copy-start.6
  24.4 0.7 copy-start.9
  25.1 0.7 copy-start.11
  25.8 0.7 copy-start.12
  31.1 2.8 %copy-start = (bf16[192,128,128]{2,1,0:T(8,128)(2,1)S(1)}, bf16[192,128,128]{2,1,0:T(8,128)(2,1)}, u32[]{:S(2)}) copy-start(bf16[192,128,128]{2,1,0:T(8,128)(2,1)} %vals.15) | copy-start | bytes 18874372
  33.9 1.6 %copy-start.3 = (bf16[8192,128]{1,0:T(8,128)(2,1)S(1)}, bf16[8192,128]{1,0:T(8,128)(2,1)}, u32[]{:S(2)}) copy-start(bf16[8192,128]{1,0:T(8,128)(2,1)} %param.7) | copy-start | bytes 6291460
  35.5 4.2 %copy-start.1 = (bf16[192,128,128]{2,1,0:T(8,128)(2,1)S(1)}, bf16[192,128,128]{2,1,0:T(8,128)(2,1)}, u32[]{:S(2)}) copy-start(bf16[192,128,128]{2,1,0:T(8,128)(2,1)} %vals.15) | copy-start | bytes 18874372
  35.5 4.2 %copy-start.4 = (bf16[8192,128]{1,0:T(8,128)(2,1)S(1)}, bf16[8192,128]{1,0:T(8,128)(2,1)}, u32[]{:S(2)}) copy-start(bf16[8192,128]{1,0:T(8,128)(2,1)} %param.7) | copy-start | bytes 6291460
  42.9 6.2 %collective-permute-start.15 = (bf16[4,128,128]{2,1,0:T(8,128)(2,1)S(1)}, bf16[4,128,128]{2,1,0:T(8,128)(2,1)S(1)}, u32[]{:S(2)}, u32[]{:S(2)}) collective-permute-start(bf16[4,128,128]{2,1,0:T(8,128)(2,1)S(1)} %get-tuple-element.46), channel_id=1, source_target_pairs={{0,1},{2,0},{4,2},{6,4},{7,6},{5,7},{3,5},{1,3},{8,9},{10,8},{12,1... | collective-permute-start | bytes 393224 | tf_op jit(solution)/shard_map/ppermute | solution.py:51
  45.0 6.3 %collective-permute-start.14 = (bf16[4,128,128]{2,1,0:T(8,128)(2,1)S(1)}, bf16[4,128,128]{2,1,0:T(8,128)(2,1)S(1)}, u32[]{:S(2)}, u32[]{:S(2)}) collective-permute-start(bf16[4,128,128]{2,1,0:T(8,128)(2,1)S(1)} %get-tuple-element.46), channel_id=1, source_target_pairs={{0,2},{2,4},{4,6},{6,7},{7,5},{5,3},{3,1},{1,0},{8,10},{10,12},{12... | collective-permute-start | bytes 393224 | tf_op jit(solution)/shard_map/ppermute | solution.py:51
  49.1 6.6 %collective-permute-start.17 = (bf16[4,128,128]{2,1,0:T(8,128)(2,1)S(1)}, bf16[4,128,128]{2,1,0:T(8,128)(2,1)S(1)}, u32[]{:S(2)}, u32[]{:S(2)}) collective-permute-start(bf16[4,128,128]{2,1,0:T(8,128)(2,1)S(1)} %collective-permute-done.15.rest_4_), channel_id=1, source_target_pairs={{0,1},{2,0},{4,2},{6,4},{7,6},{5,7},{3,5},{1,3},{8,9},{10,8},{12,1... | collective-permute-start | bytes 393224 | tf_op jit(solution)/shard_map/ppermute | solution.py:51
  51.3 5.8 %collective-permute-start.16 = (bf16[4,128,128]{2,1,0:T(8,128)(2,1)S(1)}, bf16[4,128,128]{2,1,0:T(8,128)(2,1)S(1)}, u32[]{:S(2)}, u32[]{:S(2)}) collective-permute-start(bf16[4,128,128]{2,1,0:T(8,128)(2,1)S(1)} %collective-permute-done.14.rest_3_), channel_id=1, source_target_pairs={{0,2},{2,4},{4,6},{6,7},{7,5},{5,3},{3,1},{1,0},{8,10},{10,12},{12... | collective-permute-start | bytes 393224 | tf_op jit(solution)/shard_map/ppermute | solution.py:51
  55.7 5.0 %collective-permute-start.19 = (bf16[4,128,128]{2,1,0:T(8,128)(2,1)S(1)}, bf16[4,128,128]{2,1,0:T(8,128)(2,1)S(1)}, u32[]{:S(2)}, u32[]{:S(2)}) collective-permute-start(bf16[4,128,128]{2,1,0:T(8,128)(2,1)S(1)} %collective-permute-done.17.rest_6_), channel_id=1, source_target_pairs={{0,1},{2,0},{4,2},{6,4},{7,6},{5,7},{3,5},{1,3},{8,9},{10,8},{12,1... | collective-permute-start | bytes 393224 | tf_op jit(solution)/shard_map/ppermute | solution.py:51
  57.1 5.0 %collective-permute-start.18 = (bf16[4,128,128]{2,1,0:T(8,128)(2,1)S(1)}, bf16[4,128,128]{2,1,0:T(8,128)(2,1)S(1)}, u32[]{:S(2)}, u32[]{:S(2)}) collective-permute-start(bf16[4,128,128]{2,1,0:T(8,128)(2,1)S(1)} %collective-permute-done.16.rest_5_), channel_id=1, source_target_pairs={{0,2},{2,4},{4,6},{6,7},{7,5},{5,3},{3,1},{1,0},{8,10},{10,12},{12... | collective-permute-start | bytes 393224 | tf_op jit(solution)/shard_map/ppermute | solution.py:51
  57.7 12.7 %collective-permute-start.11 = (bf16[4,128,128]{2,1,0:T(8,128)(2,1)S(1)}, bf16[4,128,128]{2,1,0:T(8,128)(2,1)S(1)}, u32[]{:S(2)}, u32[]{:S(2)}) collective-permute-start(bf16[4,128,128]{2,1,0:T(8,128)(2,1)S(1)} %get-tuple-element.43), channel_id=1, source_target_pairs={{0,8},{8,0},{16,24},{24,16},{1,9},{9,1},{17,25},{25,17},{2,10},{10... | collective-permute-start | bytes 393224 | tf_op jit(solution)/shard_map/ppermute | solution.py:286
  57.7 12.7 %collective-permute-start.12 = (bf16[4,128,128]{2,1,0:T(8,128)(2,1)S(1)}, bf16[4,128,128]{2,1,0:T(8,128)(2,1)S(1)}, u32[]{:S(2)}, u32[]{:S(2)}) collective-permute-start(bf16[4,128,128]{2,1,0:T(8,128)(2,1)S(1)} %get-tuple-element.44), channel_id=1, source_target_pairs={{0,16},{8,24},{16,0},{24,8},{1,17},{9,25},{17,1},{25,9},{2,18},{10... | collective-permute-start | bytes 393224 | tf_op jit(solution)/shard_map/ppermute | solution.py:286
  58.8 11.7 %collective-permute-start.13 = (bf16[4,128,128]{2,1,0:T(8,128)(2,1)S(1)}, bf16[4,128,128]{2,1,0:T(8,128)(2,1)S(1)}, u32[]{:S(2)}, u32[]{:S(2)}) collective-permute-start(bf16[4,128,128]{2,1,0:T(8,128)(2,1)S(1)} %get-tuple-element.45), channel_id=1, source_target_pairs={{0,24},{8,16},{16,8},{24,0},{1,25},{9,17},{17,9},{25,1},{2,26},{10... | collective-permute-start | bytes 393224 | tf_op jit(solution)/shard_map/ppermute | solution.py:286
  60.6 9.8 %collective-permute-start.21 = (bf16[2,128,128]{2,1,0:T(8,128)(2,1)S(1)}, bf16[2,128,128]{2,1,0:T(8,128)(2,1)S(1)}, u32[]{:S(2)}, u32[]{:S(2)}) collective-permute-start(bf16[2,128,128]{2,1,0:T(8,128)(2,1)S(1)} %slice.35), channel_id=1, source_target_pairs={{0,1},{2,0},{4,2},{6,4},{7,6},{5,7},{3,5},{1,3},{8,9},{10,8},{12,1... | collective-permute-start | bytes 196616 | tf_op jit(solution)/shard_map/ppermute | solution.py:51
  62.1 8.4 %collective-permute-start.20 = (bf16[2,128,128]{2,1,0:T(8,128)(2,1)S(1)}, bf16[2,128,128]{2,1,0:T(8,128)(2,1)S(1)}, u32[]{:S(2)}, u32[]{:S(2)}) collective-permute-start(bf16[2,128,128]{2,1,0:T(8,128)(2,1)S(1)} %slice.34), channel_id=1, source_target_pairs={{0,2},{2,4},{4,6},{6,7},{7,5},{5,3},{3,1},{1,0},{8,10},{10,12},{12... | collective-permute-start | bytes 196616 | tf_op jit(solution)/shard_map/ppermute | solution.py:51
  62.7 7.8 %copy-start.10 = (s32[1,4]{1,0:T(1,128)S(1)}, s32[1,4]{1,0:T(1,128)}, u32[]{:S(2)}) copy-start(s32[1,4]{1,0:T(1,128)} %hub_ids.9) | copy-start | bytes 52
  73.8 5.9 %collective-permute-start.26 = (bf16[4,128,128]{2,1,0:T(8,128)(2,1)S(1)}, bf16[4,128,128]{2,1,0:T(8,128)(2,1)S(1)}, u32[]{:S(2)}, u32[]{:S(2)}) collective-permute-start(bf16[4,128,128]{2,1,0:T(8,128)(2,1)S(1)} %get-tuple-element.55), channel_id=1, source_target_pairs={{0,1},{2,0},{4,2},{6,4},{7,6},{5,7},{3,5},{1,3},{8,9},{10,8},{12,1... | collective-permute-start | bytes 393224 | tf_op jit(solution)/shard_map/ppermute | solution.py:51
  75.4 6.0 %collective-permute-start.25 = (bf16[4,128,128]{2,1,0:T(8,128)(2,1)S(1)}, bf16[4,128,128]{2,1,0:T(8,128)(2,1)S(1)}, u32[]{:S(2)}, u32[]{:S(2)}) collective-permute-start(bf16[4,128,128]{2,1,0:T(8,128)(2,1)S(1)} %get-tuple-element.55), channel_id=1, source_target_pairs={{0,2},{2,4},{4,6},{6,7},{7,5},{5,3},{3,1},{1,0},{8,10},{10,12},{12... | collective-permute-start | bytes 393224 | tf_op jit(solution)/shard_map/ppermute | solution.py:51
  79.7 6.7 %collective-permute-start.28 = (bf16[4,128,128]{2,1,0:T(8,128)(2,1)S(1)}, bf16[4,128,128]{2,1,0:T(8,128)(2,1)S(1)}, u32[]{:S(2)}, u32[]{:S(2)}) collective-permute-start(bf16[4,128,128]{2,1,0:T(8,128)(2,1)S(1)} %collective-permute-done.26.rest_4_), channel_id=1, source_target_pairs={{0,1},{2,0},{4,2},{6,4},{7,6},{5,7},{3,5},{1,3},{8,9},{10,8},{12,1... | collective-permute-start | bytes 393224 | tf_op jit(solution)/shard_map/ppermute | solution.py:51
  81.5 5.6 %collective-permute-start.27 = (bf16[4,128,128]{2,1,0:T(8,128)(2,1)S(1)}, bf16[4,128,128]{2,1,0:T(8,128)(2,1)S(1)}, u32[]{:S(2)}, u32[]{:S(2)}) collective-permute-start(bf16[4,128,128]{2,1,0:T(8,128)(2,1)S(1)} %collective-permute-done.25.rest_3_), channel_id=1, source_target_pairs={{0,2},{2,4},{4,6},{6,7},{7,5},{5,3},{3,1},{1,0},{8,10},{10,12},{12... | collective-permute-start | bytes 393224 | tf_op jit(solution)/shard_map/ppermute | solution.py:51
  86.3 5.0 %collective-permute-start.30 = (bf16[4,128,128]{2,1,0:T(8,128)(2,1)S(1)}, bf16[4,128,128]{2,1,0:T(8,128)(2,1)S(1)}, u32[]{:S(2)}, u32[]{:S(2)}) collective-permute-start(bf16[4,128,128]{2,1,0:T(8,128)(2,1)S(1)} %collective-permute-done.28.rest_6_), channel_id=1, source_target_pairs={{0,1},{2,0},{4,2},{6,4},{7,6},{5,7},{3,5},{1,3},{8,9},{10,8},{12,1... | collective-permute-start | bytes 393224 | tf_op jit(solution)/shard_map/ppermute | solution.py:51
  87.0 5.0 %collective-permute-start.29 = (bf16[4,128,128]{2,1,0:T(8,128)(2,1)S(1)}, bf16[4,128,128]{2,1,0:T(8,128)(2,1)S(1)}, u32[]{:S(2)}, u32[]{:S(2)}) collective-permute-start(bf16[4,128,128]{2,1,0:T(8,128)(2,1)S(1)} %collective-permute-done.27.rest_5_), channel_id=1, source_target_pairs={{0,2},{2,4},{4,6},{6,7},{7,5},{5,3},{3,1},{1,0},{8,10},{10,12},{12... | collective-permute-start | bytes 393224 | tf_op jit(solution)/shard_map/ppermute | solution.py:51
  88.4 13.2 %collective-permute-start.22 = (bf16[4,128,128]{2,1,0:T(8,128)(2,1)S(1)}, bf16[4,128,128]{2,1,0:T(8,128)(2,1)S(1)}, u32[]{:S(2)}, u32[]{:S(2)}) collective-permute-start(bf16[4,128,128]{2,1,0:T(8,128)(2,1)S(1)} %get-tuple-element.52), channel_id=1, source_target_pairs={{0,8},{8,0},{16,24},{24,16},{1,9},{9,1},{17,25},{25,17},{2,10},{10... | collective-permute-start | bytes 393224 | tf_op jit(solution)/shard_map/ppermute | solution.py:286
  88.4 13.2 %collective-permute-start.23 = (bf16[4,128,128]{2,1,0:T(8,128)(2,1)S(1)}, bf16[4,128,128]{2,1,0:T(8,128)(2,1)S(1)}, u32[]{:S(2)}, u32[]{:S(2)}) collective-permute-start(bf16[4,128,128]{2,1,0:T(8,128)(2,1)S(1)} %get-tuple-element.53), channel_id=1, source_target_pairs={{0,16},{8,24},{16,0},{24,8},{1,17},{9,25},{17,1},{25,9},{2,18},{10... | collective-permute-start | bytes 393224 | tf_op jit(solution)/shard_map/ppermute | solution.py:286
  89.7 11.9 %collective-permute-start.24 = (bf16[4,128,128]{2,1,0:T(8,128)(2,1)S(1)}, bf16[4,128,128]{2,1,0:T(8,128)(2,1)S(1)}, u32[]{:S(2)}, u32[]{:S(2)}) collective-permute-start(bf16[4,128,128]{2,1,0:T(8,128)(2,1)S(1)} %get-tuple-element.54), channel_id=1, source_target_pairs={{0,24},{8,16},{16,8},{24,0},{1,25},{9,17},{17,9},{25,1},{2,26},{10... | collective-permute-start | bytes 393224 | tf_op jit(solution)/shard_map/ppermute | solution.py:286
  91.3 10.3 %collective-permute-start.32 = (bf16[2,128,128]{2,1,0:T(8,128)(2,1)S(1)}, bf16[2,128,128]{2,1,0:T(8,128)(2,1)S(1)}, u32[]{:S(2)}, u32[]{:S(2)}) collective-permute-start(bf16[2,128,128]{2,1,0:T(8,128)(2,1)S(1)} %slice.37), channel_id=1, source_target_pairs={{0,1},{2,0},{4,2},{6,4},{7,6},{5,7},{3,5},{1,3},{8,9},{10,8},{12,1... | collective-permute-start | bytes 196616 | tf_op jit(solution)/shard_map/ppermute | solution.py:51
  92.0 9.6 %collective-permute-start.31 = (bf16[2,128,128]{2,1,0:T(8,128)(2,1)S(1)}, bf16[2,128,128]{2,1,0:T(8,128)(2,1)S(1)}, u32[]{:S(2)}, u32[]{:S(2)}) collective-permute-start(bf16[2,128,128]{2,1,0:T(8,128)(2,1)S(1)} %slice.36), channel_id=1, source_target_pairs={{0,2},{2,4},{4,6},{6,7},{7,5},{5,3},{3,1},{1,0},{8,10},{10,12},{12... | collective-permute-start | bytes 196616 | tf_op jit(solution)/shard_map/ppermute | solution.py:51
  104.9 6.0 %collective-permute-start.37 = (bf16[4,128,128]{2,1,0:T(8,128)(2,1)S(1)}, bf16[4,128,128]{2,1,0:T(8,128)(2,1)S(1)}, u32[]{:S(2)}, u32[]{:S(2)}) collective-permute-start(bf16[4,128,128]{2,1,0:T(8,128)(2,1)S(1)} %get-tuple-element.63), channel_id=1, source_target_pairs={{0,1},{2,0},{4,2},{6,4},{7,6},{5,7},{3,5},{1,3},{8,9},{10,8},{12,1... | collective-permute-start | bytes 393224 | tf_op jit(solution)/shard_map/ppermute | solution.py:51
  105.9 5.0 %collective-permute-start.36 = (bf16[4,128,128]{2,1,0:T(8,128)(2,1)S(1)}, bf16[4,128,128]{2,1,0:T(8,128)(2,1)S(1)}, u32[]{:S(2)}, u32[]{:S(2)}) collective-permute-start(bf16[4,128,128]{2,1,0:T(8,128)(2,1)S(1)} %get-tuple-element.63), channel_id=1, source_target_pairs={{0,2},{2,4},{4,6},{6,7},{7,5},{5,3},{3,1},{1,0},{8,10},{10,12},{12... | collective-permute-start | bytes 393224 | tf_op jit(solution)/shard_map/ppermute | solution.py:51
  110.9 6.6 %collective-permute-start.39 = (bf16[4,128,128]{2,1,0:T(8,128)(2,1)S(1)}, bf16[4,128,128]{2,1,0:T(8,128)(2,1)S(1)}, u32[]{:S(2)}, u32[]{:S(2)}) collective-permute-start(bf16[4,128,128]{2,1,0:T(8,128)(2,1)S(1)} %collective-permute-done.37.rest_4_), channel_id=1, source_target_pairs={{0,1},{2,0},{4,2},{6,4},{7,6},{5,7},{3,5},{1,3},{8,9},{10,8},{12,1... | collective-permute-start | bytes 393224 | tf_op jit(solution)/shard_map/ppermute | solution.py:51
  110.9 6.6 %collective-permute-start.38 = (bf16[4,128,128]{2,1,0:T(8,128)(2,1)S(1)}, bf16[4,128,128]{2,1,0:T(8,128)(2,1)S(1)}, u32[]{:S(2)}, u32[]{:S(2)}) collective-permute-start(bf16[4,128,128]{2,1,0:T(8,128)(2,1)S(1)} %collective-permute-done.36.rest_3_), channel_id=1, source_target_pairs={{0,2},{2,4},{4,6},{6,7},{7,5},{5,3},{3,1},{1,0},{8,10},{10,12},{12... | collective-permute-start | bytes 393224 | tf_op jit(solution)/shard_map/ppermute | solution.py:51
  117.5 5.0 %collective-permute-start.41 = (bf16[4,128,128]{2,1,0:T(8,128)(2,1)S(1)}, bf16[4,128,128]{2,1,0:T(8,128)(2,1)S(1)}, u32[]{:S(2)}, u32[]{:S(2)}) collective-permute-start(bf16[4,128,128]{2,1,0:T(8,128)(2,1)S(1)} %collective-permute-done.39.rest_6_), channel_id=1, source_target_pairs={{0,1},{2,0},{4,2},{6,4},{7,6},{5,7},{3,5},{1,3},{8,9},{10,8},{12,1... | collective-permute-start | bytes 393224 | tf_op jit(solution)/shard_map/ppermute | solution.py:51
  117.5 5.8 %collective-permute-start.40 = (bf16[4,128,128]{2,1,0:T(8,128)(2,1)S(1)}, bf16[4,128,128]{2,1,0:T(8,128)(2,1)S(1)}, u32[]{:S(2)}, u32[]{:S(2)}) collective-permute-start(bf16[4,128,128]{2,1,0:T(8,128)(2,1)S(1)} %collective-permute-done.38.rest_5_), channel_id=1, source_target_pairs={{0,2},{2,4},{4,6},{6,7},{7,5},{5,3},{3,1},{1,0},{8,10},{10,12},{12... | collective-permute-start | bytes 393224 | tf_op jit(solution)/shard_map/ppermute | solution.py:51
  119.5 14.4 %collective-permute-start.33 = (bf16[4,128,128]{2,1,0:T(8,128)(2,1)S(1)}, bf16[4,128,128]{2,1,0:T(8,128)(2,1)S(1)}, u32[]{:S(2)}, u32[]{:S(2)}) collective-permute-start(bf16[4,128,128]{2,1,0:T(8,128)(2,1)S(1)} %get-tuple-element.60), channel_id=1, source_target_pairs={{0,8},{8,0},{16,24},{24,16},{1,9},{9,1},{17,25},{25,17},{2,10},{10... | collective-permute-start | bytes 393224 | tf_op jit(solution)/shard_map/ppermute | solution.py:286
  119.5 14.4 %collective-permute-start.34 = (bf16[4,128,128]{2,1,0:T(8,128)(2,1)S(1)}, bf16[4,128,128]{2,1,0:T(8,128)(2,1)S(1)}, u32[]{:S(2)}, u32[]{:S(2)}) collective-permute-start(bf16[4,128,128]{2,1,0:T(8,128)(2,1)S(1)} %get-tuple-element.61), channel_id=1, source_target_pairs={{0,16},{8,24},{16,0},{24,8},{1,17},{9,25},{17,1},{25,9},{2,18},{10... | collective-permute-start | bytes 393224 | tf_op jit(solution)/shard_map/ppermute | solution.py:286
  121.0 12.9 %collective-permute-start.35 = (bf16[4,128,128]{2,1,0:T(8,128)(2,1)S(1)}, bf16[4,128,128]{2,1,0:T(8,128)(2,1)S(1)}, u32[]{:S(2)}, u32[]{:S(2)}) collective-permute-start(bf16[4,128,128]{2,1,0:T(8,128)(2,1)S(1)} %get-tuple-element.62), channel_id=1, source_target_pairs={{0,24},{8,16},{16,8},{24,0},{1,25},{9,17},{17,9},{25,1},{2,26},{10... | collective-permute-start | bytes 393224 | tf_op jit(solution)/shard_map/ppermute | solution.py:286
  122.5 11.5 %collective-permute-start.43 = (bf16[2,128,128]{2,1,0:T(8,128)(2,1)S(1)}, bf16[2,128,128]{2,1,0:T(8,128)(2,1)S(1)}, u32[]{:S(2)}, u32[]{:S(2)}) collective-permute-start(bf16[2,128,128]{2,1,0:T(8,128)(2,1)S(1)} %slice.39), channel_id=1, source_target_pairs={{0,1},{2,0},{4,2},{6,4},{7,6},{5,7},{3,5},{1,3},{8,9},{10,8},{12,1... | collective-permute-start | bytes 196616 | tf_op jit(solution)/shard_map/ppermute | solution.py:51
  123.3 10.7 %collective-permute-start.42 = (bf16[2,128,128]{2,1,0:T(8,128)(2,1)S(1)}, bf16[2,128,128]{2,1,0:T(8,128)(2,1)S(1)}, u32[]{:S(2)}, u32[]{:S(2)}) collective-permute-start(bf16[2,128,128]{2,1,0:T(8,128)(2,1)S(1)} %slice.38), channel_id=1, source_target_pairs={{0,2},{2,4},{4,6},{6,7},{7,5},{5,3},{3,1},{1,0},{8,10},{10,12},{12... | collective-permute-start | bytes 196616 | tf_op jit(solution)/shard_map/ppermute | solution.py:51

commit v2 on v1

v2 whole, which is shorter than its diff:
```python
import functools
import math

import jax
import jax.numpy as jnp
from jax import lax
from jax.experimental import pallas as pl
from jax.experimental.pallas import tpu as pltpu
from jax.sharding import PartitionSpec as P

ORDER = 4
SHIFT = 0.2
THETA = 3.0

UNROLL = 16
BITS = 10
MASK = (1 << BITS) - 1
F32 = jnp.float32
BF16 = jnp.bfloat16


def bessel_scaled(order_index):
    total = 0.0
    for term in range(40):
        total += (THETA / 2.0) ** (2 * term + order_index) / (
            math.factorial(term) * math.factorial(term + order_index)
        )
    return math.exp(-THETA) * total


def coefficients():
    values = [bessel_scaled(0)]
    for order_index in range(1, ORDER + 1):
        values.append(2.0 * (-1.0) ** order_index * bessel_scaled(order_index))
    return values


WEIGHTS = coefficients()


def grp_source(g, e, n):
    return g ^ e if power_of_two(n) else (g - e) % n


def grp_target(g, e, n):
    return g ^ e if power_of_two(n) else (g + e) % n


def power_of_two(n):
    return n & (n - 1) == 0


def vmem(x):
    return pltpu.with_memory_space_constraint(x, pltpu.VMEM)


def hbm(x):
    return pltpu.with_memory_space_constraint(x, pltpu.HBM)


VMEM_SPEC = pl.BlockSpec(memory_space=pltpu.VMEM)
SMEM_SPEC = pl.BlockSpec(memory_space=pltpu.SMEM)
ANY_SPEC = pl.BlockSpec(memory_space=pl.ANY)
PARAMS = pltpu.CompilerParams(vmem_limit_bytes=8 * 1024 * 1024)


class Sizes:
    def __init__(self, mesh_shape, embed, hub_ids, send_ids, tile_val):
        self.n_grp, self.n_hub = mesh_shape["grp"], mesh_shape["hub"]
        self.blk, self.emb = tile_val.shape[1], embed.shape[1]
        self.nb = embed.shape[0] // self.blk
        self.slots = tile_val.shape[0]
        self.hub = hub_ids.shape[1]
        self.tail = send_ids.shape[2]
        self.hub_slots = (self.n_hub - 1) * self.hub
        self.rem = self.hub_slots + (self.n_grp - 1) * self.tail
        self.cap = self.slots + UNROLL
        self.off_local, self.off_first, self.off_rest = 0, self.cap, 2 * self.cap
        self.off_len = 3 * self.cap
        self.off_hub = self.off_len + 3
        self.off_send = self.off_hub + self.hub
        self.list_len = self.off_send + (self.n_grp - 1) * self.tail
        self.tile_flops = 2 * self.blk * self.blk * self.emb
        self.field_bytes = 2 * self.nb * self.blk * self.emb
        assert max(self.slots, self.nb + 1, self.nb + self.rem) <= MASK

    def block(self, n, dtype):
        return jax.ShapeDtypeStruct((n, self.blk, self.emb), dtype)

    def block_vmem(self, n, dtype):
        return pltpu.VMEM((n, self.blk, self.emb), dtype)


def read_scalars(pairs, sems):
    copies = [pltpu.make_async_copy(s, d, sems.at[i]) for i, (s, d) in enumerate(pairs)]
    for c in copies:
        c.start()
    for c in copies:
        c.wait()


def gather_kernel(z, hub_in, send_in, field, hub_out, *rest):
    tails, (hub_ids, send_ids, scalar_sem, sem) = rest[:-4], rest[-4:]
    read_scalars([(hub_in, hub_ids), (send_in, send_ids)], scalar_sem)
    g = lax.axis_index("grp")
    copies = []
    for j in range(z.hub):
        copies.append((field.at[hub_ids[0, j]], hub_out.at[j]))
    for e in range(1, z.n_grp):
        for k in range(z.tail):
            copies.append((field.at[send_ids[0, grp_target(g, e, z.n_grp), k]], tails[e - 1].at[k]))
    copies = [pltpu.make_async_copy(s, d, sem.at[i]) for i, (s, d) in enumerate(copies)]
    for c in copies:
        c.start()
    for c in copies:
        c.wait()


def hub_source(h, d, n):
    return h ^ d if power_of_two(n) else (h - d) % n


def hub_target(h, d, n):
    return h ^ d if power_of_two(n) else (h + d) % n


def bin_kernel(
    z, tile_count, hub_in, send_in, row_in, col_in, vals_in, field_in, lists, vals, field, *scratch
):
    hub_ids, send_ids, tile_row, tile_col, colmap, sent, scalar_sem, sems = scratch
    copies = [
        pltpu.make_async_copy(vals_in, vals, sems.at[0]),
        pltpu.make_async_copy(field_in, field, sems.at[1]),
    ]
    for c in copies:
        c.start()
    read_scalars(
        [(hub_in, hub_ids), (send_in, send_ids), (row_in, tile_row), (col_in, tile_col)],
        scalar_sem,
    )
    g = lax.axis_index("grp")
    mine = lax.axis_index("hub")
    for j in range(z.hub):
        lists[z.off_hub + j] = hub_ids[0, j]
    for e in range(1, z.n_grp):
        for k in range(z.tail):
            lists[z.off_send + (e - 1) * z.tail + k] = send_ids[0, grp_target(g, e, z.n_grp), k]

    def local_cols(i, c):
        sent[i] = 0
        colmap[i] = i
        return c

    lax.fori_loop(0, z.nb, local_cols, 0, unroll=8)
    for j in range(z.hub):
        sent[hub_ids[0, j]] = 1
    for d in range(z.n_hub):
        h = hub_source(mine, d, z.n_hub)
        for j in range(z.hub):
            spot = hub_ids[0, j] if d == 0 else z.nb + (d - 1) * z.hub + j
            colmap[z.nb + h * z.hub + j] = spot
    base = z.nb + z.n_hub * z.hub
    for e in range(z.n_grp):
        src = grp_source(g, e, z.n_grp)
        dst = grp_target(g, e, z.n_grp)
        for k in range(z.tail):
            if e == 0:
                colmap[base + src * z.tail + k] = send_ids[0, g, k]
            else:
                colmap[base + src * z.tail + k] = z.nb + z.hub_slots + (e - 1) * z.tail + k
                sent[send_ids[0, dst, k]] = 1

    total = tile_count[0]
    group = 8 if z.slots % 8 == 0 else 1

    def place(i, counts):
        n0, n1, n2 = counts
        ts = [i * group + u for u in range(group)]
        rows = [tile_row[0, t] for t in ts]
        spots = [colmap[tile_col[0, t]] for t in ts]
        sents = [sent[r] for r in rows]
        entries, places = [], []
        for t, row, spot, out in zip(ts, rows, spots, sents):
            live = (t < total).astype(jnp.int32)
            local = (spot < z.nb).astype(jnp.int32)
            first = (1 - local) * out
            rest = (1 - local) * (1 - out)
            places.append(
                jnp.where(local == 1, z.off_local + n0, jnp.where(first == 1, z.off_first + n1, z.off_rest + n2))
            )
            entries.append(t + (row << BITS) + ((spot - (1 - local) * z.nb) << (2 * BITS)))
            n0, n1, n2 = n0 + local * live, n1 + first * live, n2 + rest * live
        for entry, where in zip(entries, places):
            lists[where] = entry
        return n0, n1, n2

    zero = jnp.int32(0)
    counts = lax.fori_loop(0, (total + group - 1) // group, place, (zero, zero, zero))
    for n, (off, length) in enumerate(zip((z.off_local, z.off_first, z.off_rest), counts)):
        for u in range(UNROLL):
            lists[off + length + u] = z.nb << BITS
        lists[z.off_len + n] = length
    for c in copies:
        c.wait()


def accumulate(z, lists, which, vals, source, acc, scale=None):
    off = (z.off_local, z.off_first, z.off_rest)[which]
    length = lists[z.off_len + which]

    def body(i, c):
        entries = [lists[off + i * UNROLL + u] for u in range(UNROLL)]
        prods = [
            jnp.dot(vals[e & MASK], source[e >> (2 * BITS)], preferred_element_type=F32)
            for e in entries
        ]
        for e, p in zip(entries, prods):
            row = (e >> BITS) & MASK
            acc[row] = acc[row] + (p if scale is None else scale * p)
        return c

    lax.fori_loop(0, (length + UNROLL - 1) // UNROLL, body, 0)


def fetch(parts, refs, rem, sems):
    copies = []
    for i, ((slot, n), ref) in enumerate(zip(parts, refs)):
        copies.append(pltpu.make_async_copy(ref, rem.at[pl.ds(slot, n)], sems.at[i]))
    for c in copies:
        c.start()
    for c in copies:
        c.wait()


def start_kernel(z, lists, vals, field, acc):
    def body(r, c):
        acc[r] = -SHIFT * field[r].astype(F32)
        return c

    lax.fori_loop(0, z.nb, body, 0)
    accumulate(z, lists, 0, vals, field, acc)


def edge_kernel(z, parts, step, lists, vals, prev, acc_in, *rest):
    n = len(parts)
    refs, rest = rest[:n], rest[n:]
    acc, rem, hub_out = rest[:3]
    tails = rest[3:-1]
    fetch(parts, refs, rem, rest[-1])
    accumulate(z, lists, 1, vals, rem, acc)

    def value(row):
        if step == 1:
            return acc[row].astype(BF16)
        return (2.0 * acc[row] - prev[row].astype(F32)).astype(BF16)

    for j in range(z.hub):
        hub_out[j] = value(lists[z.off_hub + j])
    for e in range(1, z.n_grp):
        for k in range(z.tail):
            tails[e - 1][k] = value(lists[z.off_send + (e - 1) * z.tail + k])


def finish_kernel(z, step, lists, vals, rem, *rest):
    fields = rest[:step]
    acc, field = rest[-2:]
    accumulate(z, lists, 2, vals, rem, acc)

    def body(r, c):
        if step == 1:
            t = acc[r].astype(BF16)
        else:
            t = (2.0 * acc[r] - fields[step - 2][r].astype(F32)).astype(BF16)
        field[r] = t
        t = t.astype(F32)
        if step < ORDER - 1:
            acc[r] = -SHIFT * t
        else:
            total = (WEIGHTS[step] - 2.0 * SHIFT * WEIGHTS[ORDER]) * t
            for k in range(step):
                w = WEIGHTS[k] - WEIGHTS[ORDER] * (k == ORDER - 2)
                total = total + w * fields[k][r].astype(F32)
            acc[r] = total
        return c

    lax.fori_loop(0, z.nb, body, 0)


def local_kernel(z, scale, lists, vals, field, acc_in, acc):
    accumulate(z, lists, 0, vals, field, acc, scale)


def last_kernel(z, parts, lists, vals, acc_in, *rest):
    n = len(parts)
    refs, rest = rest[:n], rest[n:]
    acc, out, rem, sems, out_sem = rest
    fetch(parts, refs, rem, sems)
    accumulate(z, lists, 1, vals, rem, acc, 2.0 * WEIGHTS[ORDER])
    accumulate(z, lists, 2, vals, rem, acc, 2.0 * WEIGHTS[ORDER])
    c = pltpu.make_async_copy(acc.at[pl.ds(0, z.nb)], out, out_sem)
    c.start()
    c.wait()


def exchange(z, hub, tails):
    got = {}

    def send(x, d):
        return lax.ppermute(x, "hub", [(i, hub_target(i, d, z.n_hub)) for i in range(z.n_hub)])

    n = z.n_hub
    if power_of_two(n):
        bits = [1 << b for b in range(n.bit_length() - 1)]
        for b in reversed(bits):
            got[b] = send(hub, b)
        others = [d for d in range(1, n) if d not in got]
        for d in sorted(others, key=lambda d: -d):
            held = [b for b in bits if d & b]
            b = held[-1] if len(held) == 2 else held[0]
            got[d] = send(got[b], d ^ b)
    else:
        for d in range(1, n):
            got[d] = send(hub, d)
    arrays = [got[d] for d in range(1, n)]
    parts = [((d - 1) * z.hub, z.hub) for d in range(1, n)]
    for e in range(1, z.n_grp):
        arrays.append(
            lax.ppermute(tails[e - 1], "grp", [(i, grp_target(i, e, z.n_grp)) for i in range(z.n_grp)])
        )
        parts.append((z.hub_slots + (e - 1) * z.tail, z.tail))
    return arrays, tuple(parts)


def cost(z, tiles, nbytes):
    return pl.CostEstimate(
        flops=tiles * z.tile_flops,
        bytes_accessed=nbytes + tiles * 2 * z.blk * (z.blk + 5 * z.emb),
        transcendentals=0,
    )


def shards(mesh_shape, embed, hub_ids, send_ids, tile_row, tile_col, tile_val, tile_count):
    z = Sizes(mesh_shape, embed, hub_ids, send_ids, tile_val)
    ngt = z.n_grp - 1
    field0 = embed.reshape(z.nb, z.blk, z.emb)
    sent_shapes = [z.block(z.hub, BF16)] + [z.block(z.tail, BF16)] * ngt
    hub_ids, send_ids = hbm(hub_ids), hbm(send_ids)

    hub, *tails = pl.pallas_call(
        functools.partial(gather_kernel, z),
        out_shape=sent_shapes,
        in_specs=[ANY_SPEC] * 3,
        out_specs=[ANY_SPEC] * (1 + ngt),
        scratch_shapes=[
            pltpu.SMEM(hub_ids.shape, jnp.int32),
            pltpu.SMEM(send_ids.shape, jnp.int32),
            pltpu.SemaphoreType.DMA((2,)),
            pltpu.SemaphoreType.DMA((z.hub + ngt * z.tail,)),
        ],
        compiler_params=PARAMS,
        name="gather",
    )(hub_ids, send_ids, hbm(field0))
    arrays, parts = exchange(z, hub, tails)

    lists, vals, field = pl.pallas_call(
        functools.partial(bin_kernel, z),
        out_shape=[
            pltpu.SMEM((z.list_len,), jnp.int32),
            pltpu.VMEM(tile_val.shape, BF16),
            z.block_vmem(z.nb, BF16),
        ],
        in_specs=[SMEM_SPEC] + [ANY_SPEC] * 6,
        out_specs=[SMEM_SPEC, VMEM_SPEC, VMEM_SPEC],
        scratch_shapes=[
            pltpu.SMEM(hub_ids.shape, jnp.int32),
            pltpu.SMEM(send_ids.shape, jnp.int32),
            pltpu.SMEM(tile_row.shape, jnp.int32),
            pltpu.SMEM(tile_col.shape, jnp.int32),
            pltpu.SMEM((z.nb + z.n_hub * z.hub + z.n_grp * z.tail,), jnp.int32),
            pltpu.SMEM((z.nb,), jnp.int32),
            pltpu.SemaphoreType.DMA((4,)),
            pltpu.SemaphoreType.DMA((2,)),
        ],
        compiler_params=PARAMS,
        cost_estimate=cost(z, 0, 2 * (2 * z.slots * z.blk * z.blk + z.field_bytes)),
        name="binning",
    )(tile_count, hub_ids, send_ids, hbm(tile_row), hbm(tile_col), hbm(tile_val), hbm(field0))

    acc_shape = z.block_vmem(z.nb + 1, F32)
    vals, field = vmem(vals), vmem(field)
    lists = pltpu.with_memory_space_constraint(lists, pltpu.SMEM)
    acc = pl.pallas_call(
        functools.partial(start_kernel, z),
        out_shape=acc_shape,
        in_specs=[SMEM_SPEC, VMEM_SPEC, VMEM_SPEC],
        out_specs=VMEM_SPEC,
        compiler_params=PARAMS,
        cost_estimate=cost(z, z.slots // 2, 3 * z.field_bytes),
        name="start",
    )(lists, vals, field)

    fields = [field]
    sems = pltpu.SemaphoreType.DMA((len(parts),))
    for step in range(1, ORDER):
        prev = fields[max(step - 2, 0)]
        acc, rem, hub, *tails = pl.pallas_call(
            functools.partial(edge_kernel, z, parts, step),
            out_shape=[acc_shape, z.block_vmem(z.rem, BF16)] + sent_shapes,
            in_specs=[SMEM_SPEC] + [VMEM_SPEC] * 3 + [ANY_SPEC] * len(parts),
            out_specs=[VMEM_SPEC] * (3 + ngt),
            input_output_aliases={3: 0},
            scratch_shapes=[sems],
            compiler_params=PARAMS,
            cost_estimate=cost(z, z.slots // 8, 2 * z.rem * z.blk * z.emb),
            name="edge",
        )(lists, vals, prev, vmem(acc), *arrays)
        arrays, _ = exchange(z, hub, tails)
        acc, new = pl.pallas_call(
            functools.partial(finish_kernel, z, step),
            out_shape=[acc_shape, z.block_vmem(z.nb, BF16)],
            in_specs=[SMEM_SPEC] + [VMEM_SPEC] * (3 + step),
            out_specs=[VMEM_SPEC] * 2,
            input_output_aliases={3 + step: 0},
            compiler_params=PARAMS,
            cost_estimate=cost(z, z.slots // 4, 5 * z.field_bytes),
            name="finish",
        )(lists, vals, vmem(rem), *fields, vmem(acc))
        new = vmem(new)
        fields.append(new)
        acc = pl.pallas_call(
            functools.partial(local_kernel, z, 2.0 * WEIGHTS[ORDER] if step == ORDER - 1 else None),
            out_shape=acc_shape,
            in_specs=[SMEM_SPEC] + [VMEM_SPEC] * 3,
            out_specs=VMEM_SPEC,
            input_output_aliases={3: 0},
            compiler_params=PARAMS,
            cost_estimate=cost(z, z.slots // 2, 0),
            name="local",
        )(lists, vals, new, vmem(acc))

    _, out = pl.pallas_call(
        functools.partial(last_kernel, z, parts),
        out_shape=[acc_shape, z.block(z.nb, F32)],
        in_specs=[SMEM_SPEC] + [VMEM_SPEC] * 2 + [ANY_SPEC] * len(parts),
        out_specs=[VMEM_SPEC, ANY_SPEC],
        input_output_aliases={2: 0},
        scratch_shapes=[pltpu.VMEM((z.rem, z.blk, z.emb), BF16), sems, pltpu.SemaphoreType.DMA(())],
        compiler_params=PARAMS,
        name="last",
    )(lists, vals, vmem(acc), *arrays)
    return out.reshape(embed.shape[0], z.emb)


def solution(mesh):
    return jax.shard_map(
        functools.partial(shards, dict(mesh.shape)),
        mesh=mesh,
        in_specs=(
            P(("grp", "hub"), None),
            P(("grp", "hub"), None),
            P(("grp", "hub"), None, None),
            P(("grp", "hub"), None),
            P(("grp", "hub"), None),
            P(("grp", "hub"), None, None),
            P(("grp", "hub")),
        ),
        out_specs=P(("grp", "hub"), None),
        check_vma=False,
    )
```

time: 141 us -> 94.8 us (0.67)
  Pallas kernels: 52.2 us -> 35 us
  waiting for transfers between devices: 33.5 us -> 17.1 us
  local copies, waits for them, and re-layouts: 10 us -> 0 us
  starting transfers between devices: 44.2 us -> 42.5 us
    ppermute x32 -> x28, waiting for transfers between devices: 33.5 us -> 17 us  [send(): lax.ppermute(x, 'hub', [(i, hub_target(i, d, z.n_hub)) for i in range(z.n...]
    pallas_call x6 -> x9, Pallas kernels: 41 us -> 26.5 us  [the longest x3 7.53 us: shards(): pl.pallas_call(functools.partial(local_kernel, z, 2.0 * WEIGHTS[ORDER] if...]
    unnamed x26 -> x0, local copies, waits for them, and re-layouts: 10 us -> none
    pallas_call x3, Pallas kernels: 9.71 us -> 6.68 us  [shards(): pl.pallas_call(functools.partial(edge_kernel, z, parts, step), out_shape=...]
    ppermute x12, starting transfers between devices: 7.44 us -> 5.65 us  [exchange(): lax.ppermute(tails[e - 1], 'grp', [(i, grp_target(i, e, z.n_grp)) for i i...]
    ppermute x32 -> x28, starting transfers between devices: 36.8 us -> 36.9 us  [send(): lax.ppermute(x, 'hub', [(i, hub_target(i, d, z.n_hub)) for i in range(z.n...]
  transfers between devices with their start and end apart: 44 -> 40, of which waited for: 14 -> 5; matrix products, arithmetic and copies ran while one was open for 0% -> 0% of each run, Pallas kernels for 24% -> 22%
where the time goes in v2:
time: 94.8 us; the launch traced here: 95.6 us
  starting transfers between devices  42.5 us (45%)
  Pallas kernels  35 us (37%)
  waiting for transfers between devices  17.1 us (18%)
  between operations  0.96 us (1%)
    ppermute x28, starting transfers between devices, send(): lax.ppermute(x, 'hub', [(i, hub_target(i, d, z.n_hub)) for i in range(z.n...  36.9 us
    ppermute x28, waiting for transfers between devices, send(): lax.ppermute(x, 'hub', [(i, hub_target(i, d, z.n_hub)) for i in range(z.n...  17 us
    pallas_call x3, Pallas kernels, shards(): pl.pallas_call(functools.partial(local_kernel, z, 2.0 * WEIGHTS[ORDER] if...  7.53 us
    pallas_call x3, Pallas kernels, shards(): pl.pallas_call(functools.partial(finish_kernel, z, step), out_shape=[acc_...  6.99 us
    pallas_call x3, Pallas kernels, shards(): pl.pallas_call(functools.partial(edge_kernel, z, parts, step), out_shape=...  6.68 us
    ppermute x12, starting transfers between devices, exchange(): lax.ppermute(tails[e - 1], 'grp', [(i, grp_target(i, e, z.n_grp)) for i i...  5.65 us
    pallas_call x1, Pallas kernels, shards(): pl.pallas_call(functools.partial(last_kernel, z, parts), out_shape=[acc_s...  5.08 us
    pallas_call x1, Pallas kernels, shards(): pl.pallas_call(functools.partial(bin_kernel, z), out_shape=[pltpu.SMEM((z...  3.73 us
  transfers between devices with their start and end apart: 40, of which 5 were waited for; matrix products, arithmetic and copies ran while one was open for 0% of the time, Pallas kernels for 22%

profile of v2, /device:TPU:0, one launch (start us, length us, event | category | flops | bytes accessed | tf_op | source)
XLA Modules:
  0.0 95.6 jit_solution(2809945064686626920)
XLA Ops:
  0.0 1.9 %gather.1 = (bf16[4,128,128]{2,1,0:T(8,128)(2,1)S(1)}, bf16[4,128,128]{2,1,0:T(8,128)(2,1)S(1)}, bf16[4,128,128]{2,1,0:T(8,128)(2,1)S(1)}, bf16[4,128,128]{2,1,0:T(8,128)(2,1)S(1)}) custom-call(s32[1,4]{1,0:T(1,128)} %hub_in.3, s32[1,4,4]{2,1,0:T(4,128)} %send_in.3, bf16[64,128,128]{2,1,0:T(8,128)(2,1)} %bitcast.2), custom_call_target="tpu_custom_call" | custom-call | tf_op jit(solution)/shard_map/gather/pallas_call | solution.py:349
  1.9 0.5 collective-permute-start.7
  2.4 3.7 %collective-permute-start.3 = (bf16[4,128,128]{2,1,0:T(8,128)(2,1)S(1)}, bf16[4,128,128]{2,1,0:T(8,128)(2,1)S(1)}, u32[]{:S(2)}, u32[]{:S(2)}) collective-permute-start(bf16[4,128,128]{2,1,0:T(8,128)(2,1)S(1)} %get-tuple-element.40), channel_id=1, source_target_pairs={{0,4},{1,5},{2,6},{3,7},{4,0},{5,1},{6,2},{7,3},{8,12},{9,13},{10,... | collective-permute-start | bytes 393224 | tf_op jit(solution)/shard_map/ppermute | solution.py:309
  6.0 1.5 %collective-permute-start.8 = (bf16[4,128,128]{2,1,0:T(8,128)(2,1)S(1)}, bf16[4,128,128]{2,1,0:T(8,128)(2,1)S(1)}, u32[]{:S(2)}, u32[]{:S(2)}) collective-permute-start(bf16[4,128,128]{2,1,0:T(8,128)(2,1)S(1)} %get-tuple-element.42), channel_id=1, source_target_pairs={{0,16},{8,24},{16,0},{24,8},{1,17},{9,25},{17,1},{25,9},{2,18},{10... | collective-permute-start | bytes 393224 | tf_op jit(solution)/shard_map/ppermute | solution.py:328
  7.5 1.6 %collective-permute-start.1 = (bf16[4,128,128]{2,1,0:T(8,128)(2,1)S(1)}, bf16[4,128,128]{2,1,0:T(8,128)(2,1)S(1)}, u32[]{:S(2)}, u32[]{:S(2)}) collective-permute-start(bf16[4,128,128]{2,1,0:T(8,128)(2,1)S(1)} %get-tuple-element.40), channel_id=1, source_target_pairs={{0,2},{1,3},{2,0},{3,1},{4,6},{5,7},{6,4},{7,5},{8,10},{9,11},{10,... | collective-permute-start | bytes 393224 | tf_op jit(solution)/shard_map/ppermute | solution.py:309
  9.1 1.5 %collective-permute-start = (bf16[4,128,128]{2,1,0:T(8,128)(2,1)S(1)}, bf16[4,128,128]{2,1,0:T(8,128)(2,1)S(1)}, u32[]{:S(2)}, u32[]{:S(2)}) collective-permute-start(bf16[4,128,128]{2,1,0:T(8,128)(2,1)S(1)} %get-tuple-element.40), channel_id=1, source_target_pairs={{0,1},{1,0},{2,3},{3,2},{4,5},{5,4},{6,7},{7,6},{8,9},{9,8},{10,11... | collective-permute-start | bytes 393224 | tf_op jit(solution)/shard_map/ppermute | solution.py:309
  10.6 2.4 %collective-permute-done.3.rest_3_ = bf16[4,128,128]{2,1,0:T(8,128)(2,1)S(1)} collective-permute-done((bf16[4,128,128]{2,1,0:T(8,128)(2,1)S(1)}, bf16[4,128,128]{2,1,0:T(8,128)(2,1)S(1)}, u32[]{:S(2)}, u32[]{:S(2)}) %collective-permute-start.3) | collective-permute-done | bytes 131104 | tf_op jit(solution)/shard_map/ppermute | solution.py:309
  13.1 0.7 collective-permute-start.5
  13.8 1.5 %collective-permute-start.4 = (bf16[4,128,128]{2,1,0:T(8,128)(2,1)S(1)}, bf16[4,128,128]{2,1,0:T(8,128)(2,1)S(1)}, u32[]{:S(2)}, u32[]{:S(2)}) collective-permute-start(bf16[4,128,128]{2,1,0:T(8,128)(2,1)S(1)} %collective-permute-done.3.rest_3_), channel_id=1, source_target_pairs={{0,1},{1,0},{2,3},{3,2},{4,5},{5,4},{6,7},{7,6},{8,9},{9,8},{10,11... | collective-permute-start | bytes 393224 | tf_op jit(solution)/shard_map/ppermute | solution.py:309
  15.3 0.0 collective-permute-done.1.rest_1_
  15.3 0.8 collective-permute-start.2
  16.0 2.6 %collective-permute-start.6 = (bf16[4,128,128]{2,1,0:T(8,128)(2,1)S(1)}, bf16[4,128,128]{2,1,0:T(8,128)(2,1)S(1)}, u32[]{:S(2)}, u32[]{:S(2)}) collective-permute-start(bf16[4,128,128]{2,1,0:T(8,128)(2,1)S(1)} %collective-permute-done.rest_0_), channel_id=1, source_target_pairs={{0,6},{1,7},{2,4},{3,5},{4,2},{5,3},{6,0},{7,1},{8,14},{9,15},{10,... | collective-permute-start | bytes 393224 | tf_op jit(solution)/shard_map/ppermute | solution.py:309
  19.3 3.7 %binning.1 = (s32[643]{0:T(1024)S(4)}, bf16[192,128,128]{2,1,0:T(8,128)(2,1)S(1)}, bf16[64,128,128]{2,1,0:T(8,128)(2,1)S(1)}) custom-call(s32[1]{0:T(128)S(6)} %copy.28.tile_count, s32[1,4]{1,0:T(1,128)} %hub_in.3, s32[1,4,4]{2,1,0:T(4,128)} %send_in.3, s32[1,192]{1,0:T(1,128)} %row_in.1, s32[1,192]{1,0:T(1,128)} %col_in.1, bf16[192,128,128]{2,1,0:T(8,128)(2,1)} %vals_in.1, ...), custom_call_target="tpu_custom_call" | custom-call | bytes 16777216 | tf_op jit(solution)/shard_map/binning/pallas_call | solution.py:365
  23.0 3.2 %start.1.acc_in = f32[65,128,128]{2,1,0:T(8,128)S(1)} custom-call(s32[643]{0:T(1024)S(4)} %get-tuple-element.37.lists, bf16[192,128,128]{2,1,0:T(8,128)(2,1)S(1)} %get-tuple-element.38.vals, bf16[64,128,128]{2,1,0:T(8,128)(2,1)S(1)} %get-tuple-element.39.field.prev.rest_0_), custom_call_target="tpu_custom_call" | custom-call | flops 402653184 | bytes 25165824 | tf_op jit(solution)/shard_map/start/pallas_call | solution.py:392
  26.2 0.0 collective-permute-done.9.rest_9_
  26.2 0.0 collective-permute-done.4.rest_4_
  26.3 0.0 collective-permute-done.2.rest_2_
  26.3 2.2 %edge.3 = (f32[65,128,128]{2,1,0:T(8,128)S(1)}, bf16[40,128,128]{2,1,0:T(8,128)(2,1)S(1)}, bf16[4,128,128]{2,1,0:T(8,128)(2,1)S(1)}, bf16[4,128,128]{2,1,0:T(8,1...) custom-call(s32[643]{0:T(1024)S(4)} %get-tuple-element.37.lists, ...), custom_call_target="tpu_custom_call", output_to_operand_aliasing={{0}: (3, {})} | custom-call | flops 100663296 | bytes 6029312 | tf_op jit(solution)/shard_map/edge/pallas_call | solution.py:406
  28.5 0.1 collective-permute-start.17
  28.5 0.4 collective-permute-start.13
  28.9 1.8 %collective-permute-start.18 = (bf16[4,128,128]{2,1,0:T(8,128)(2,1)S(1)}, bf16[4,128,128]{2,1,0:T(8,128)(2,1)S(1)}, u32[]{:S(2)}, u32[]{:S(2)}) collective-permute-start(bf16[4,128,128]{2,1,0:T(8,128)(2,1)S(1)} %get-tuple-element.50), channel_id=1, source_target_pairs={{0,16},{8,24},{16,0},{24,8},{1,17},{9,25},{17,1},{25,9},{2,18},{10... | collective-permute-start | bytes 393224 | tf_op jit(solution)/shard_map/ppermute | solution.py:328
  30.7 0.6 collective-permute-start.11
  31.3 2.0 %collective-permute-start.10 = (bf16[4,128,128]{2,1,0:T(8,128)(2,1)S(1)}, bf16[4,128,128]{2,1,0:T(8,128)(2,1)S(1)}, u32[]{:S(2)}, u32[]{:S(2)}) collective-permute-start(bf16[4,128,128]{2,1,0:T(8,128)(2,1)S(1)} %get-tuple-element.48), channel_id=1, source_target_pairs={{0,1},{1,0},{2,3},{3,2},{4,5},{5,4},{6,7},{7,6},{8,9},{9,8},{10,11... | collective-permute-start | bytes 393224 | tf_op jit(solution)/shard_map/ppermute | solution.py:309
  33.3 0.0 collective-permute-done.17.rest_7_
  33.3 0.0 collective-permute-start.19
  33.3 4.9 %collective-permute-done.13.rest_3_ = bf16[4,128,128]{2,1,0:T(8,128)(2,1)S(1)} collective-permute-done((bf16[4,128,128]{2,1,0:T(8,128)(2,1)S(1)}, bf16[4,128,128]{2,1,0:T(8,128)(2,1)S(1)}, u32[]{:S(2)}, u32[]{:S(2)}) %collective-permute-start.13) | collective-permute-done | bytes 131104 | tf_op jit(solution)/shard_map/ppermute | solution.py:309
  38.3 0.0 collective-permute-start.15
  38.3 0.0 collective-permute-done.18.rest_8_
  38.3 0.7 collective-permute-start.14
  38.9 1.4 %collective-permute-start.12 = (bf16[4,128,128]{2,1,0:T(8,128)(2,1)S(1)}, bf16[4,128,128]{2,1,0:T(8,128)(2,1)S(1)}, u32[]{:S(2)}, u32[]{:S(2)}) collective-permute-start(bf16[4,128,128]{2,1,0:T(8,128)(2,1)S(1)} %collective-permute-done.11.rest_1_), channel_id=1, source_target_pairs={{0,1},{1,0},{2,3},{3,2},{4,5},{5,4},{6,7},{7,6},{8,9},{9,8},{10,11... | collective-permute-start | bytes 393224 | tf_op jit(solution)/shard_map/ppermute | solution.py:309
  40.3 0.0 collective-permute-done.10.rest_0_
  40.3 2.8 %collective-permute-start.16 = (bf16[4,128,128]{2,1,0:T(8,128)(2,1)S(1)}, bf16[4,128,128]{2,1,0:T(8,128)(2,1)S(1)}, u32[]{:S(2)}, u32[]{:S(2)}) collective-permute-start(bf16[4,128,128]{2,1,0:T(8,128)(2,1)S(1)} %collective-permute-done.10.rest_0_), channel_id=1, source_target_pairs={{0,6},{1,7},{2,4},{3,5},{4,2},{5,3},{6,0},{7,1},{8,14},{9,15},{10,... | collective-permute-start | bytes 393224 | tf_op jit(solution)/shard_map/ppermute | solution.py:309
  43.1 1.7 %finish.3 = (f32[65,128,128]{2,1,0:T(8,128)S(1)}, bf16[64,128,128]{2,1,0:T(8,128)(2,1)S(1)}) custom-call(s32[643]{0:T(1024)S(4)} %get-tuple-element.37.lists, bf16[192,128,128]{2,1,0:T(8,128)(2,1)S(1)} %get-tuple-element.38.vals, bf16[40,128,128]{2,1,0:T(8,128)(2,1)S(1)} %get-tuple-element.44.rem, ...), custom_call_target="tpu_custom_call", output_to_operand_aliasing={{0}: (4, {})} | custom-call | flops 201326592 | bytes 19922944 | tf_op jit(solution)/shard_map/finish/pallas_call | solution.py:418
  44.8 2.5 %local.3.acc_in = f32[65,128,128]{2,1,0:T(8,128)S(1)} custom-call(s32[643]{0:T(1024)S(4)} %get-tuple-element.37.lists, bf16[192,128,128]{2,1,0:T(8,128)(2,1)S(1)} %get-tuple-element.38.vals, bf16[64,128,128]{2,1,0:T(8,128)(2,1)S(1)} %get-tuple-element.46.field.rest_1_.prev, f32[65,128,128]{2,1,0:T(8,128)S(1)} %get-tuple-element.47.acc_in), custom_call_target="tpu_custom_call", output_to_operand_aliasing={{}: (3, {})} | custom-call | flops 402653184 | bytes 18874368 | tf_op jit(solution)/shard_map/local/pallas_call | solution.py:430
  47.4 0.0 collective-permute-done.19.rest_9_
  47.4 0.0 collective-permute-done.14.rest_4_
  47.4 0.0 collective-permute-done.12.rest_2_
  47.4 2.2 %edge.4 = (f32[65,128,128]{2,1,0:T(8,128)S(1)}, bf16[40,128,128]{2,1,0:T(8,128)(2,1)S(1)}, bf16[4,128,128]{2,1,0:T(8,128)(2,1)S(1)}, bf16[4,128,128]{2,1,0:T(8,1...) custom-call(s32[643]{0:T(1024)S(4)} %get-tuple-element.37.lists, ...), custom_call_target="tpu_custom_call", output_to_operand_aliasing={{0}: (3, {})} | custom-call | flops 100663296 | bytes 6029312 | tf_op jit(solution)/shard_map/edge/pallas_call | solution.py:406
  49.7 0.1 collective-permute-start.27
  49.7 2.2 %collective-permute-start.23 = (bf16[4,128,128]{2,1,0:T(8,128)(2,1)S(1)}, bf16[4,128,128]{2,1,0:T(8,128)(2,1)S(1)}, u32[]{:S(2)}, u32[]{:S(2)}) collective-permute-start(bf16[4,128,128]{2,1,0:T(8,128)(2,1)S(1)} %get-tuple-element.56), channel_id=1, source_target_pairs={{0,4},{1,5},{2,6},{3,7},{4,0},{5,1},{6,2},{7,3},{8,12},{9,13},{10,... | collective-permute-start | bytes 393224 | tf_op jit(solution)/shard_map/ppermute | solution.py:309
  52.0 1.1 %collective-permute-start.28 = (bf16[4,128,128]{2,1,0:T(8,128)(2,1)S(1)}, bf16[4,128,128]{2,1,0:T(8,128)(2,1)S(1)}, u32[]{:S(2)}, u32[]{:S(2)}) collective-permute-start(bf16[4,128,128]{2,1,0:T(8,128)(2,1)S(1)} %get-tuple-element.58), channel_id=1, source_target_pairs={{0,16},{8,24},{16,0},{24,8},{1,17},{9,25},{17,1},{25,9},{2,18},{10... | collective-permute-start | bytes 393224 | tf_op jit(solution)/shard_map/ppermute | solution.py:328
  53.1 0.3 collective-permute-start.21
  53.4 1.3 %collective-permute-start.20 = (bf16[4,128,128]{2,1,0:T(8,128)(2,1)S(1)}, bf16[4,128,128]{2,1,0:T(8,128)(2,1)S(1)}, u32[]{:S(2)}, u32[]{:S(2)}) collective-permute-start(bf16[4,128,128]{2,1,0:T(8,128)(2,1)S(1)} %get-tuple-element.56), channel_id=1, source_target_pairs={{0,1},{1,0},{2,3},{3,2},{4,5},{5,4},{6,7},{7,6},{8,9},{9,8},{10,11... | collective-permute-start | bytes 393224 | tf_op jit(solution)/shard_map/ppermute | solution.py:309
  54.8 0.0 collective-permute-done.27.rest_7_
  54.8 0.0 collective-permute-start.29
  54.8 4.7 %collective-permute-done.23.rest_3_ = bf16[4,128,128]{2,1,0:T(8,128)(2,1)S(1)} collective-permute-done((bf16[4,128,128]{2,1,0:T(8,128)(2,1)S(1)}, bf16[4,128,128]{2,1,0:T(8,128)(2,1)S(1)}, u32[]{:S(2)}, u32[]{:S(2)}) %collective-permute-start.23) | collective-permute-done | bytes 131104 | tf_op jit(solution)/shard_map/ppermute | solution.py:309
  59.5 0.5 collective-permute-start.24
  60.0 1.6 %collective-permute-start.22 = (bf16[4,128,128]{2,1,0:T(8,128)(2,1)S(1)}, bf16[4,128,128]{2,1,0:T(8,128)(2,1)S(1)}, u32[]{:S(2)}, u32[]{:S(2)}) collective-permute-start(bf16[4,128,128]{2,1,0:T(8,128)(2,1)S(1)} %collective-permute-done.21.rest_1_), channel_id=1, source_target_pairs={{0,1},{1,0},{2,3},{3,2},{4,5},{5,4},{6,7},{7,6},{8,9},{9,8},{10,11... | collective-permute-start | bytes 393224 | tf_op jit(solution)/shard_map/ppermute | solution.py:309
  61.5 2.5 %collective-permute-start.26 = (bf16[4,128,128]{2,1,0:T(8,128)(2,1)S(1)}, bf16[4,128,128]{2,1,0:T(8,128)(2,1)S(1)}, u32[]{:S(2)}, u32[]{:S(2)}) collective-permute-start(bf16[4,128,128]{2,1,0:T(8,128)(2,1)S(1)} %collective-permute-done.20.rest_0_), channel_id=1, source_target_pairs={{0,6},{1,7},{2,4},{3,5},{4,2},{5,3},{6,0},{7,1},{8,14},{9,15},{10,... | collective-permute-start | bytes 393224 | tf_op jit(solution)/shard_map/ppermute | solution.py:309
  64.0 2.1 %finish.4 = (f32[65,128,128]{2,1,0:T(8,128)S(1)}, bf16[64,128,128]{2,1,0:T(8,128)(2,1)S(1)}) custom-call(s32[643]{0:T(1024)S(4)} %get-tuple-element.37.lists, bf16[192,128,128]{2,1,0:T(8,128)(2,1)S(1)} %get-tuple-element.38.vals, bf16[40,128,128]{2,1,0:T(8,128)(2,1)S(1)} %get-tuple-element.52.rem, ...), custom_call_target="tpu_custom_call", output_to_operand_aliasing={{0}: (5, {})} | custom-call | flops 201326592 | bytes 19922944 | tf_op jit(solution)/shard_map/finish/pallas_call | solution.py:418
  66.1 2.5 %local.4.acc_in = f32[65,128,128]{2,1,0:T(8,128)S(1)} custom-call(s32[643]{0:T(1024)S(4)} %get-tuple-element.37.lists, bf16[192,128,128]{2,1,0:T(8,128)(2,1)S(1)} %get-tuple-element.38.vals, bf16[64,128,128]{2,1,0:T(8,128)(2,1)S(1)} %get-tuple-element.54.field.rest_2_, f32[65,128,128]{2,1,0:T(8,128)S(1)} %get-tuple-element.55.acc_in), custom_call_target="tpu_custom_call", output_to_operand_aliasing={{}: (3, {})} | custom-call | flops 402653184 | bytes 18874368 | tf_op jit(solution)/shard_map/local/pallas_call | solution.py:430
  68.7 2.2 %edge.5 = (f32[65,128,128]{2,1,0:T(8,128)S(1)}, bf16[40,128,128]{2,1,0:T(8,128)(2,1)S(1)}, bf16[4,128,128]{2,1,0:T(8,128)(2,1)S(1)}, bf16[4,128,128]{2,1,0:T(8,1...) custom-call(s32[643]{0:T(1024)S(4)} %get-tuple-element.37.lists, ...), custom_call_target="tpu_custom_call", output_to_operand_aliasing={{0}: (3, {})} | custom-call | flops 100663296 | bytes 6029312 | tf_op jit(solution)/shard_map/edge/pallas_call | solution.py:406
  70.9 0.1 collective-permute-start.37
  71.0 2.9 %collective-permute-start.33 = (bf16[4,128,128]{2,1,0:T(8,128)(2,1)S(1)}, bf16[4,128,128]{2,1,0:T(8,128)(2,1)S(1)}, u32[]{:S(2)}, u32[]{:S(2)}) collective-permute-start(bf16[4,128,128]{2,1,0:T(8,128)(2,1)S(1)} %get-tuple-element.64), channel_id=1, source_target_pairs={{0,4},{1,5},{2,6},{3,7},{4,0},{5,1},{6,2},{7,3},{8,12},{9,13},{10,... | collective-permute-start | bytes 393224 | tf_op jit(solution)/shard_map/ppermute | solution.py:309
  73.9 0.5 collective-permute-start.38
  74.4 1.7 %collective-permute-start.30 = (bf16[4,128,128]{2,1,0:T(8,128)(2,1)S(1)}, bf16[4,128,128]{2,1,0:T(8,128)(2,1)S(1)}, u32[]{:S(2)}, u32[]{:S(2)}) collective-permute-start(bf16[4,128,128]{2,1,0:T(8,128)(2,1)S(1)} %get-tuple-element.64), channel_id=1, source_target_pairs={{0,1},{1,0},{2,3},{3,2},{4,5},{5,4},{6,7},{7,6},{8,9},{9,8},{10,11... | collective-permute-start | bytes 393224 | tf_op jit(solution)/shard_map/ppermute | solution.py:309
  76.1 4.8 %collective-permute-done.33.rest_3_ = bf16[4,128,128]{2,1,0:T(8,128)(2,1)S(1)} collective-permute-done((bf16[4,128,128]{2,1,0:T(8,128)(2,1)S(1)}, bf16[4,128,128]{2,1,0:T(8,128)(2,1)S(1)}, u32[]{:S(2)}, u32[]{:S(2)}) %collective-permute-start.33) | collective-permute-done | bytes 131104 | tf_op jit(solution)/shard_map/ppermute | solution.py:309
  80.9 0.4 collective-permute-start.34
  81.2 0.1 collective-permute-done.31.rest_1_
  81.4 1.5 %collective-permute-start.32 = (bf16[4,128,128]{2,1,0:T(8,128)(2,1)S(1)}, bf16[4,128,128]{2,1,0:T(8,128)(2,1)S(1)}, u32[]{:S(2)}, u32[]{:S(2)}) collective-permute-start(bf16[4,128,128]{2,1,0:T(8,128)(2,1)S(1)} %collective-permute-done.31.rest_1_), channel_id=1, source_target_pairs={{0,1},{1,0},{2,3},{3,2},{4,5},{5,4},{6,7},{7,6},{8,9},{9,8},{10,11... | collective-permute-start | bytes 393224 | tf_op jit(solution)/shard_map/ppermute | solution.py:309
  82.9 1.8 %collective-permute-start.36 = (bf16[4,128,128]{2,1,0:T(8,128)(2,1)S(1)}, bf16[4,128,128]{2,1,0:T(8,128)(2,1)S(1)}, u32[]{:S(2)}, u32[]{:S(2)}) collective-permute-start(bf16[4,128,128]{2,1,0:T(8,128)(2,1)S(1)} %collective-permute-done.30.rest_0_), channel_id=1, source_target_pairs={{0,6},{1,7},{2,4},{3,5},{4,2},{5,3},{6,0},{7,1},{8,14},{9,15},{10,... | collective-permute-start | bytes 393224 | tf_op jit(solution)/shard_map/ppermute | solution.py:309
  84.8 3.2 %finish.5 = (f32[65,128,128]{2,1,0:T(8,128)S(1)}, bf16[64,128,128]{2,1,0:T(8,128)(2,1)S(1)}) custom-call(s32[643]{0:T(1024)S(4)} %get-tuple-element.37.lists, bf16[192,128,128]{2,1,0:T(8,128)(2,1)S(1)} %get-tuple-element.38.vals, bf16[40,128,128]{2,1,0:T(8,128)(2,1)S(1)} %get-tuple-element.60.rem, ...), custom_call_target="tpu_custom_call", output_to_operand_aliasing={{0}: (6, {})} | custom-call | flops 201326592 | bytes 19922944 | tf_op jit(solution)/shard_map/finish/pallas_call | solution.py:418
  87.9 2.5 %local.5.acc_in = f32[65,128,128]{2,1,0:T(8,128)S(1)} custom-call(s32[643]{0:T(1024)S(4)} %get-tuple-element.37.lists, bf16[192,128,128]{2,1,0:T(8,128)(2,1)S(1)} %get-tuple-element.38.vals, bf16[64,128,128]{2,1,0:T(8,128)(2,1)S(1)} %get-tuple-element.62.field, f32[65,128,128]{2,1,0:T(8,128)S(1)} %get-tuple-element.63.acc_in), custom_call_target="tpu_custom_call", output_to_operand_aliasing={{}: (3, {})} | custom-call | flops 402653184 | bytes 18874368 | tf_op jit(solution)/shard_map/local/pallas_call | solution.py:430
  90.5 5.1 %last.1 = (f32[65,128,128]{2,1,0:T(8,128)S(1)}, f32[64,128,128]{2,1,0:T(8,128)}) custom-call(s32[643]{0:T(1024)S(4)} %get-tuple-element.37.lists, bf16[192,128,128]{2,1,0:T(8,128)(2,1)S(1)} %get-tuple-element.38.vals, f32[65,128,128]{2,1,0:T(8,128)S(1)} %local.5.acc_in, ...), custom_call_target="tpu_custom_call", output_to_operand_aliasing={{0}: (2, {})} | custom-call | tf_op jit(solution)/shard_map/last/pallas_call | solution.py:441
  (29 shorter events, 0.1 us)
Async XLA Ops:
  1.9 8.8 %collective-permute-start.7 = (bf16[4,128,128]{2,1,0:T(8,128)(2,1)S(1)}, bf16[4,128,128]{2,1,0:T(8,128)(2,1)S(1)}, u32[]{:S(2)}, u32[]{:S(2)}) collective-permute-start(bf16[4,128,128]{2,1,0:T(8,128)(2,1)S(1)} %get-tuple-element.41), channel_id=1, source_target_pairs={{0,8},{8,0},{16,24},{24,16},{1,9},{9,1},{17,25},{25,17},{2,10},{10... | collective-permute-start | bytes 393224 | tf_op jit(solution)/shard_map/ppermute | solution.py:328
  2.4 10.7 %collective-permute-start.3 = (bf16[4,128,128]{2,1,0:T(8,128)(2,1)S(1)}, bf16[4,128,128]{2,1,0:T(8,128)(2,1)S(1)}, u32[]{:S(2)}, u32[]{:S(2)}) collective-permute-start(bf16[4,128,128]{2,1,0:T(8,128)(2,1)S(1)} %get-tuple-element.40), channel_id=1, source_target_pairs={{0,4},{1,5},{2,6},{3,7},{4,0},{5,1},{6,2},{7,3},{8,12},{9,13},{10,... | collective-permute-start | bytes 393224 | tf_op jit(solution)/shard_map/ppermute | solution.py:309
  6.0 7.7 %collective-permute-start.8 = (bf16[4,128,128]{2,1,0:T(8,128)(2,1)S(1)}, bf16[4,128,128]{2,1,0:T(8,128)(2,1)S(1)}, u32[]{:S(2)}, u32[]{:S(2)}) collective-permute-start(bf16[4,128,128]{2,1,0:T(8,128)(2,1)S(1)} %get-tuple-element.42), channel_id=1, source_target_pairs={{0,16},{8,24},{16,0},{24,8},{1,17},{9,25},{17,1},{25,9},{2,18},{10... | collective-permute-start | bytes 393224 | tf_op jit(solution)/shard_map/ppermute | solution.py:328
  7.5 7.7 %collective-permute-start.1 = (bf16[4,128,128]{2,1,0:T(8,128)(2,1)S(1)}, bf16[4,128,128]{2,1,0:T(8,128)(2,1)S(1)}, u32[]{:S(2)}, u32[]{:S(2)}) collective-permute-start(bf16[4,128,128]{2,1,0:T(8,128)(2,1)S(1)} %get-tuple-element.40), channel_id=1, source_target_pairs={{0,2},{1,3},{2,0},{3,1},{4,6},{5,7},{6,4},{7,5},{8,10},{9,11},{10,... | collective-permute-start | bytes 393224 | tf_op jit(solution)/shard_map/ppermute | solution.py:309
  9.1 6.9 %collective-permute-start = (bf16[4,128,128]{2,1,0:T(8,128)(2,1)S(1)}, bf16[4,128,128]{2,1,0:T(8,128)(2,1)S(1)}, u32[]{:S(2)}, u32[]{:S(2)}) collective-permute-start(bf16[4,128,128]{2,1,0:T(8,128)(2,1)S(1)} %get-tuple-element.40), channel_id=1, source_target_pairs={{0,1},{1,0},{2,3},{3,2},{4,5},{5,4},{6,7},{7,6},{8,9},{9,8},{10,11... | collective-permute-start | bytes 393224 | tf_op jit(solution)/shard_map/ppermute | solution.py:309
  10.6 15.6 %collective-permute-start.9 = (bf16[4,128,128]{2,1,0:T(8,128)(2,1)S(1)}, bf16[4,128,128]{2,1,0:T(8,128)(2,1)S(1)}, u32[]{:S(2)}, u32[]{:S(2)}) collective-permute-start(bf16[4,128,128]{2,1,0:T(8,128)(2,1)S(1)} %get-tuple-element.43), channel_id=1, source_target_pairs={{0,24},{8,16},{16,8},{24,0},{1,25},{9,17},{17,9},{25,1},{2,26},{10... | collective-permute-start | bytes 393224 | tf_op jit(solution)/shard_map/ppermute | solution.py:328
  13.1 13.2 %collective-permute-start.5 = (bf16[4,128,128]{2,1,0:T(8,128)(2,1)S(1)}, bf16[4,128,128]{2,1,0:T(8,128)(2,1)S(1)}, u32[]{:S(2)}, u32[]{:S(2)}) collective-permute-start(bf16[4,128,128]{2,1,0:T(8,128)(2,1)S(1)} %collective-permute-done.3.rest_3_), channel_id=1, source_target_pairs={{0,2},{1,3},{2,0},{3,1},{4,6},{5,7},{6,4},{7,5},{8,10},{9,11},{10,... | collective-permute-start | bytes 393224 | tf_op jit(solution)/shard_map/ppermute | solution.py:309
  13.8 12.5 %collective-permute-start.4 = (bf16[4,128,128]{2,1,0:T(8,128)(2,1)S(1)}, bf16[4,128,128]{2,1,0:T(8,128)(2,1)S(1)}, u32[]{:S(2)}, u32[]{:S(2)}) collective-permute-start(bf16[4,128,128]{2,1,0:T(8,128)(2,1)S(1)} %collective-permute-done.3.rest_3_), channel_id=1, source_target_pairs={{0,1},{1,0},{2,3},{3,2},{4,5},{5,4},{6,7},{7,6},{8,9},{9,8},{10,11... | collective-permute-start | bytes 393224 | tf_op jit(solution)/shard_map/ppermute | solution.py:309
  15.3 11.0 %collective-permute-start.2 = (bf16[4,128,128]{2,1,0:T(8,128)(2,1)S(1)}, bf16[4,128,128]{2,1,0:T(8,128)(2,1)S(1)}, u32[]{:S(2)}, u32[]{:S(2)}) collective-permute-start(bf16[4,128,128]{2,1,0:T(8,128)(2,1)S(1)} %collective-permute-done.1.rest_1_), channel_id=1, source_target_pairs={{0,1},{1,0},{2,3},{3,2},{4,5},{5,4},{6,7},{7,6},{8,9},{9,8},{10,11... | collective-permute-start | bytes 393224 | tf_op jit(solution)/shard_map/ppermute | solution.py:309
  16.0 10.2 %collective-permute-start.6 = (bf16[4,128,128]{2,1,0:T(8,128)(2,1)S(1)}, bf16[4,128,128]{2,1,0:T(8,128)(2,1)S(1)}, u32[]{:S(2)}, u32[]{:S(2)}) collective-permute-start(bf16[4,128,128]{2,1,0:T(8,128)(2,1)S(1)} %collective-permute-done.rest_0_), channel_id=1, source_target_pairs={{0,6},{1,7},{2,4},{3,5},{4,2},{5,3},{6,0},{7,1},{8,14},{9,15},{10,... | collective-permute-start | bytes 393224 | tf_op jit(solution)/shard_map/ppermute | solution.py:309
  28.5 4.9 %collective-permute-start.17 = (bf16[4,128,128]{2,1,0:T(8,128)(2,1)S(1)}, bf16[4,128,128]{2,1,0:T(8,128)(2,1)S(1)}, u32[]{:S(2)}, u32[]{:S(2)}) collective-permute-start(bf16[4,128,128]{2,1,0:T(8,128)(2,1)S(1)} %get-tuple-element.49), channel_id=1, source_target_pairs={{0,8},{8,0},{16,24},{24,16},{1,9},{9,1},{17,25},{25,17},{2,10},{10... | collective-permute-start | bytes 393224 | tf_op jit(solution)/shard_map/ppermute | solution.py:328
  28.5 9.7 %collective-permute-start.13 = (bf16[4,128,128]{2,1,0:T(8,128)(2,1)S(1)}, bf16[4,128,128]{2,1,0:T(8,128)(2,1)S(1)}, u32[]{:S(2)}, u32[]{:S(2)}) collective-permute-start(bf16[4,128,128]{2,1,0:T(8,128)(2,1)S(1)} %get-tuple-element.48), channel_id=1, source_target_pairs={{0,4},{1,5},{2,6},{3,7},{4,0},{5,1},{6,2},{7,3},{8,12},{9,13},{10,... | collective-permute-start | bytes 393224 | tf_op jit(solution)/shard_map/ppermute | solution.py:309
  28.9 9.4 %collective-permute-start.18 = (bf16[4,128,128]{2,1,0:T(8,128)(2,1)S(1)}, bf16[4,128,128]{2,1,0:T(8,128)(2,1)S(1)}, u32[]{:S(2)}, u32[]{:S(2)}) collective-permute-start(bf16[4,128,128]{2,1,0:T(8,128)(2,1)S(1)} %get-tuple-element.50), channel_id=1, source_target_pairs={{0,16},{8,24},{16,0},{24,8},{1,17},{9,25},{17,1},{25,9},{2,18},{10... | collective-permute-start | bytes 393224 | tf_op jit(solution)/shard_map/ppermute | solution.py:328
  30.7 8.3 %collective-permute-start.11 = (bf16[4,128,128]{2,1,0:T(8,128)(2,1)S(1)}, bf16[4,128,128]{2,1,0:T(8,128)(2,1)S(1)}, u32[]{:S(2)}, u32[]{:S(2)}) collective-permute-start(bf16[4,128,128]{2,1,0:T(8,128)(2,1)S(1)} %get-tuple-element.48), channel_id=1, source_target_pairs={{0,2},{1,3},{2,0},{3,1},{4,6},{5,7},{6,4},{7,5},{8,10},{9,11},{10,... | collective-permute-start | bytes 393224 | tf_op jit(solution)/shard_map/ppermute | solution.py:309
  31.3 9.0 %collective-permute-start.10 = (bf16[4,128,128]{2,1,0:T(8,128)(2,1)S(1)}, bf16[4,128,128]{2,1,0:T(8,128)(2,1)S(1)}, u32[]{:S(2)}, u32[]{:S(2)}) collective-permute-start(bf16[4,128,128]{2,1,0:T(8,128)(2,1)S(1)} %get-tuple-element.48), channel_id=1, source_target_pairs={{0,1},{1,0},{2,3},{3,2},{4,5},{5,4},{6,7},{7,6},{8,9},{9,8},{10,11... | collective-permute-start | bytes 393224 | tf_op jit(solution)/shard_map/ppermute | solution.py:309
  33.3 14.0 %collective-permute-start.19 = (bf16[4,128,128]{2,1,0:T(8,128)(2,1)S(1)}, bf16[4,128,128]{2,1,0:T(8,128)(2,1)S(1)}, u32[]{:S(2)}, u32[]{:S(2)}) collective-permute-start(bf16[4,128,128]{2,1,0:T(8,128)(2,1)S(1)} %get-tuple-element.51), channel_id=1, source_target_pairs={{0,24},{8,16},{16,8},{24,0},{1,25},{9,17},{17,9},{25,1},{2,26},{10... | collective-permute-start | bytes 393224 | tf_op jit(solution)/shard_map/ppermute | solution.py:328
  38.3 9.1 %collective-permute-start.15 = (bf16[4,128,128]{2,1,0:T(8,128)(2,1)S(1)}, bf16[4,128,128]{2,1,0:T(8,128)(2,1)S(1)}, u32[]{:S(2)}, u32[]{:S(2)}) collective-permute-start(bf16[4,128,128]{2,1,0:T(8,128)(2,1)S(1)} %collective-permute-done.13.rest_3_), channel_id=1, source_target_pairs={{0,2},{1,3},{2,0},{3,1},{4,6},{5,7},{6,4},{7,5},{8,10},{9,11},{10,... | collective-permute-start | bytes 393224 | tf_op jit(solution)/shard_map/ppermute | solution.py:309
  38.3 9.1 %collective-permute-start.14 = (bf16[4,128,128]{2,1,0:T(8,128)(2,1)S(1)}, bf16[4,128,128]{2,1,0:T(8,128)(2,1)S(1)}, u32[]{:S(2)}, u32[]{:S(2)}) collective-permute-start(bf16[4,128,128]{2,1,0:T(8,128)(2,1)S(1)} %collective-permute-done.13.rest_3_), channel_id=1, source_target_pairs={{0,1},{1,0},{2,3},{3,2},{4,5},{5,4},{6,7},{7,6},{8,9},{9,8},{10,11... | collective-permute-start | bytes 393224 | tf_op jit(solution)/shard_map/ppermute | solution.py:309
  38.9 8.5 %collective-permute-start.12 = (bf16[4,128,128]{2,1,0:T(8,128)(2,1)S(1)}, bf16[4,128,128]{2,1,0:T(8,128)(2,1)S(1)}, u32[]{:S(2)}, u32[]{:S(2)}) collective-permute-start(bf16[4,128,128]{2,1,0:T(8,128)(2,1)S(1)} %collective-permute-done.11.rest_1_), channel_id=1, source_target_pairs={{0,1},{1,0},{2,3},{3,2},{4,5},{5,4},{6,7},{7,6},{8,9},{9,8},{10,11... | collective-permute-start | bytes 393224 | tf_op jit(solution)/shard_map/ppermute | solution.py:309
  40.3 7.1 %collective-permute-start.16 = (bf16[4,128,128]{2,1,0:T(8,128)(2,1)S(1)}, bf16[4,128,128]{2,1,0:T(8,128)(2,1)S(1)}, u32[]{:S(2)}, u32[]{:S(2)}) collective-permute-start(bf16[4,128,128]{2,1,0:T(8,128)(2,1)S(1)} %collective-permute-done.10.rest_0_), channel_id=1, source_target_pairs={{0,6},{1,7},{2,4},{3,5},{4,2},{5,3},{6,0},{7,1},{8,14},{9,15},{10,... | collective-permute-start | bytes 393224 | tf_op jit(solution)/shard_map/ppermute | solution.py:309
  49.7 5.1 %collective-permute-start.27 = (bf16[4,128,128]{2,1,0:T(8,128)(2,1)S(1)}, bf16[4,128,128]{2,1,0:T(8,128)(2,1)S(1)}, u32[]{:S(2)}, u32[]{:S(2)}) collective-permute-start(bf16[4,128,128]{2,1,0:T(8,128)(2,1)S(1)} %get-tuple-element.57), channel_id=1, source_target_pairs={{0,8},{8,0},{16,24},{24,16},{1,9},{9,1},{17,25},{25,17},{2,10},{10... | collective-permute-start | bytes 393224 | tf_op jit(solution)/shard_map/ppermute | solution.py:328
  49.7 9.7 %collective-permute-start.23 = (bf16[4,128,128]{2,1,0:T(8,128)(2,1)S(1)}, bf16[4,128,128]{2,1,0:T(8,128)(2,1)S(1)}, u32[]{:S(2)}, u32[]{:S(2)}) collective-permute-start(bf16[4,128,128]{2,1,0:T(8,128)(2,1)S(1)} %get-tuple-element.56), channel_id=1, source_target_pairs={{0,4},{1,5},{2,6},{3,7},{4,0},{5,1},{6,2},{7,3},{8,12},{9,13},{10,... | collective-permute-start | bytes 393224 | tf_op jit(solution)/shard_map/ppermute | solution.py:309
  52.0 7.5 %collective-permute-start.28 = (bf16[4,128,128]{2,1,0:T(8,128)(2,1)S(1)}, bf16[4,128,128]{2,1,0:T(8,128)(2,1)S(1)}, u32[]{:S(2)}, u32[]{:S(2)}) collective-permute-start(bf16[4,128,128]{2,1,0:T(8,128)(2,1)S(1)} %get-tuple-element.58), channel_id=1, source_target_pairs={{0,16},{8,24},{16,0},{24,8},{1,17},{9,25},{17,1},{25,9},{2,18},{10... | collective-permute-start | bytes 393224 | tf_op jit(solution)/shard_map/ppermute | solution.py:328
  53.1 6.9 %collective-permute-start.21 = (bf16[4,128,128]{2,1,0:T(8,128)(2,1)S(1)}, bf16[4,128,128]{2,1,0:T(8,128)(2,1)S(1)}, u32[]{:S(2)}, u32[]{:S(2)}) collective-permute-start(bf16[4,128,128]{2,1,0:T(8,128)(2,1)S(1)} %get-tuple-element.56), channel_id=1, source_target_pairs={{0,2},{1,3},{2,0},{3,1},{4,6},{5,7},{6,4},{7,5},{8,10},{9,11},{10,... | collective-permute-start | bytes 393224 | tf_op jit(solution)/shard_map/ppermute | solution.py:309
  53.4 8.1 %collective-permute-start.20 = (bf16[4,128,128]{2,1,0:T(8,128)(2,1)S(1)}, bf16[4,128,128]{2,1,0:T(8,128)(2,1)S(1)}, u32[]{:S(2)}, u32[]{:S(2)}) collective-permute-start(bf16[4,128,128]{2,1,0:T(8,128)(2,1)S(1)} %get-tuple-element.56), channel_id=1, source_target_pairs={{0,1},{1,0},{2,3},{3,2},{4,5},{5,4},{6,7},{7,6},{8,9},{9,8},{10,11... | collective-permute-start | bytes 393224 | tf_op jit(solution)/shard_map/ppermute | solution.py:309
  54.8 13.8 %collective-permute-start.29 = (bf16[4,128,128]{2,1,0:T(8,128)(2,1)S(1)}, bf16[4,128,128]{2,1,0:T(8,128)(2,1)S(1)}, u32[]{:S(2)}, u32[]{:S(2)}) collective-permute-start(bf16[4,128,128]{2,1,0:T(8,128)(2,1)S(1)} %get-tuple-element.59), channel_id=1, source_target_pairs={{0,24},{8,16},{16,8},{24,0},{1,25},{9,17},{17,9},{25,1},{2,26},{10... | collective-permute-start | bytes 393224 | tf_op jit(solution)/shard_map/ppermute | solution.py:328
  59.5 9.1 %collective-permute-start.25 = (bf16[4,128,128]{2,1,0:T(8,128)(2,1)S(1)}, bf16[4,128,128]{2,1,0:T(8,128)(2,1)S(1)}, u32[]{:S(2)}, u32[]{:S(2)}) collective-permute-start(bf16[4,128,128]{2,1,0:T(8,128)(2,1)S(1)} %collective-permute-done.23.rest_3_), channel_id=1, source_target_pairs={{0,2},{1,3},{2,0},{3,1},{4,6},{5,7},{6,4},{7,5},{8,10},{9,11},{10,... | collective-permute-start | bytes 393224 | tf_op jit(solution)/shard_map/ppermute | solution.py:309
  59.5 9.2 %collective-permute-start.24 = (bf16[4,128,128]{2,1,0:T(8,128)(2,1)S(1)}, bf16[4,128,128]{2,1,0:T(8,128)(2,1)S(1)}, u32[]{:S(2)}, u32[]{:S(2)}) collective-permute-start(bf16[4,128,128]{2,1,0:T(8,128)(2,1)S(1)} %collective-permute-done.23.rest_3_), channel_id=1, source_target_pairs={{0,1},{1,0},{2,3},{3,2},{4,5},{5,4},{6,7},{7,6},{8,9},{9,8},{10,11... | collective-permute-start | bytes 393224 | tf_op jit(solution)/shard_map/ppermute | solution.py:309
  60.0 8.7 %collective-permute-start.22 = (bf16[4,128,128]{2,1,0:T(8,128)(2,1)S(1)}, bf16[4,128,128]{2,1,0:T(8,128)(2,1)S(1)}, u32[]{:S(2)}, u32[]{:S(2)}) collective-permute-start(bf16[4,128,128]{2,1,0:T(8,128)(2,1)S(1)} %collective-permute-done.21.rest_1_), channel_id=1, source_target_pairs={{0,1},{1,0},{2,3},{3,2},{4,5},{5,4},{6,7},{7,6},{8,9},{9,8},{10,11... | collective-permute-start | bytes 393224 | tf_op jit(solution)/shard_map/ppermute | solution.py:309
  61.5 7.1 %collective-permute-start.26 = (bf16[4,128,128]{2,1,0:T(8,128)(2,1)S(1)}, bf16[4,128,128]{2,1,0:T(8,128)(2,1)S(1)}, u32[]{:S(2)}, u32[]{:S(2)}) collective-permute-start(bf16[4,128,128]{2,1,0:T(8,128)(2,1)S(1)} %collective-permute-done.20.rest_0_), channel_id=1, source_target_pairs={{0,6},{1,7},{2,4},{3,5},{4,2},{5,3},{6,0},{7,1},{8,14},{9,15},{10,... | collective-permute-start | bytes 393224 | tf_op jit(solution)/shard_map/ppermute | solution.py:309
  70.9 5.2 %collective-permute-start.37 = (bf16[4,128,128]{2,1,0:T(8,128)(2,1)S(1)}, bf16[4,128,128]{2,1,0:T(8,128)(2,1)S(1)}, u32[]{:S(2)}, u32[]{:S(2)}) collective-permute-start(bf16[4,128,128]{2,1,0:T(8,128)(2,1)S(1)} %get-tuple-element.65), channel_id=1, source_target_pairs={{0,8},{8,0},{16,24},{24,16},{1,9},{9,1},{17,25},{25,17},{2,10},{10... | collective-permute-start | bytes 393224 | tf_op jit(solution)/shard_map/ppermute | solution.py:328
  71.0 9.9 %collective-permute-start.33 = (bf16[4,128,128]{2,1,0:T(8,128)(2,1)S(1)}, bf16[4,128,128]{2,1,0:T(8,128)(2,1)S(1)}, u32[]{:S(2)}, u32[]{:S(2)}) collective-permute-start(bf16[4,128,128]{2,1,0:T(8,128)(2,1)S(1)} %get-tuple-element.64), channel_id=1, source_target_pairs={{0,4},{1,5},{2,6},{3,7},{4,0},{5,1},{6,2},{7,3},{8,12},{9,13},{10,... | collective-permute-start | bytes 393224 | tf_op jit(solution)/shard_map/ppermute | solution.py:309
  73.9 7.0 %collective-permute-start.38 = (bf16[4,128,128]{2,1,0:T(8,128)(2,1)S(1)}, bf16[4,128,128]{2,1,0:T(8,128)(2,1)S(1)}, u32[]{:S(2)}, u32[]{:S(2)}) collective-permute-start(bf16[4,128,128]{2,1,0:T(8,128)(2,1)S(1)} %get-tuple-element.66), channel_id=1, source_target_pairs={{0,16},{8,24},{16,0},{24,8},{1,17},{9,25},{17,1},{25,9},{2,18},{10... | collective-permute-start | bytes 393224 | tf_op jit(solution)/shard_map/ppermute | solution.py:328
  74.4 7.0 %collective-permute-start.31 = (bf16[4,128,128]{2,1,0:T(8,128)(2,1)S(1)}, bf16[4,128,128]{2,1,0:T(8,128)(2,1)S(1)}, u32[]{:S(2)}, u32[]{:S(2)}) collective-permute-start(bf16[4,128,128]{2,1,0:T(8,128)(2,1)S(1)} %get-tuple-element.64), channel_id=1, source_target_pairs={{0,2},{1,3},{2,0},{3,1},{4,6},{5,7},{6,4},{7,5},{8,10},{9,11},{10,... | collective-permute-start | bytes 393224 | tf_op jit(solution)/shard_map/ppermute | solution.py:309
  74.4 8.5 %collective-permute-start.30 = (bf16[4,128,128]{2,1,0:T(8,128)(2,1)S(1)}, bf16[4,128,128]{2,1,0:T(8,128)(2,1)S(1)}, u32[]{:S(2)}, u32[]{:S(2)}) collective-permute-start(bf16[4,128,128]{2,1,0:T(8,128)(2,1)S(1)} %get-tuple-element.64), channel_id=1, source_target_pairs={{0,1},{1,0},{2,3},{3,2},{4,5},{5,4},{6,7},{7,6},{8,9},{9,8},{10,11... | collective-permute-start | bytes 393224 | tf_op jit(solution)/shard_map/ppermute | solution.py:309
  76.1 14.3 %collective-permute-start.39 = (bf16[4,128,128]{2,1,0:T(8,128)(2,1)S(1)}, bf16[4,128,128]{2,1,0:T(8,128)(2,1)S(1)}, u32[]{:S(2)}, u32[]{:S(2)}) collective-permute-start(bf16[4,128,128]{2,1,0:T(8,128)(2,1)S(1)} %get-tuple-element.67), channel_id=1, source_target_pairs={{0,24},{8,16},{16,8},{24,0},{1,25},{9,17},{17,9},{25,1},{2,26},{10... | collective-permute-start | bytes 393224 | tf_op jit(solution)/shard_map/ppermute | solution.py:328
  80.9 9.6 %collective-permute-start.35 = (bf16[4,128,128]{2,1,0:T(8,128)(2,1)S(1)}, bf16[4,128,128]{2,1,0:T(8,128)(2,1)S(1)}, u32[]{:S(2)}, u32[]{:S(2)}) collective-permute-start(bf16[4,128,128]{2,1,0:T(8,128)(2,1)S(1)} %collective-permute-done.33.rest_3_), channel_id=1, source_target_pairs={{0,2},{1,3},{2,0},{3,1},{4,6},{5,7},{6,4},{7,5},{8,10},{9,11},{10,... | collective-permute-start | bytes 393224 | tf_op jit(solution)/shard_map/ppermute | solution.py:309
  80.9 9.6 %collective-permute-start.34 = (bf16[4,128,128]{2,1,0:T(8,128)(2,1)S(1)}, bf16[4,128,128]{2,1,0:T(8,128)(2,1)S(1)}, u32[]{:S(2)}, u32[]{:S(2)}) collective-permute-start(bf16[4,128,128]{2,1,0:T(8,128)(2,1)S(1)} %collective-permute-done.33.rest_3_), channel_id=1, source_target_pairs={{0,1},{1,0},{2,3},{3,2},{4,5},{5,4},{6,7},{7,6},{8,9},{9,8},{10,11... | collective-permute-start | bytes 393224 | tf_op jit(solution)/shard_map/ppermute | solution.py:309
  81.4 9.1 %collective-permute-start.32 = (bf16[4,128,128]{2,1,0:T(8,128)(2,1)S(1)}, bf16[4,128,128]{2,1,0:T(8,128)(2,1)S(1)}, u32[]{:S(2)}, u32[]{:S(2)}) collective-permute-start(bf16[4,128,128]{2,1,0:T(8,128)(2,1)S(1)} %collective-permute-done.31.rest_1_), channel_id=1, source_target_pairs={{0,1},{1,0},{2,3},{3,2},{4,5},{5,4},{6,7},{7,6},{8,9},{9,8},{10,11... | collective-permute-start | bytes 393224 | tf_op jit(solution)/shard_map/ppermute | solution.py:309
  82.9 7.6 %collective-permute-start.36 = (bf16[4,128,128]{2,1,0:T(8,128)(2,1)S(1)}, bf16[4,128,128]{2,1,0:T(8,128)(2,1)S(1)}, u32[]{:S(2)}, u32[]{:S(2)}) collective-permute-start(bf16[4,128,128]{2,1,0:T(8,128)(2,1)S(1)} %collective-permute-done.30.rest_0_), channel_id=1, source_target_pairs={{0,6},{1,7},{2,4},{3,5},{4,2},{5,3},{6,0},{7,1},{8,14},{9,15},{10,... | collective-permute-start | bytes 393224 | tf_op jit(solution)/shard_map/ppermute | solution.py:309

commit v3 on v2

v3 whole, which is shorter than its diff:
```python
import functools
import math

import jax
import jax.numpy as jnp
from jax import lax
from jax.experimental import pallas as pl
from jax.experimental.pallas import tpu as pltpu
from jax.sharding import PartitionSpec as P

ORDER = 4
SHIFT = 0.2
THETA = 3.0

UNROLL = 16
START_SHARE = 0
FINISH_SHARE = 6
BITS = 10
MASK = (1 << BITS) - 1
F32 = jnp.float32
BF16 = jnp.bfloat16


def bessel_scaled(order_index):
    total = 0.0
    for term in range(40):
        total += (THETA / 2.0) ** (2 * term + order_index) / (
            math.factorial(term) * math.factorial(term + order_index)
        )
    return math.exp(-THETA) * total


def coefficients():
    values = [bessel_scaled(0)]
    for order_index in range(1, ORDER + 1):
        values.append(2.0 * (-1.0) ** order_index * bessel_scaled(order_index))
    return values


WEIGHTS = coefficients()


def grp_source(g, e, n):
    return g ^ e if power_of_two(n) else (g - e) % n


def grp_target(g, e, n):
    return g ^ e if power_of_two(n) else (g + e) % n


def power_of_two(n):
    return n & (n - 1) == 0


def vmem(x):
    return pltpu.with_memory_space_constraint(x, pltpu.VMEM)


def hbm(x):
    return pltpu.with_memory_space_constraint(x, pltpu.HBM)


VMEM_SPEC = pl.BlockSpec(memory_space=pltpu.VMEM)
SMEM_SPEC = pl.BlockSpec(memory_space=pltpu.SMEM)
ANY_SPEC = pl.BlockSpec(memory_space=pl.ANY)
PARAMS = pltpu.CompilerParams(vmem_limit_bytes=8 * 1024 * 1024)


def hub_source(h, d, n):
    return h ^ d if power_of_two(n) else (h - d) % n


def hub_target(h, d, n):
    return h ^ d if power_of_two(n) else (h + d) % n


def grp_messages(n):
    if power_of_two(n) and n >= 4:
        return [(1, [1])] + [(e, [e, e + 1]) for e in range(2, n, 2)]
    return [(e, [e]) for e in range(1, n)]


def hub_plan(n, hub):
    if not power_of_two(n):
        return list(range(1, n)), []
    bits = [1 << b for b in range(n.bit_length() - 1)]
    second = {b: [] for b in bits}
    for d in range(n - 1, 0, -1):
        held = [b for b in bits if d & b]
        if len(held) > 2:
            second.setdefault(d ^ held[-1], []).append((d, held[-1], range(hub)))
        elif d == 3:
            second[1].append((3, 2, range(hub // 2)))
            second[2].insert(0, (3, 1, range(hub // 2, hub)))
        elif len(held) == 2:
            second[held[0]].append((d, held[1], range(hub)))
    second = [(via, [p for p in pairs if len(p[2])]) for via, pairs in second.items()]
    return bits[::-1], [(via, pairs) for via, pairs in second if pairs]


class Sizes:
    def __init__(self, mesh_shape, embed, hub_ids, send_ids, tile_val):
        self.n_grp, self.n_hub = mesh_shape["grp"], mesh_shape["hub"]
        self.blk, self.emb = tile_val.shape[1], embed.shape[1]
        self.nb = embed.shape[0] // self.blk
        self.slots = tile_val.shape[0]
        self.hub = hub_ids.shape[1]
        self.tail = send_ids.shape[2]
        self.messages = grp_messages(self.n_grp)
        self.hub_first, self.hub_second = hub_plan(self.n_hub, self.hub)
        self.hub_slot, self.tail_slot = {}, {}
        for d in self.hub_first:
            self.hub_slot[d] = len(self.hub_slot) * self.hub
        used = len(self.hub_slot) * self.hub
        for e in range(1, self.n_grp):
            self.tail_slot[e] = used + (e - 1) * self.tail
        self.rem_first = used + (self.n_grp - 1) * self.tail
        used = self.rem_first
        for d in [d for _, pairs in self.hub_second for d, _, _ in pairs]:
            if d not in self.hub_slot:
                self.hub_slot[d] = used
                used += self.hub
        self.rem = used
        self.cap = self.slots + UNROLL
        self.off = [n * self.cap for n in range(4)]
        self.off_len = 4 * self.cap
        self.off_hub = self.off_len + 4
        self.off_send = self.off_hub + self.hub
        self.list_len = self.off_send + (self.n_grp - 1) * self.tail
        self.tile_flops = 2 * self.blk * self.blk * self.emb
        self.field_bytes = 2 * self.nb * self.blk * self.emb
        assert max(self.slots, self.nb + 1, self.nb + self.rem) <= MASK

    def block(self, n, dtype):
        return jax.ShapeDtypeStruct((n, self.blk, self.emb), dtype)

    def block_vmem(self, n, dtype):
        return pltpu.VMEM((n, self.blk, self.emb), dtype)


def read_scalars(pairs, sems):
    copies = [pltpu.make_async_copy(s, d, sems.at[i]) for i, (s, d) in enumerate(pairs)]
    for c in copies:
        c.start()
    for c in copies:
        c.wait()


def gather_kernel(z, hub_in, send_in, field, hub_out, *rest):
    tails, (hub_ids, send_ids, scalar_sem, sem) = rest[:-4], rest[-4:]
    read_scalars([(hub_in, hub_ids), (send_in, send_ids)], scalar_sem)
    g = lax.axis_index("grp")
    copies = []
    for j in range(z.hub):
        copies.append((field.at[hub_ids[0, j]], hub_out.at[j]))
    for (_, shifts), out in zip(z.messages, tails):
        for i, e in enumerate(shifts):
            for k in range(z.tail):
                copies.append((field.at[send_ids[0, grp_target(g, e, z.n_grp), k]], out.at[i * z.tail + k]))
    copies = [pltpu.make_async_copy(s, d, sem.at[i]) for i, (s, d) in enumerate(copies)]
    for c in copies:
        c.start()
    for c in copies:
        c.wait()


def bin_kernel(
    z, tile_count, hub_in, send_in, row_in, col_in, vals_in, field_in, lists, vals, field, *scratch
):
    hub_ids, send_ids, tile_row, tile_col, colmap, sent, scalar_sem, sems = scratch
    copies = [
        pltpu.make_async_copy(vals_in, vals, sems.at[0]),
        pltpu.make_async_copy(field_in, field, sems.at[1]),
    ]
    for c in copies:
        c.start()
    read_scalars(
        [(hub_in, hub_ids), (send_in, send_ids), (row_in, tile_row), (col_in, tile_col)],
        scalar_sem,
    )
    g = lax.axis_index("grp")
    mine = lax.axis_index("hub")
    for j in range(z.hub):
        lists[z.off_hub + j] = hub_ids[0, j]
    for n, e in enumerate(e for _, shifts in z.messages for e in shifts):
        for k in range(z.tail):
            lists[z.off_send + n * z.tail + k] = send_ids[0, grp_target(g, e, z.n_grp), k]

    def local_cols(i, c):
        sent[i] = 0
        colmap[i] = i
        return c

    lax.fori_loop(0, z.nb, local_cols, 0, unroll=8)
    for j in range(z.hub):
        sent[hub_ids[0, j]] = 1
    for d in range(z.n_hub):
        h = hub_source(mine, d, z.n_hub)
        for j in range(z.hub):
            spot = hub_ids[0, j] if d == 0 else z.nb + z.hub_slot[d] + j
            colmap[z.nb + h * z.hub + j] = spot
    base = z.nb + z.n_hub * z.hub
    for e in range(z.n_grp):
        src = grp_source(g, e, z.n_grp)
        dst = grp_target(g, e, z.n_grp)
        for k in range(z.tail):
            if e == 0:
                colmap[base + src * z.tail + k] = send_ids[0, g, k]
            else:
                colmap[base + src * z.tail + k] = z.nb + z.tail_slot[e] + k
                sent[send_ids[0, dst, k]] = 1

    total = tile_count[0]
    group = 8 if z.slots % 8 == 0 else 1

    def place(i, counts):
        counts = list(counts)
        ts = [i * group + u for u in range(group)]
        rows = [tile_row[0, t] for t in ts]
        spots = [colmap[tile_col[0, t]] for t in ts]
        sents = [sent[r] for r in rows]
        entries, places = [], []
        for t, row, spot, out in zip(ts, rows, spots, sents):
            live = (t < total).astype(jnp.int32)
            second = (spot >= z.nb + z.rem_first).astype(jnp.int32)
            remote = (spot >= z.nb).astype(jnp.int32)
            kinds = [1 - remote, remote - second, second * out, second * (1 - out)]
            where = jnp.int32(0)
            for n, kind in enumerate(kinds):
                where = where + kind * (z.off[n] + counts[n])
                counts[n] = counts[n] + kind * live
            places.append(where)
            spot = spot - remote * z.nb - second * z.rem_first
            entries.append(t + (row << BITS) + (spot << (2 * BITS)))
        for entry, where in zip(entries, places):
            lists[where] = entry
        return tuple(counts)

    zero = jnp.int32(0)
    counts = lax.fori_loop(0, (total + group - 1) // group, place, (zero,) * 4)
    for n, (off, length) in enumerate(zip(z.off, counts)):
        for u in range(UNROLL):
            lists[off + length + u] = z.nb << BITS
        lists[z.off_len + n] = length
    for c in copies:
        c.wait()


def accumulate(z, lists, which, vals, source, acc, scale=None, begin=0, end=16):
    off = z.off[which]
    groups = (lists[z.off_len + which] + UNROLL - 1) // UNROLL

    def body(i, c):
        entries = [lists[off + i * UNROLL + u] for u in range(UNROLL)]
        prods = [
            jnp.dot(vals[e & MASK], source[e >> (2 * BITS)], preferred_element_type=F32)
            for e in entries
        ]
        for e, p in zip(entries, prods):
            row = (e >> BITS) & MASK
            acc[row] = acc[row] + (p if scale is None else scale * p)
        return c

    lax.fori_loop(groups * begin // 16, groups * end // 16, body, 0)


def fetch(parts, refs, rem, sems):
    copies = []
    for i, ((slot, n), ref) in enumerate(zip(parts, refs)):
        copies.append(pltpu.make_async_copy(ref.at[pl.ds(0, n)], rem.at[pl.ds(slot, n)], sems.at[i]))
    for c in copies:
        c.start()
    return copies


def start_kernel(z, lists, vals, field, acc):
    def body(r, c):
        acc[r] = -SHIFT * field[r].astype(F32)
        return c

    lax.fori_loop(0, z.nb, body, 0)
    accumulate(z, lists, 0, vals, field, acc, end=START_SHARE)


def edge_kernel(z, parts, step, lists, vals, prev, acc_in, *rest):
    n = len(parts)
    refs, rest = rest[:n], rest[n:]
    acc, rem, hub_out = rest[:3]
    tails = rest[3:-1]
    for c in fetch(parts, refs, rem, rest[-1]):
        c.wait()
    accumulate(z, lists, 2, vals, rem, acc)

    def value(row):
        if step == 1:
            return acc[row].astype(BF16)
        return (2.0 * acc[row] - prev[row].astype(F32)).astype(BF16)

    for j in range(z.hub):
        hub_out[j] = value(lists[z.off_hub + j])
    n = 0
    for (_, shifts), out in zip(z.messages, tails):
        for k in range(len(shifts) * z.tail):
            out[k] = value(lists[z.off_send + n])
            n += 1


def finish_kernel(z, step, lists, vals, rem, *rest):
    fields = rest[:step]
    acc, field = rest[-2:]
    accumulate(z, lists, 3, vals, rem, acc)

    def body(r, c):
        if step == 1:
            t = acc[r].astype(BF16)
        else:
            t = (2.0 * acc[r] - fields[step - 2][r].astype(F32)).astype(BF16)
        field[r] = t
        t = t.astype(F32)
        if step < ORDER - 1:
            acc[r] = -SHIFT * t
        else:
            total = (WEIGHTS[step] - 2.0 * SHIFT * WEIGHTS[ORDER]) * t
            for k in range(step):
                w = WEIGHTS[k] - WEIGHTS[ORDER] * (k == ORDER - 2)
                total = total + w * fields[k][r].astype(F32)
            acc[r] = total
        return c

    lax.fori_loop(0, z.nb, body, 0)
    accumulate(z, lists, 0, vals, field, acc, step_scale(step), end=FINISH_SHARE)


def step_scale(step):
    return 2.0 * WEIGHTS[ORDER] if step == ORDER - 1 else None


def local_kernel(z, parts, step, lists, vals, field, acc_in, *rest):
    n = len(parts)
    refs, (acc, rem, sems) = rest[:n], rest[n:]
    copies = fetch(parts, refs, rem, sems)
    share = START_SHARE if step == 0 else FINISH_SHARE
    accumulate(z, lists, 0, vals, field, acc, step_scale(step), begin=share)
    for c in copies:
        c.wait()
    accumulate(z, lists, 1, vals, rem, acc, step_scale(step))


def last_kernel(z, parts, lists, vals, acc_in, *rest):
    n = len(parts)
    refs, rest = rest[:n], rest[n:]
    acc, out, rem, sems, out_sem = rest
    for c in fetch(parts, refs, rem, sems):
        c.wait()
    accumulate(z, lists, 2, vals, rem, acc, step_scale(ORDER - 1))
    accumulate(z, lists, 3, vals, rem, acc, step_scale(ORDER - 1))
    c = pltpu.make_async_copy(acc.at[pl.ds(0, z.nb)], out, out_sem)
    c.start()
    c.wait()


def over_hub(z, x, d):
    return lax.ppermute(x, "hub", [(i, hub_target(i, d, z.n_hub)) for i in range(z.n_hub)])


def over_grp(z, x, e):
    return lax.ppermute(x, "grp", [(i, grp_target(i, e, z.n_grp)) for i in range(z.n_grp)])


def first_stage(z, hub, tails):
    got = {d: over_hub(z, hub, d) for d in z.hub_first}
    arrays = [got[d] for d in z.hub_first]
    parts = [(z.hub_slot[d], z.hub) for d in z.hub_first]
    for (e, shifts), tail in zip(z.messages, tails):
        mail = over_grp(z, tail, e)
        arrays.append(mail)
        parts.append((z.tail_slot[shifts[0]], z.tail))
        if len(shifts) == 2:
            arrays.append(over_grp(z, mail[z.tail :], 1))
            parts.append((z.tail_slot[shifts[1]], z.tail))
    return got, arrays, tuple(parts)


def second_stage(z, got):
    arrays, parts = [], []
    for via, pairs in z.hub_second:
        held = [got[b][blocks.start : blocks.stop] for _, b, blocks in pairs]
        held = held[0] if len(held) == 1 else jnp.concatenate(held)
        arrays.append(over_hub(z, held, via))
        d, _, blocks = pairs[0]
        parts.append((z.hub_slot[d] + blocks.start - z.rem_first, held.shape[0]))
    return arrays, tuple(parts)


def cost(z, tiles, nbytes):
    return pl.CostEstimate(
        flops=tiles * z.tile_flops,
        bytes_accessed=nbytes + tiles * 2 * z.blk * (z.blk + 5 * z.emb),
        transcendentals=0,
    )


def shards(mesh_shape, embed, hub_ids, send_ids, tile_row, tile_col, tile_val, tile_count):
    z = Sizes(mesh_shape, embed, hub_ids, send_ids, tile_val)
    field0 = embed.reshape(z.nb, z.blk, z.emb)
    sent_shapes = [z.block(z.hub, BF16)] + [z.block(len(shifts) * z.tail, BF16) for _, shifts in z.messages]
    hub_ids, send_ids = hbm(hub_ids), hbm(send_ids)

    hub, *tails = pl.pallas_call(
        functools.partial(gather_kernel, z),
        out_shape=sent_shapes,
        in_specs=[ANY_SPEC] * 3,
        out_specs=[ANY_SPEC] * len(sent_shapes),
        scratch_shapes=[
            pltpu.SMEM(hub_ids.shape, jnp.int32),
            pltpu.SMEM(send_ids.shape, jnp.int32),
            pltpu.SemaphoreType.DMA((2,)),
            pltpu.SemaphoreType.DMA((z.hub + (z.n_grp - 1) * z.tail,)),
        ],
        compiler_params=PARAMS,
        name="gather",
    )(hub_ids, send_ids, hbm(field0))
    got, arrays, parts = first_stage(z, hub, tails)

    lists, vals, field = pl.pallas_call(
        functools.partial(bin_kernel, z),
        out_shape=[
            pltpu.SMEM((z.list_len,), jnp.int32),
            pltpu.VMEM(tile_val.shape, BF16),
            z.block_vmem(z.nb, BF16),
        ],
        in_specs=[SMEM_SPEC] + [ANY_SPEC] * 6,
        out_specs=[SMEM_SPEC, VMEM_SPEC, VMEM_SPEC],
        scratch_shapes=[
            pltpu.SMEM(hub_ids.shape, jnp.int32),
            pltpu.SMEM(send_ids.shape, jnp.int32),
            pltpu.SMEM(tile_row.shape, jnp.int32),
            pltpu.SMEM(tile_col.shape, jnp.int32),
            pltpu.SMEM((z.nb + z.n_hub * z.hub + z.n_grp * z.tail,), jnp.int32),
            pltpu.SMEM((z.nb,), jnp.int32),
            pltpu.SemaphoreType.DMA((4,)),
            pltpu.SemaphoreType.DMA((2,)),
        ],
        compiler_params=PARAMS,
        cost_estimate=cost(z, 0, 2 * (2 * z.slots * z.blk * z.blk + z.field_bytes)),
        name="binning",
    )(tile_count, hub_ids, send_ids, hbm(tile_row), hbm(tile_col), hbm(tile_val), hbm(field0))

    acc_shape = z.block_vmem(z.nb + 1, F32)
    vals, field = vmem(vals), vmem(field)
    lists = pltpu.with_memory_space_constraint(lists, pltpu.SMEM)
    acc = pl.pallas_call(
        functools.partial(start_kernel, z),
        out_shape=acc_shape,
        in_specs=[SMEM_SPEC, VMEM_SPEC, VMEM_SPEC],
        out_specs=VMEM_SPEC,
        compiler_params=PARAMS,
        cost_estimate=cost(z, z.slots // 2, 3 * z.field_bytes),
        name="start",
    )(lists, vals, field)

    fields = [field]
    for step in range(ORDER):
        if step > 0:
            acc, rem, hub, *tails = pl.pallas_call(
                functools.partial(edge_kernel, z, late_parts, step),
                out_shape=[acc_shape, z.block_vmem(z.rem - z.rem_first, BF16)] + sent_shapes,
                in_specs=[SMEM_SPEC] + [VMEM_SPEC] * 3 + [ANY_SPEC] * len(late_parts),
                out_specs=[VMEM_SPEC] * (2 + len(sent_shapes)),
                input_output_aliases={3: 0},
                scratch_shapes=[pltpu.SemaphoreType.DMA((len(late_parts),))],
                compiler_params=PARAMS,
                cost_estimate=cost(z, z.slots // 16, 2 * z.rem * z.blk * z.emb),
                name="edge",
            )(lists, vals, fields[max(step - 2, 0)], vmem(acc), *late)
            got, arrays, parts = first_stage(z, hub, tails)
            acc, new = pl.pallas_call(
                functools.partial(finish_kernel, z, step),
                out_shape=[acc_shape, z.block_vmem(z.nb, BF16)],
                in_specs=[SMEM_SPEC] + [VMEM_SPEC] * (3 + step),
                out_specs=[VMEM_SPEC] * 2,
                input_output_aliases={3 + step: 0},
                compiler_params=PARAMS,
                cost_estimate=cost(z, z.slots // 4, 5 * z.field_bytes),
                name="finish",
            )(lists, vals, vmem(rem), *fields, vmem(acc))
            fields.append(vmem(new))
        got, acc = lax.optimization_barrier((got, acc))
        late, late_parts = second_stage(z, got)
        acc = pl.pallas_call(
            functools.partial(local_kernel, z, parts, step),
            out_shape=acc_shape,
            in_specs=[SMEM_SPEC] + [VMEM_SPEC] * 3 + [ANY_SPEC] * len(parts),
            out_specs=VMEM_SPEC,
            input_output_aliases={3: 0},
            scratch_shapes=[
                pltpu.VMEM((z.rem_first, z.blk, z.emb), BF16),
                pltpu.SemaphoreType.DMA((len(parts),)),
            ],
            compiler_params=PARAMS,
            cost_estimate=cost(z, z.slots // 2, 0),
            name="local",
        )(lists, vals, fields[-1], vmem(acc), *arrays)

    _, out = pl.pallas_call(
        functools.partial(last_kernel, z, late_parts),
        out_shape=[acc_shape, z.block(z.nb, F32)],
        in_specs=[SMEM_SPEC] + [VMEM_SPEC] * 2 + [ANY_SPEC] * len(late_parts),
        out_specs=[VMEM_SPEC, ANY_SPEC],
        input_output_aliases={2: 0},
        scratch_shapes=[
            pltpu.VMEM((z.rem - z.rem_first, z.blk, z.emb), BF16),
            pltpu.SemaphoreType.DMA((len(late_parts),)),
            pltpu.SemaphoreType.DMA(()),
        ],
        compiler_params=PARAMS,
        name="last",
    )(lists, vals, vmem(acc), *late)
    return out.reshape(embed.shape[0], z.emb)


def solution(mesh):
    return jax.shard_map(
        functools.partial(shards, dict(mesh.shape)),
        mesh=mesh,
        in_specs=(
            P(("grp", "hub"), None),
            P(("grp", "hub"), None),
            P(("grp", "hub"), None, None),
            P(("grp", "hub"), None),
            P(("grp", "hub"), None),
            P(("grp", "hub"), None, None),
            P(("grp", "hub")),
        ),
        out_specs=P(("grp", "hub"), None),
        check_vma=False,
    )
```

time: 94.8 us -> 86.7 us (0.915)
  starting transfers between devices: 42.5 us -> 37.8 us
  Pallas kernels: 35 us -> 32.4 us
  waiting for transfers between devices: 17.1 us -> 15.6 us
    ppermute x40 -> x36, starting transfers between devices: 42.5 us -> 37.8 us  [the longest x24 30.1 us: over_hub(): lax.ppermute(x, 'hub', [(i, hub_target(i, d, z.n_hub)) for i in range(z.n...]
    pallas_call x1, Pallas kernels: 3.17 us -> 0.64 us  [shards(): pl.pallas_call(functools.partial(start_kernel, z), out_shape=acc_shape, i...]
    ppermute x40 -> x36, waiting for transfers between devices: 17.1 us -> 15.6 us  [the longest x24 15.5 us: over_hub(): lax.ppermute(x, 'hub', [(i, hub_target(i, d, z.n_hub)) for i in range(z.n...]
    pallas_call x7 -> x8, Pallas kernels: 19.3 us -> 19.2 us  [the longest x4 12.2 us: shards(): pl.pallas_call(functools.partial(local_kernel, z, parts, step), out_shape...]
  transfers between devices with their start and end apart: 40 -> 36, of which waited for: 5 -> 10; matrix products, arithmetic and copies ran while one was open for 0% -> 0% of each run, Pallas kernels for 22% -> 27%
where the time goes in v3:
time: 86.7 us; the launch traced here: 86.9 us
  starting transfers between devices  37.8 us (44%)
  Pallas kernels  32.4 us (37%)
  waiting for transfers between devices  15.6 us (18%)
  between operations  0.93 us (1%)
    ppermute x24, starting transfers between devices, over_hub(): lax.ppermute(x, 'hub', [(i, hub_target(i, d, z.n_hub)) for i in range(z.n...  30.1 us
    ppermute x24, waiting for transfers between devices, over_hub(): lax.ppermute(x, 'hub', [(i, hub_target(i, d, z.n_hub)) for i in range(z.n...  15.5 us
    pallas_call x4, Pallas kernels, shards(): pl.pallas_call(functools.partial(local_kernel, z, parts, step), out_shape...  12.2 us
    ppermute x12, starting transfers between devices, over_grp(): lax.ppermute(x, 'grp', [(i, grp_target(i, e, z.n_grp)) for i in range(z.n...  7.72 us
    pallas_call x3, Pallas kernels, shards(): pl.pallas_call(functools.partial(finish_kernel, z, step), out_shape=[acc_...  7.16 us
    pallas_call x1, Pallas kernels, shards(): pl.pallas_call(functools.partial(last_kernel, z, late_parts), out_shape=[...  3.66 us
    pallas_call x1, Pallas kernels, shards(): pl.pallas_call(functools.partial(bin_kernel, z), out_shape=[pltpu.SMEM((z...  3.5 us
    pallas_call x3, Pallas kernels, shards(): pl.pallas_call(functools.partial(edge_kernel, z, late_parts, step), out_s...  3.41 us
  transfers between devices with their start and end apart: 36, of which 10 were waited for; matrix products, arithmetic and copies ran while one was open for 0% of the time, Pallas kernels for 27%

profile of v3, /device:TPU:0, one launch (start us, length us, event | category | flops | bytes accessed | tf_op | source)
XLA Modules:
  0.0 86.9 jit_solution(7431245440530010499)
XLA Ops:
  0.0 1.9 %gather.1 = (bf16[4,128,128]{2,1,0:T(8,128)(2,1)S(1)}, bf16[4,128,128]{2,1,0:T(8,128)(2,1)S(1)}, bf16[8,128,128]{2,1,0:T(8,128)(2,1)S(1)}) custom-call(s32[1,4]{1,0:T(1,128)} %hub_in.3, s32[1,4,4]{2,1,0:T(4,128)} %send_in.3, bf16[64,128,128]{2,1,0:T(8,128)(2,1)} %bitcast.2), custom_call_target="tpu_custom_call" | custom-call | tf_op jit(solution)/shard_map/gather/pallas_call | solution.py:409
  1.9 4.1 %collective-permute-start.2 = (bf16[4,128,128]{2,1,0:T(8,128)(2,1)S(1)}, bf16[4,128,128]{2,1,0:T(8,128)(2,1)S(1)}, u32[]{:S(2)}, u32[]{:S(2)}) collective-permute-start(bf16[4,128,128]{2,1,0:T(8,128)(2,1)S(1)} %get-tuple-element.52), channel_id=1, source_target_pairs={{0,4},{1,5},{2,6},{3,7},{4,0},{5,1},{6,2},{7,3},{8,12},{9,13},{10,... | collective-permute-start | bytes 393224 | tf_op jit(solution)/shard_map/ppermute | solution.py:363
  6.0 1.6 %collective-permute-start.1 = (bf16[4,128,128]{2,1,0:T(8,128)(2,1)S(1)}, bf16[4,128,128]{2,1,0:T(8,128)(2,1)S(1)}, u32[]{:S(2)}, u32[]{:S(2)}) collective-permute-start(bf16[4,128,128]{2,1,0:T(8,128)(2,1)S(1)} %get-tuple-element.52), channel_id=1, source_target_pairs={{0,2},{1,3},{2,0},{3,1},{4,6},{5,7},{6,4},{7,5},{8,10},{9,11},{10,... | collective-permute-start | bytes 393224 | tf_op jit(solution)/shard_map/ppermute | solution.py:363
  7.5 1.5 %collective-permute-start = (bf16[4,128,128]{2,1,0:T(8,128)(2,1)S(1)}, bf16[4,128,128]{2,1,0:T(8,128)(2,1)S(1)}, u32[]{:S(2)}, u32[]{:S(2)}) collective-permute-start(bf16[4,128,128]{2,1,0:T(8,128)(2,1)S(1)} %get-tuple-element.52), channel_id=1, source_target_pairs={{0,1},{1,0},{2,3},{3,2},{4,5},{5,4},{6,7},{7,6},{8,9},{9,8},{10,11... | collective-permute-start | bytes 393224 | tf_op jit(solution)/shard_map/ppermute | solution.py:363
  9.1 1.5 %collective-permute-start.4 = (bf16[8,128,128]{2,1,0:T(8,128)(2,1)S(1)}, bf16[8,128,128]{2,1,0:T(8,128)(2,1)S(1)}, u32[]{:S(2)}, u32[]{:S(2)}) collective-permute-start(bf16[8,128,128]{2,1,0:T(8,128)(2,1)S(1)} %get-tuple-element.55), channel_id=1, source_target_pairs={{0,16},{8,24},{16,0},{24,8},{1,17},{9,25},{17,1},{25,9},{2,18},{10... | collective-permute-start | bytes 786440 | tf_op jit(solution)/shard_map/ppermute | solution.py:367
  11.2 3.5 %binning.1 = (s32[852]{0:T(1024)S(4)}, bf16[192,128,128]{2,1,0:T(8,128)(2,1)S(1)}, bf16[64,128,128]{2,1,0:T(8,128)(2,1)S(1)}) custom-call(s32[1]{0:T(128)S(6)} %copy.30.tile_count, s32[1,4]{1,0:T(1,128)} %hub_in.3, s32[1,4,4]{2,1,0:T(4,128)} %send_in.3, s32[1,192]{1,0:T(1,128)} %row_in.1, s32[1,192]{1,0:T(1,128)} %col_in.1, bf16[192,128,128]{2,1,0:T(8,128)(2,1)} %vals_in.1, ...), custom_call_target="tpu_custom_call" | custom-call | bytes 16777216 | tf_op jit(solution)/shard_map/binning/pallas_call | solution.py:425
  14.7 0.6 start.1.acc_in
  15.4 0.0 collective-permute-done.2.rest_0_
  15.4 0.0 collective-permute-done.1.rest_1_
  15.5 0.5 collective-permute-start.7
  16.0 1.7 %collective-permute-start.6 = (bf16[6,128,128]{2,1,0:T(8,128)(2,1)S(1)}, bf16[6,128,128]{2,1,0:T(8,128)(2,1)S(1)}, u32[]{:S(2)}, u32[]{:S(2)}) collective-permute-start(bf16[6,128,128]{2,1,0:T(8,128)(2,1)S(1)} %get-tuple-element.100), channel_id=1, source_target_pairs={{0,1},{1,0},{2,3},{3,2},{4,5},{5,4},{6,7},{7,6},{8,9},{9,8},{10,11... | collective-permute-start | bytes 589832 | tf_op jit(solution)/shard_map/ppermute | solution.py:363
  17.6 0.0 collective-permute-start.3
  17.6 0.0 collective-permute-done.4.rest_4_
  17.7 0.6 collective-permute-start.5
  18.2 1.4 %collective-permute-start.8 = (bf16[4,128,128]{2,1,0:T(8,128)(2,1)S(1)}, bf16[4,128,128]{2,1,0:T(8,128)(2,1)S(1)}, u32[]{:S(2)}, u32[]{:S(2)}) collective-permute-start(bf16[4,128,128]{2,1,0:T(8,128)(2,1)S(1)} %collective-permute-done.2.rest_0_), channel_id=1, source_target_pairs={{0,3},{1,2},{2,1},{3,0},{4,7},{5,6},{6,5},{7,4},{8,11},{9,10},{10,... | collective-permute-start | bytes 393224 | tf_op jit(solution)/shard_map/ppermute | solution.py:363
  19.6 0.0 collective-permute-done.3.rest_3_
  19.6 0.0 collective-permute-done.5.rest_5_
  19.6 3.3 %local.4.acc_in = f32[65,128,128]{2,1,0:T(8,128)S(1)} custom-call(s32[852]{0:T(1024)S(4)} %get-tuple-element.49.lists, bf16[192,128,128]{2,1,0:T(8,128)(2,1)S(1)} %get-tuple-element.50.vals, bf16[64,128,128]{2,1,0:T(8,128)(2,1)S(1)} %get-tuple-element.51.field.prev.rest_0_, f32[65,128,128]{2,1,0:T(8,128)S(1)} %start.1.acc_in, ...), custom_call_target="tpu_custom_call", output_to_operand_aliasing={{}: (3, {})} | custom-call | flops 402653184 | bytes 18874368 | tf_op jit(solution)/shard_map/local/pallas_call | solution.py:490
  22.9 2.2 %collective-permute-done.8.rest_2_ = bf16[4,128,128]{2,1,0:T(8,128)(2,1)S(1)} collective-permute-done((bf16[4,128,128]{2,1,0:T(8,128)(2,1)S(1)}, bf16[4,128,128]{2,1,0:T(8,128)(2,1)S(1)}, u32[]{:S(2)}, u32[]{:S(2)}) %collective-permute-start.8) | collective-permute-done | bytes 131104 | tf_op jit(solution)/shard_map/ppermute | solution.py:363
  25.1 0.0 collective-permute-done.6.rest_0_
  25.1 1.1 %edge.3 = (f32[65,128,128]{2,1,0:T(8,128)S(1)}, bf16[16,128,128]{2,1,0:T(8,128)(2,1)S(1)}, bf16[4,128,128]{2,1,0:T(8,128)(2,1)S(1)}, bf16[4,128,128]{2,1,0:T(8,128)(2,1)S(1)}, bf16[8,128,128]{2,1,0:T(8,128)(2,1)S(1)}) custom-call(s32[852]{0:T(1024)S(4)} %get-tuple-element.49.lists, ...), custom_call_target="tpu_custom_call", output_to_operand_aliasing={{0}: (3, {})} | custom-call | flops 50331648 | bytes 3670016 | tf_op jit(solution)/shard_map/edge/pallas_call | solution.py:465
  26.2 0.5 collective-permute-start.11
  26.7 1.6 %collective-permute-start.10 = (bf16[4,128,128]{2,1,0:T(8,128)(2,1)S(1)}, bf16[4,128,128]{2,1,0:T(8,128)(2,1)S(1)}, u32[]{:S(2)}, u32[]{:S(2)}) collective-permute-start(bf16[4,128,128]{2,1,0:T(8,128)(2,1)S(1)} %get-tuple-element.62), channel_id=1, source_target_pairs={{0,2},{1,3},{2,0},{3,1},{4,6},{5,7},{6,4},{7,5},{8,10},{9,11},{10,... | collective-permute-start | bytes 393224 | tf_op jit(solution)/shard_map/ppermute | solution.py:363
  28.3 0.6 collective-permute-start.9
  28.9 1.5 %collective-permute-start.13 = (bf16[8,128,128]{2,1,0:T(8,128)(2,1)S(1)}, bf16[8,128,128]{2,1,0:T(8,128)(2,1)S(1)}, u32[]{:S(2)}, u32[]{:S(2)}) collective-permute-start(bf16[8,128,128]{2,1,0:T(8,128)(2,1)S(1)} %get-tuple-element.66), channel_id=1, source_target_pairs={{0,16},{8,24},{16,0},{24,8},{1,17},{9,25},{17,1},{25,9},{2,18},{10... | collective-permute-start | bytes 786440 | tf_op jit(solution)/shard_map/ppermute | solution.py:367
  30.4 1.8 %finish.3 = (f32[65,128,128]{2,1,0:T(8,128)S(1)}, bf16[64,128,128]{2,1,0:T(8,128)(2,1)S(1)}) custom-call(s32[852]{0:T(1024)S(4)} %get-tuple-element.49.lists, bf16[192,128,128]{2,1,0:T(8,128)(2,1)S(1)} %get-tuple-element.50.vals, bf16[16,128,128]{2,1,0:T(8,128)(2,1)S(1)} %get-tuple-element.59.rem, ...), custom_call_target="tpu_custom_call", output_to_operand_aliasing={{0}: (4, {})} | custom-call | flops 201326592 | bytes 19922944 | tf_op jit(solution)/shard_map/finish/pallas_call | solution.py:477
  32.2 2.9 %collective-permute-done.11.rest_0_ = bf16[4,128,128]{2,1,0:T(8,128)(2,1)S(1)} collective-permute-done((bf16[4,128,128]{2,1,0:T(8,128)(2,1)S(1)}, bf16[4,128,128]{2,1,0:T(8,128)(2,1)S(1)}, u32[]{:S(2)}, u32[]{:S(2)}) %collective-permute-start.11) | collective-permute-done | bytes 131104 | tf_op jit(solution)/shard_map/ppermute | solution.py:363
  35.1 0.0 collective-permute-done.10.rest_1_
  35.1 0.1 collective-permute-start.16
  35.2 0.5 collective-permute-start.15
  35.7 0.6 collective-permute-start.14
  36.3 3.0 %collective-permute-start.17 = (bf16[4,128,128]{2,1,0:T(8,128)(2,1)S(1)}, bf16[4,128,128]{2,1,0:T(8,128)(2,1)S(1)}, u32[]{:S(2)}, u32[]{:S(2)}) collective-permute-start(bf16[4,128,128]{2,1,0:T(8,128)(2,1)S(1)} %collective-permute-done.11.rest_0_), channel_id=1, source_target_pairs={{0,3},{1,2},{2,1},{3,0},{4,7},{5,6},{6,5},{7,4},{8,11},{9,10},{10,... | collective-permute-start | bytes 393224 | tf_op jit(solution)/shard_map/ppermute | solution.py:363
  39.3 3.0 %local.5.acc_in = f32[65,128,128]{2,1,0:T(8,128)S(1)} custom-call(s32[852]{0:T(1024)S(4)} %get-tuple-element.49.lists, bf16[192,128,128]{2,1,0:T(8,128)(2,1)S(1)} %get-tuple-element.50.vals, bf16[64,128,128]{2,1,0:T(8,128)(2,1)S(1)} %get-tuple-element.61.field.rest_1_.prev, ...), custom_call_target="tpu_custom_call", output_to_operand_aliasing={{}: (3, {})} | custom-call | flops 402653184 | bytes 18874368 | tf_op jit(solution)/shard_map/local/pallas_call | solution.py:490
  42.3 2.0 %collective-permute-done.17.rest_2_ = bf16[4,128,128]{2,1,0:T(8,128)(2,1)S(1)} collective-permute-done((bf16[4,128,128]{2,1,0:T(8,128)(2,1)S(1)}, bf16[4,128,128]{2,1,0:T(8,128)(2,1)S(1)}, u32[]{:S(2)}, u32[]{:S(2)}) %collective-permute-start.17) | collective-permute-done | bytes 131104 | tf_op jit(solution)/shard_map/ppermute | solution.py:363
  44.3 0.4 collective-permute-done.15.rest_0_
  44.8 1.1 %edge.4 = (f32[65,128,128]{2,1,0:T(8,128)S(1)}, bf16[16,128,128]{2,1,0:T(8,128)(2,1)S(1)}, bf16[4,128,128]{2,1,0:T(8,128)(2,1)S(1)}, bf16[4,128,128]{2,1,0:T(8,128)(2,1)S(1)}, bf16[8,128,128]{2,1,0:T(8,128)(2,1)S(1)}) custom-call(s32[852]{0:T(1024)S(4)} %get-tuple-element.49.lists, ...), custom_call_target="tpu_custom_call", output_to_operand_aliasing={{0}: (3, {})} | custom-call | flops 50331648 | bytes 3670016 | tf_op jit(solution)/shard_map/edge/pallas_call | solution.py:465
  45.9 0.8 collective-permute-start.20
  46.7 1.1 %collective-permute-start.19 = (bf16[4,128,128]{2,1,0:T(8,128)(2,1)S(1)}, bf16[4,128,128]{2,1,0:T(8,128)(2,1)S(1)}, u32[]{:S(2)}, u32[]{:S(2)}) collective-permute-start(bf16[4,128,128]{2,1,0:T(8,128)(2,1)S(1)} %get-tuple-element.73), channel_id=1, source_target_pairs={{0,2},{1,3},{2,0},{3,1},{4,6},{5,7},{6,4},{7,5},{8,10},{9,11},{10,... | collective-permute-start | bytes 393224 | tf_op jit(solution)/shard_map/ppermute | solution.py:363
  47.8 0.9 %collective-permute-start.18 = (bf16[4,128,128]{2,1,0:T(8,128)(2,1)S(1)}, bf16[4,128,128]{2,1,0:T(8,128)(2,1)S(1)}, u32[]{:S(2)}, u32[]{:S(2)}) collective-permute-start(bf16[4,128,128]{2,1,0:T(8,128)(2,1)S(1)} %get-tuple-element.73), channel_id=1, source_target_pairs={{0,1},{1,0},{2,3},{3,2},{4,5},{5,4},{6,7},{7,6},{8,9},{9,8},{10,11... | collective-permute-start | bytes 393224 | tf_op jit(solution)/shard_map/ppermute | solution.py:363
  48.7 2.0 %collective-permute-start.22 = (bf16[8,128,128]{2,1,0:T(8,128)(2,1)S(1)}, bf16[8,128,128]{2,1,0:T(8,128)(2,1)S(1)}, u32[]{:S(2)}, u32[]{:S(2)}) collective-permute-start(bf16[8,128,128]{2,1,0:T(8,128)(2,1)S(1)} %get-tuple-element.77), channel_id=1, source_target_pairs={{0,16},{8,24},{16,0},{24,8},{1,17},{9,25},{17,1},{25,9},{2,18},{10... | collective-permute-start | bytes 786440 | tf_op jit(solution)/shard_map/ppermute | solution.py:367
  50.7 2.2 %finish.4 = (f32[65,128,128]{2,1,0:T(8,128)S(1)}, bf16[64,128,128]{2,1,0:T(8,128)(2,1)S(1)}) custom-call(s32[852]{0:T(1024)S(4)} %get-tuple-element.49.lists, bf16[192,128,128]{2,1,0:T(8,128)(2,1)S(1)} %get-tuple-element.50.vals, bf16[16,128,128]{2,1,0:T(8,128)(2,1)S(1)} %get-tuple-element.70.rem, ...), custom_call_target="tpu_custom_call", output_to_operand_aliasing={{0}: (5, {})} | custom-call | flops 201326592 | bytes 19922944 | tf_op jit(solution)/shard_map/finish/pallas_call | solution.py:477
  52.8 0.7 collective-permute-done.19.rest_1_
  53.6 0.7 collective-permute-start.25
  54.3 1.9 %collective-permute-start.24 = (bf16[6,128,128]{2,1,0:T(8,128)(2,1)S(1)}, bf16[6,128,128]{2,1,0:T(8,128)(2,1)S(1)}, u32[]{:S(2)}, u32[]{:S(2)}) collective-permute-start(bf16[6,128,128]{2,1,0:T(8,128)(2,1)S(1)} %get-tuple-element.96), channel_id=1, source_target_pairs={{0,1},{1,0},{2,3},{3,2},{4,5},{5,4},{6,7},{7,6},{8,9},{9,8},{10,11... | collective-permute-start | bytes 589832 | tf_op jit(solution)/shard_map/ppermute | solution.py:363
  56.2 0.6 collective-permute-start.23
  56.8 0.9 %collective-permute-start.26 = (bf16[4,128,128]{2,1,0:T(8,128)(2,1)S(1)}, bf16[4,128,128]{2,1,0:T(8,128)(2,1)S(1)}, u32[]{:S(2)}, u32[]{:S(2)}) collective-permute-start(bf16[4,128,128]{2,1,0:T(8,128)(2,1)S(1)} %collective-permute-done.20.rest_0_), channel_id=1, source_target_pairs={{0,3},{1,2},{2,1},{3,0},{4,7},{5,6},{6,5},{7,4},{8,11},{9,10},{10,... | collective-permute-start | bytes 393224 | tf_op jit(solution)/shard_map/ppermute | solution.py:363
  57.7 0.1 collective-permute-done.23.rest_5_
  57.8 2.9 %local.6.acc_in = f32[65,128,128]{2,1,0:T(8,128)S(1)} custom-call(s32[852]{0:T(1024)S(4)} %get-tuple-element.49.lists, bf16[192,128,128]{2,1,0:T(8,128)(2,1)S(1)} %get-tuple-element.50.vals, bf16[64,128,128]{2,1,0:T(8,128)(2,1)S(1)} %get-tuple-element.72.field.rest_2_, f32[65,128,128]{2,1,0:T(8,128)S(1)} %get-tuple-element.75.acc_in, ...), custom_call_target="tpu_custom_call", output_to_operand_aliasing={{}: (3, {})} | custom-call | flops 402653184 | bytes 18874368 | tf_op jit(solution)/shard_map/local/pallas_call | solution.py:490
  60.8 3.5 %collective-permute-done.26.rest_2_ = bf16[4,128,128]{2,1,0:T(8,128)(2,1)S(1)} collective-permute-done((bf16[4,128,128]{2,1,0:T(8,128)(2,1)S(1)}, bf16[4,128,128]{2,1,0:T(8,128)(2,1)S(1)}, u32[]{:S(2)}, u32[]{:S(2)}) %collective-permute-start.26) | collective-permute-done | bytes 131104 | tf_op jit(solution)/shard_map/ppermute | solution.py:363
  64.2 1.2 %edge.5 = (f32[65,128,128]{2,1,0:T(8,128)S(1)}, bf16[16,128,128]{2,1,0:T(8,128)(2,1)S(1)}, bf16[4,128,128]{2,1,0:T(8,128)(2,1)S(1)}, bf16[4,128,128]{2,1,0:T(8,128)(2,1)S(1)}, bf16[8,128,128]{2,1,0:T(8,128)(2,1)S(1)}) custom-call(s32[852]{0:T(1024)S(4)} %get-tuple-element.49.lists, ...), custom_call_target="tpu_custom_call", output_to_operand_aliasing={{0}: (3, {})} | custom-call | flops 50331648 | bytes 3670016 | tf_op jit(solution)/shard_map/edge/pallas_call | solution.py:465
  65.4 1.2 %collective-permute-start.29 = (bf16[4,128,128]{2,1,0:T(8,128)(2,1)S(1)}, bf16[4,128,128]{2,1,0:T(8,128)(2,1)S(1)}, u32[]{:S(2)}, u32[]{:S(2)}) collective-permute-start(bf16[4,128,128]{2,1,0:T(8,128)(2,1)S(1)} %get-tuple-element.84), channel_id=1, source_target_pairs={{0,4},{1,5},{2,6},{3,7},{4,0},{5,1},{6,2},{7,3},{8,12},{9,13},{10,... | collective-permute-start | bytes 393224 | tf_op jit(solution)/shard_map/ppermute | solution.py:363
  66.6 1.3 %collective-permute-start.28 = (bf16[4,128,128]{2,1,0:T(8,128)(2,1)S(1)}, bf16[4,128,128]{2,1,0:T(8,128)(2,1)S(1)}, u32[]{:S(2)}, u32[]{:S(2)}) collective-permute-start(bf16[4,128,128]{2,1,0:T(8,128)(2,1)S(1)} %get-tuple-element.84), channel_id=1, source_target_pairs={{0,2},{1,3},{2,0},{3,1},{4,6},{5,7},{6,4},{7,5},{8,10},{9,11},{10,... | collective-permute-start | bytes 393224 | tf_op jit(solution)/shard_map/ppermute | solution.py:363
  67.9 0.6 collective-permute-start.27
  68.6 0.5 collective-permute-start.31
  69.1 3.2 %finish.5 = (f32[65,128,128]{2,1,0:T(8,128)S(1)}, bf16[64,128,128]{2,1,0:T(8,128)(2,1)S(1)}) custom-call(s32[852]{0:T(1024)S(4)} %get-tuple-element.49.lists, bf16[192,128,128]{2,1,0:T(8,128)(2,1)S(1)} %get-tuple-element.50.vals, bf16[16,128,128]{2,1,0:T(8,128)(2,1)S(1)} %get-tuple-element.81.rem, ...), custom_call_target="tpu_custom_call", output_to_operand_aliasing={{0}: (6, {})} | custom-call | flops 201326592 | bytes 19922944 | tf_op jit(solution)/shard_map/finish/pallas_call | solution.py:477
  72.3 1.6 %collective-permute-done.29.rest_0_ = bf16[4,128,128]{2,1,0:T(8,128)(2,1)S(1)} collective-permute-done((bf16[4,128,128]{2,1,0:T(8,128)(2,1)S(1)}, bf16[4,128,128]{2,1,0:T(8,128)(2,1)S(1)}, u32[]{:S(2)}, u32[]{:S(2)}) %collective-permute-start.29) | collective-permute-done | bytes 131104 | tf_op jit(solution)/shard_map/ppermute | solution.py:363
  73.9 0.1 collective-permute-start.34
  74.0 1.6 %collective-permute-start.33 = (bf16[6,128,128]{2,1,0:T(8,128)(2,1)S(1)}, bf16[6,128,128]{2,1,0:T(8,128)(2,1)S(1)}, u32[]{:S(2)}, u32[]{:S(2)}) collective-permute-start(bf16[6,128,128]{2,1,0:T(8,128)(2,1)S(1)} %get-tuple-element.94), channel_id=1, source_target_pairs={{0,1},{1,0},{2,3},{3,2},{4,5},{5,4},{6,7},{7,6},{8,9},{9,8},{10,11... | collective-permute-start | bytes 589832 | tf_op jit(solution)/shard_map/ppermute | solution.py:363
  75.6 0.6 collective-permute-start.32
  76.2 1.9 %collective-permute-start.35 = (bf16[4,128,128]{2,1,0:T(8,128)(2,1)S(1)}, bf16[4,128,128]{2,1,0:T(8,128)(2,1)S(1)}, u32[]{:S(2)}, u32[]{:S(2)}) collective-permute-start(bf16[4,128,128]{2,1,0:T(8,128)(2,1)S(1)} %collective-permute-done.29.rest_0_), channel_id=1, source_target_pairs={{0,3},{1,2},{2,1},{3,0},{4,7},{5,6},{6,5},{7,4},{8,11},{9,10},{10,... | collective-permute-start | bytes 393224 | tf_op jit(solution)/shard_map/ppermute | solution.py:363
  78.1 2.9 %local.7.acc_in = f32[65,128,128]{2,1,0:T(8,128)S(1)} custom-call(s32[852]{0:T(1024)S(4)} %get-tuple-element.49.lists, bf16[192,128,128]{2,1,0:T(8,128)(2,1)S(1)} %get-tuple-element.50.vals, bf16[64,128,128]{2,1,0:T(8,128)(2,1)S(1)} %get-tuple-element.83.field, f32[65,128,128]{2,1,0:T(8,128)S(1)} %get-tuple-element.86.acc_in, ...), custom_call_target="tpu_custom_call", output_to_operand_aliasing={{}: (3, {})} | custom-call | flops 402653184 | bytes 18874368 | tf_op jit(solution)/shard_map/local/pallas_call | solution.py:490
  81.0 1.7 %collective-permute-done.35.rest_2_ = bf16[4,128,128]{2,1,0:T(8,128)(2,1)S(1)} collective-permute-done((bf16[4,128,128]{2,1,0:T(8,128)(2,1)S(1)}, bf16[4,128,128]{2,1,0:T(8,128)(2,1)S(1)}, u32[]{:S(2)}, u32[]{:S(2)}) %collective-permute-start.35) | collective-permute-done | bytes 131104 | tf_op jit(solution)/shard_map/ppermute | solution.py:363
  82.7 0.5 collective-permute-done.33.rest_0_
  83.2 3.7 %last.1 = (f32[65,128,128]{2,1,0:T(8,128)S(1)}, f32[64,128,128]{2,1,0:T(8,128)}) custom-call(s32[852]{0:T(1024)S(4)} %get-tuple-element.49.lists, bf16[192,128,128]{2,1,0:T(8,128)(2,1)S(1)} %get-tuple-element.50.vals, f32[65,128,128]{2,1,0:T(8,128)S(1)} %local.7.acc_in, ...), custom_call_target="tpu_custom_call", output_to_operand_aliasing={{0}: (2, {})} | custom-call | tf_op jit(solution)/shard_map/last/pallas_call | solution.py:505
  (38 shorter events, 0.3 us)
Async XLA Ops:
  1.9 13.5 %collective-permute-start.2 = (bf16[4,128,128]{2,1,0:T(8,128)(2,1)S(1)}, bf16[4,128,128]{2,1,0:T(8,128)(2,1)S(1)}, u32[]{:S(2)}, u32[]{:S(2)}) collective-permute-start(bf16[4,128,128]{2,1,0:T(8,128)(2,1)S(1)} %get-tuple-element.52), channel_id=1, source_target_pairs={{0,4},{1,5},{2,6},{3,7},{4,0},{5,1},{6,2},{7,3},{8,12},{9,13},{10,... | collective-permute-start | bytes 393224 | tf_op jit(solution)/shard_map/ppermute | solution.py:363
  6.0 9.4 %collective-permute-start.1 = (bf16[4,128,128]{2,1,0:T(8,128)(2,1)S(1)}, bf16[4,128,128]{2,1,0:T(8,128)(2,1)S(1)}, u32[]{:S(2)}, u32[]{:S(2)}) collective-permute-start(bf16[4,128,128]{2,1,0:T(8,128)(2,1)S(1)} %get-tuple-element.52), channel_id=1, source_target_pairs={{0,2},{1,3},{2,0},{3,1},{4,6},{5,7},{6,4},{7,5},{8,10},{9,11},{10,... | collective-permute-start | bytes 393224 | tf_op jit(solution)/shard_map/ppermute | solution.py:363
  7.5 7.9 %collective-permute-start = (bf16[4,128,128]{2,1,0:T(8,128)(2,1)S(1)}, bf16[4,128,128]{2,1,0:T(8,128)(2,1)S(1)}, u32[]{:S(2)}, u32[]{:S(2)}) collective-permute-start(bf16[4,128,128]{2,1,0:T(8,128)(2,1)S(1)} %get-tuple-element.52), channel_id=1, source_target_pairs={{0,1},{1,0},{2,3},{3,2},{4,5},{5,4},{6,7},{7,6},{8,9},{9,8},{10,11... | collective-permute-start | bytes 393224 | tf_op jit(solution)/shard_map/ppermute | solution.py:363
  9.1 8.6 %collective-permute-start.4 = (bf16[8,128,128]{2,1,0:T(8,128)(2,1)S(1)}, bf16[8,128,128]{2,1,0:T(8,128)(2,1)S(1)}, u32[]{:S(2)}, u32[]{:S(2)}) collective-permute-start(bf16[8,128,128]{2,1,0:T(8,128)(2,1)S(1)} %get-tuple-element.55), channel_id=1, source_target_pairs={{0,16},{8,24},{16,0},{24,8},{1,17},{9,25},{17,1},{25,9},{2,18},{10... | collective-permute-start | bytes 786440 | tf_op jit(solution)/shard_map/ppermute | solution.py:367
  15.5 9.6 %collective-permute-start.7 = (bf16[6,128,128]{2,1,0:T(8,128)(2,1)S(1)}, bf16[6,128,128]{2,1,0:T(8,128)(2,1)S(1)}, u32[]{:S(2)}, u32[]{:S(2)}) collective-permute-start(bf16[6,128,128]{2,1,0:T(8,128)(2,1)S(1)} %get-tuple-element.99), channel_id=1, source_target_pairs={{0,2},{1,3},{2,0},{3,1},{4,6},{5,7},{6,4},{7,5},{8,10},{9,11},{10,... | collective-permute-start | bytes 589832 | tf_op jit(solution)/shard_map/ppermute | solution.py:363
  16.0 9.1 %collective-permute-start.6 = (bf16[6,128,128]{2,1,0:T(8,128)(2,1)S(1)}, bf16[6,128,128]{2,1,0:T(8,128)(2,1)S(1)}, u32[]{:S(2)}, u32[]{:S(2)}) collective-permute-start(bf16[6,128,128]{2,1,0:T(8,128)(2,1)S(1)} %get-tuple-element.100), channel_id=1, source_target_pairs={{0,1},{1,0},{2,3},{3,2},{4,5},{5,4},{6,7},{7,6},{8,9},{9,8},{10,11... | collective-permute-start | bytes 589832 | tf_op jit(solution)/shard_map/ppermute | solution.py:363
  17.6 2.0 %collective-permute-start.3 = (bf16[4,128,128]{2,1,0:T(8,128)(2,1)S(1)}, bf16[4,128,128]{2,1,0:T(8,128)(2,1)S(1)}, u32[]{:S(2)}, u32[]{:S(2)}) collective-permute-start(bf16[4,128,128]{2,1,0:T(8,128)(2,1)S(1)} %get-tuple-element.54), channel_id=1, source_target_pairs={{0,8},{8,0},{16,24},{24,16},{1,9},{9,1},{17,25},{25,17},{2,10},{10... | collective-permute-start | bytes 393224 | tf_op jit(solution)/shard_map/ppermute | solution.py:367
  17.7 2.0 %collective-permute-start.5 = (bf16[4,128,128]{2,1,0:T(8,128)(2,1)S(1)}, bf16[4,128,128]{2,1,0:T(8,128)(2,1)S(1)}, u32[]{:S(2)}, u32[]{:S(2)}) collective-permute-start(bf16[4,128,128]{2,1,0:T(8,128)(2,1)S(1)} %slice.48), channel_id=1, source_target_pairs={{0,8},{8,0},{16,24},{24,16},{1,9},{9,1},{17,25},{25,17},{2,10},{10... | collective-permute-start | bytes 393224 | tf_op jit(solution)/shard_map/ppermute | solution.py:367
  18.2 6.9 %collective-permute-start.8 = (bf16[4,128,128]{2,1,0:T(8,128)(2,1)S(1)}, bf16[4,128,128]{2,1,0:T(8,128)(2,1)S(1)}, u32[]{:S(2)}, u32[]{:S(2)}) collective-permute-start(bf16[4,128,128]{2,1,0:T(8,128)(2,1)S(1)} %collective-permute-done.2.rest_0_), channel_id=1, source_target_pairs={{0,3},{1,2},{2,1},{3,0},{4,7},{5,6},{6,5},{7,4},{8,11},{9,10},{10,... | collective-permute-start | bytes 393224 | tf_op jit(solution)/shard_map/ppermute | solution.py:363
  26.2 8.9 %collective-permute-start.11 = (bf16[4,128,128]{2,1,0:T(8,128)(2,1)S(1)}, bf16[4,128,128]{2,1,0:T(8,128)(2,1)S(1)}, u32[]{:S(2)}, u32[]{:S(2)}) collective-permute-start(bf16[4,128,128]{2,1,0:T(8,128)(2,1)S(1)} %get-tuple-element.62), channel_id=1, source_target_pairs={{0,4},{1,5},{2,6},{3,7},{4,0},{5,1},{6,2},{7,3},{8,12},{9,13},{10,... | collective-permute-start | bytes 393224 | tf_op jit(solution)/shard_map/ppermute | solution.py:363
  26.7 8.4 %collective-permute-start.10 = (bf16[4,128,128]{2,1,0:T(8,128)(2,1)S(1)}, bf16[4,128,128]{2,1,0:T(8,128)(2,1)S(1)}, u32[]{:S(2)}, u32[]{:S(2)}) collective-permute-start(bf16[4,128,128]{2,1,0:T(8,128)(2,1)S(1)} %get-tuple-element.62), channel_id=1, source_target_pairs={{0,2},{1,3},{2,0},{3,1},{4,6},{5,7},{6,4},{7,5},{8,10},{9,11},{10,... | collective-permute-start | bytes 393224 | tf_op jit(solution)/shard_map/ppermute | solution.py:363
  28.3 6.8 %collective-permute-start.9 = (bf16[4,128,128]{2,1,0:T(8,128)(2,1)S(1)}, bf16[4,128,128]{2,1,0:T(8,128)(2,1)S(1)}, u32[]{:S(2)}, u32[]{:S(2)}) collective-permute-start(bf16[4,128,128]{2,1,0:T(8,128)(2,1)S(1)} %get-tuple-element.62), channel_id=1, source_target_pairs={{0,1},{1,0},{2,3},{3,2},{4,5},{5,4},{6,7},{7,6},{8,9},{9,8},{10,11... | collective-permute-start | bytes 393224 | tf_op jit(solution)/shard_map/ppermute | solution.py:363
  28.9 6.8 %collective-permute-start.13 = (bf16[8,128,128]{2,1,0:T(8,128)(2,1)S(1)}, bf16[8,128,128]{2,1,0:T(8,128)(2,1)S(1)}, u32[]{:S(2)}, u32[]{:S(2)}) collective-permute-start(bf16[8,128,128]{2,1,0:T(8,128)(2,1)S(1)} %get-tuple-element.66), channel_id=1, source_target_pairs={{0,16},{8,24},{16,0},{24,8},{1,17},{9,25},{17,1},{25,9},{2,18},{10... | collective-permute-start | bytes 786440 | tf_op jit(solution)/shard_map/ppermute | solution.py:367
  35.1 9.2 %collective-permute-start.16 = (bf16[6,128,128]{2,1,0:T(8,128)(2,1)S(1)}, bf16[6,128,128]{2,1,0:T(8,128)(2,1)S(1)}, u32[]{:S(2)}, u32[]{:S(2)}) collective-permute-start(bf16[6,128,128]{2,1,0:T(8,128)(2,1)S(1)} %get-tuple-element.97), channel_id=1, source_target_pairs={{0,2},{1,3},{2,0},{3,1},{4,6},{5,7},{6,4},{7,5},{8,10},{9,11},{10,... | collective-permute-start | bytes 589832 | tf_op jit(solution)/shard_map/ppermute | solution.py:363
  35.2 9.6 %collective-permute-start.15 = (bf16[6,128,128]{2,1,0:T(8,128)(2,1)S(1)}, bf16[6,128,128]{2,1,0:T(8,128)(2,1)S(1)}, u32[]{:S(2)}, u32[]{:S(2)}) collective-permute-start(bf16[6,128,128]{2,1,0:T(8,128)(2,1)S(1)} %get-tuple-element.98), channel_id=1, source_target_pairs={{0,1},{1,0},{2,3},{3,2},{4,5},{5,4},{6,7},{7,6},{8,9},{9,8},{10,11... | collective-permute-start | bytes 589832 | tf_op jit(solution)/shard_map/ppermute | solution.py:363
  35.7 3.6 %collective-permute-start.12 = (bf16[4,128,128]{2,1,0:T(8,128)(2,1)S(1)}, bf16[4,128,128]{2,1,0:T(8,128)(2,1)S(1)}, u32[]{:S(2)}, u32[]{:S(2)}) collective-permute-start(bf16[4,128,128]{2,1,0:T(8,128)(2,1)S(1)} %get-tuple-element.65), channel_id=1, source_target_pairs={{0,8},{8,0},{16,24},{24,16},{1,9},{9,1},{17,25},{25,17},{2,10},{10... | collective-permute-start | bytes 393224 | tf_op jit(solution)/shard_map/ppermute | solution.py:367
  35.7 3.6 %collective-permute-start.14 = (bf16[4,128,128]{2,1,0:T(8,128)(2,1)S(1)}, bf16[4,128,128]{2,1,0:T(8,128)(2,1)S(1)}, u32[]{:S(2)}, u32[]{:S(2)}) collective-permute-start(bf16[4,128,128]{2,1,0:T(8,128)(2,1)S(1)} %slice.49), channel_id=1, source_target_pairs={{0,8},{8,0},{16,24},{24,16},{1,9},{9,1},{17,25},{25,17},{2,10},{10... | collective-permute-start | bytes 393224 | tf_op jit(solution)/shard_map/ppermute | solution.py:367
  36.3 8.0 %collective-permute-start.17 = (bf16[4,128,128]{2,1,0:T(8,128)(2,1)S(1)}, bf16[4,128,128]{2,1,0:T(8,128)(2,1)S(1)}, u32[]{:S(2)}, u32[]{:S(2)}) collective-permute-start(bf16[4,128,128]{2,1,0:T(8,128)(2,1)S(1)} %collective-permute-done.11.rest_0_), channel_id=1, source_target_pairs={{0,3},{1,2},{2,1},{3,0},{4,7},{5,6},{6,5},{7,4},{8,11},{9,10},{10,... | collective-permute-start | bytes 393224 | tf_op jit(solution)/shard_map/ppermute | solution.py:363
  45.9 6.9 %collective-permute-start.20 = (bf16[4,128,128]{2,1,0:T(8,128)(2,1)S(1)}, bf16[4,128,128]{2,1,0:T(8,128)(2,1)S(1)}, u32[]{:S(2)}, u32[]{:S(2)}) collective-permute-start(bf16[4,128,128]{2,1,0:T(8,128)(2,1)S(1)} %get-tuple-element.73), channel_id=1, source_target_pairs={{0,4},{1,5},{2,6},{3,7},{4,0},{5,1},{6,2},{7,3},{8,12},{9,13},{10,... | collective-permute-start | bytes 393224 | tf_op jit(solution)/shard_map/ppermute | solution.py:363
  46.7 6.8 %collective-permute-start.19 = (bf16[4,128,128]{2,1,0:T(8,128)(2,1)S(1)}, bf16[4,128,128]{2,1,0:T(8,128)(2,1)S(1)}, u32[]{:S(2)}, u32[]{:S(2)}) collective-permute-start(bf16[4,128,128]{2,1,0:T(8,128)(2,1)S(1)} %get-tuple-element.73), channel_id=1, source_target_pairs={{0,2},{1,3},{2,0},{3,1},{4,6},{5,7},{6,4},{7,5},{8,10},{9,11},{10,... | collective-permute-start | bytes 393224 | tf_op jit(solution)/shard_map/ppermute | solution.py:363
  47.8 5.7 %collective-permute-start.18 = (bf16[4,128,128]{2,1,0:T(8,128)(2,1)S(1)}, bf16[4,128,128]{2,1,0:T(8,128)(2,1)S(1)}, u32[]{:S(2)}, u32[]{:S(2)}) collective-permute-start(bf16[4,128,128]{2,1,0:T(8,128)(2,1)S(1)} %get-tuple-element.73), channel_id=1, source_target_pairs={{0,1},{1,0},{2,3},{3,2},{4,5},{5,4},{6,7},{7,6},{8,9},{9,8},{10,11... | collective-permute-start | bytes 393224 | tf_op jit(solution)/shard_map/ppermute | solution.py:363
  48.7 7.5 %collective-permute-start.22 = (bf16[8,128,128]{2,1,0:T(8,128)(2,1)S(1)}, bf16[8,128,128]{2,1,0:T(8,128)(2,1)S(1)}, u32[]{:S(2)}, u32[]{:S(2)}) collective-permute-start(bf16[8,128,128]{2,1,0:T(8,128)(2,1)S(1)} %get-tuple-element.77), channel_id=1, source_target_pairs={{0,16},{8,24},{16,0},{24,8},{1,17},{9,25},{17,1},{25,9},{2,18},{10... | collective-permute-start | bytes 786440 | tf_op jit(solution)/shard_map/ppermute | solution.py:367
  53.6 10.6 %collective-permute-start.25 = (bf16[6,128,128]{2,1,0:T(8,128)(2,1)S(1)}, bf16[6,128,128]{2,1,0:T(8,128)(2,1)S(1)}, u32[]{:S(2)}, u32[]{:S(2)}) collective-permute-start(bf16[6,128,128]{2,1,0:T(8,128)(2,1)S(1)} %get-tuple-element.95), channel_id=1, source_target_pairs={{0,2},{1,3},{2,0},{3,1},{4,6},{5,7},{6,4},{7,5},{8,10},{9,11},{10,... | collective-permute-start | bytes 589832 | tf_op jit(solution)/shard_map/ppermute | solution.py:363
  54.3 9.9 %collective-permute-start.24 = (bf16[6,128,128]{2,1,0:T(8,128)(2,1)S(1)}, bf16[6,128,128]{2,1,0:T(8,128)(2,1)S(1)}, u32[]{:S(2)}, u32[]{:S(2)}) collective-permute-start(bf16[6,128,128]{2,1,0:T(8,128)(2,1)S(1)} %get-tuple-element.96), channel_id=1, source_target_pairs={{0,1},{1,0},{2,3},{3,2},{4,5},{5,4},{6,7},{7,6},{8,9},{9,8},{10,11... | collective-permute-start | bytes 589832 | tf_op jit(solution)/shard_map/ppermute | solution.py:363
  56.2 1.5 %collective-permute-start.21 = (bf16[4,128,128]{2,1,0:T(8,128)(2,1)S(1)}, bf16[4,128,128]{2,1,0:T(8,128)(2,1)S(1)}, u32[]{:S(2)}, u32[]{:S(2)}) collective-permute-start(bf16[4,128,128]{2,1,0:T(8,128)(2,1)S(1)} %get-tuple-element.76), channel_id=1, source_target_pairs={{0,8},{8,0},{16,24},{24,16},{1,9},{9,1},{17,25},{25,17},{2,10},{10... | collective-permute-start | bytes 393224 | tf_op jit(solution)/shard_map/ppermute | solution.py:367
  56.2 1.6 %collective-permute-start.23 = (bf16[4,128,128]{2,1,0:T(8,128)(2,1)S(1)}, bf16[4,128,128]{2,1,0:T(8,128)(2,1)S(1)}, u32[]{:S(2)}, u32[]{:S(2)}) collective-permute-start(bf16[4,128,128]{2,1,0:T(8,128)(2,1)S(1)} %slice.50), channel_id=1, source_target_pairs={{0,8},{8,0},{16,24},{24,16},{1,9},{9,1},{17,25},{25,17},{2,10},{10... | collective-permute-start | bytes 393224 | tf_op jit(solution)/shard_map/ppermute | solution.py:367
  56.8 7.4 %collective-permute-start.26 = (bf16[4,128,128]{2,1,0:T(8,128)(2,1)S(1)}, bf16[4,128,128]{2,1,0:T(8,128)(2,1)S(1)}, u32[]{:S(2)}, u32[]{:S(2)}) collective-permute-start(bf16[4,128,128]{2,1,0:T(8,128)(2,1)S(1)} %collective-permute-done.20.rest_0_), channel_id=1, source_target_pairs={{0,3},{1,2},{2,1},{3,0},{4,7},{5,6},{6,5},{7,4},{8,11},{9,10},{10,... | collective-permute-start | bytes 393224 | tf_op jit(solution)/shard_map/ppermute | solution.py:363
  65.4 8.4 %collective-permute-start.29 = (bf16[4,128,128]{2,1,0:T(8,128)(2,1)S(1)}, bf16[4,128,128]{2,1,0:T(8,128)(2,1)S(1)}, u32[]{:S(2)}, u32[]{:S(2)}) collective-permute-start(bf16[4,128,128]{2,1,0:T(8,128)(2,1)S(1)} %get-tuple-element.84), channel_id=1, source_target_pairs={{0,4},{1,5},{2,6},{3,7},{4,0},{5,1},{6,2},{7,3},{8,12},{9,13},{10,... | collective-permute-start | bytes 393224 | tf_op jit(solution)/shard_map/ppermute | solution.py:363
  66.6 7.2 %collective-permute-start.28 = (bf16[4,128,128]{2,1,0:T(8,128)(2,1)S(1)}, bf16[4,128,128]{2,1,0:T(8,128)(2,1)S(1)}, u32[]{:S(2)}, u32[]{:S(2)}) collective-permute-start(bf16[4,128,128]{2,1,0:T(8,128)(2,1)S(1)} %get-tuple-element.84), channel_id=1, source_target_pairs={{0,2},{1,3},{2,0},{3,1},{4,6},{5,7},{6,4},{7,5},{8,10},{9,11},{10,... | collective-permute-start | bytes 393224 | tf_op jit(solution)/shard_map/ppermute | solution.py:363
  67.9 5.9 %collective-permute-start.27 = (bf16[4,128,128]{2,1,0:T(8,128)(2,1)S(1)}, bf16[4,128,128]{2,1,0:T(8,128)(2,1)S(1)}, u32[]{:S(2)}, u32[]{:S(2)}) collective-permute-start(bf16[4,128,128]{2,1,0:T(8,128)(2,1)S(1)} %get-tuple-element.84), channel_id=1, source_target_pairs={{0,1},{1,0},{2,3},{3,2},{4,5},{5,4},{6,7},{7,6},{8,9},{9,8},{10,11... | collective-permute-start | bytes 393224 | tf_op jit(solution)/shard_map/ppermute | solution.py:363
  68.6 7.0 %collective-permute-start.31 = (bf16[8,128,128]{2,1,0:T(8,128)(2,1)S(1)}, bf16[8,128,128]{2,1,0:T(8,128)(2,1)S(1)}, u32[]{:S(2)}, u32[]{:S(2)}) collective-permute-start(bf16[8,128,128]{2,1,0:T(8,128)(2,1)S(1)} %get-tuple-element.88), channel_id=1, source_target_pairs={{0,16},{8,24},{16,0},{24,8},{1,17},{9,25},{17,1},{25,9},{2,18},{10... | collective-permute-start | bytes 786440 | tf_op jit(solution)/shard_map/ppermute | solution.py:367
  73.9 8.8 %collective-permute-start.34 = (bf16[6,128,128]{2,1,0:T(8,128)(2,1)S(1)}, bf16[6,128,128]{2,1,0:T(8,128)(2,1)S(1)}, u32[]{:S(2)}, u32[]{:S(2)}) collective-permute-start(bf16[6,128,128]{2,1,0:T(8,128)(2,1)S(1)} %get-tuple-element.93), channel_id=1, source_target_pairs={{0,2},{1,3},{2,0},{3,1},{4,6},{5,7},{6,4},{7,5},{8,10},{9,11},{10,... | collective-permute-start | bytes 589832 | tf_op jit(solution)/shard_map/ppermute | solution.py:363
  74.0 9.2 %collective-permute-start.33 = (bf16[6,128,128]{2,1,0:T(8,128)(2,1)S(1)}, bf16[6,128,128]{2,1,0:T(8,128)(2,1)S(1)}, u32[]{:S(2)}, u32[]{:S(2)}) collective-permute-start(bf16[6,128,128]{2,1,0:T(8,128)(2,1)S(1)} %get-tuple-element.94), channel_id=1, source_target_pairs={{0,1},{1,0},{2,3},{3,2},{4,5},{5,4},{6,7},{7,6},{8,9},{9,8},{10,11... | collective-permute-start | bytes 589832 | tf_op jit(solution)/shard_map/ppermute | solution.py:363
  75.6 2.5 %collective-permute-start.30 = (bf16[4,128,128]{2,1,0:T(8,128)(2,1)S(1)}, bf16[4,128,128]{2,1,0:T(8,128)(2,1)S(1)}, u32[]{:S(2)}, u32[]{:S(2)}) collective-permute-start(bf16[4,128,128]{2,1,0:T(8,128)(2,1)S(1)} %get-tuple-element.87), channel_id=1, source_target_pairs={{0,8},{8,0},{16,24},{24,16},{1,9},{9,1},{17,25},{25,17},{2,10},{10... | collective-permute-start | bytes 393224 | tf_op jit(solution)/shard_map/ppermute | solution.py:367
  75.6 2.4 %collective-permute-start.32 = (bf16[4,128,128]{2,1,0:T(8,128)(2,1)S(1)}, bf16[4,128,128]{2,1,0:T(8,128)(2,1)S(1)}, u32[]{:S(2)}, u32[]{:S(2)}) collective-permute-start(bf16[4,128,128]{2,1,0:T(8,128)(2,1)S(1)} %slice.51), channel_id=1, source_target_pairs={{0,8},{8,0},{16,24},{24,16},{1,9},{9,1},{17,25},{25,17},{2,10},{10... | collective-permute-start | bytes 393224 | tf_op jit(solution)/shard_map/ppermute | solution.py:367
  76.2 6.5 %collective-permute-start.35 = (bf16[4,128,128]{2,1,0:T(8,128)(2,1)S(1)}, bf16[4,128,128]{2,1,0:T(8,128)(2,1)S(1)}, u32[]{:S(2)}, u32[]{:S(2)}) collective-permute-start(bf16[4,128,128]{2,1,0:T(8,128)(2,1)S(1)} %collective-permute-done.29.rest_0_), channel_id=1, source_target_pairs={{0,3},{1,2},{2,1},{3,0},{4,7},{5,6},{6,5},{7,4},{8,11},{9,10},{10,... | collective-permute-start | bytes 393224 | tf_op jit(solution)/shard_map/ppermute | solution.py:363

commit v4 on v3

--- a/solution.py
+++ b/solution.py
@@ -13,8 +13,7 @@
 THETA = 3.0
 
 UNROLL = 16
-START_SHARE = 0
-FINISH_SHARE = 6
+FINISH_SHARE = (0, 6, 6, 0)
 BITS = 10
 MASK = (1 << BITS) - 1
 F32 = jnp.float32
@@ -122,7 +121,7 @@
                 used += self.hub
         self.rem = used
         self.cap = self.slots + UNROLL
-        self.off = [n * self.cap for n in range(4)]
+        self.off_local, self.off_first, self.middle = 0, self.cap, 3 * self.cap
         self.off_len = 4 * self.cap
         self.off_hub = self.off_len + 4
         self.off_send = self.off_hub + self.hub
@@ -131,6 +130,11 @@
         self.field_bytes = 2 * self.nb * self.blk * self.emb
         assert max(self.slots, self.nb + 1, self.nb + self.rem) <= MASK
 
+    def remote_code(self, slot):
+        if slot < self.rem_first:
+            return (slot << (2 * BITS)) + 1
+        return ((slot - self.rem_first) << (2 * BITS)) + 2
+
     def block(self, n, dtype):
         return jax.ShapeDtypeStruct((n, self.blk, self.emb), dtype)
 
@@ -146,8 +150,10 @@
         c.wait()
 
 
-def gather_kernel(z, hub_in, send_in, field, hub_out, *rest):
-    tails, (hub_ids, send_ids, scalar_sem, sem) = rest[:-4], rest[-4:]
+def gather_kernel(z, hub_in, send_in, field, field_out, hub_out, *rest):
+    tails, (hub_ids, send_ids, scalar_sem, sem, field_sem) = rest[:-5], rest[-5:]
+    whole = pltpu.make_async_copy(field, field_out, field_sem)
+    whole.start()
     read_scalars([(hub_in, hub_ids), (send_in, send_ids)], scalar_sem)
     g = lax.axis_index("grp")
     copies = []
@@ -162,18 +168,15 @@
         c.start()
     for c in copies:
         c.wait()
+    whole.wait()
 
 
 def bin_kernel(
-    z, tile_count, hub_in, send_in, row_in, col_in, vals_in, field_in, lists, vals, field, *scratch
+    z, tile_count, hub_in, send_in, row_in, col_in, vals_in, lists, vals, *scratch
 ):
-    hub_ids, send_ids, tile_row, tile_col, colmap, sent, scalar_sem, sems = scratch
-    copies = [
-        pltpu.make_async_copy(vals_in, vals, sems.at[0]),
-        pltpu.make_async_copy(field_in, field, sems.at[1]),
-    ]
-    for c in copies:
-        c.start()
+    hub_ids, send_ids, tile_row, tile_col, colmap, unsent, ends, scalar_sem, load_sem = scratch
+    load = pltpu.make_async_copy(vals_in, vals, load_sem)
+    load.start()
     read_scalars(
         [(hub_in, hub_ids), (send_in, send_ids), (row_in, tile_row), (col_in, tile_col)],
         scalar_sem,
@@ -187,68 +190,69 @@
             lists[z.off_send + n * z.tail + k] = send_ids[0, grp_target(g, e, z.n_grp), k]
 
     def local_cols(i, c):
-        sent[i] = 0
-        colmap[i] = i
+        unsent[i] = 1
+        colmap[i] = i << (2 * BITS)
         return c
 
     lax.fori_loop(0, z.nb, local_cols, 0, unroll=8)
     for j in range(z.hub):
-        sent[hub_ids[0, j]] = 1
+        unsent[hub_ids[0, j]] = 0
     for d in range(z.n_hub):
         h = hub_source(mine, d, z.n_hub)
         for j in range(z.hub):
-            spot = hub_ids[0, j] if d == 0 else z.nb + z.hub_slot[d] + j
-            colmap[z.nb + h * z.hub + j] = spot
+            code = hub_ids[0, j] << (2 * BITS) if d == 0 else z.remote_code(z.hub_slot[d] + j)
+            colmap[z.nb + h * z.hub + j] = code
     base = z.nb + z.n_hub * z.hub
     for e in range(z.n_grp):
         src = grp_source(g, e, z.n_grp)
         dst = grp_target(g, e, z.n_grp)
         for k in range(z.tail):
             if e == 0:
-                colmap[base + src * z.tail + k] = send_ids[0, g, k]
+                colmap[base + src * z.tail + k] = send_ids[0, g, k] << (2 * BITS)
             else:
-                colmap[base + src * z.tail + k] = z.nb + z.tail_slot[e] + k
-                sent[send_ids[0, dst, k]] = 1
+                colmap[base + src * z.tail + k] = z.remote_code(z.tail_slot[e] + k)
+                unsent[send_ids[0, dst, k]] = 0
 
     total = tile_count[0]
     group = 8 if z.slots % 8 == 0 else 1
 
-    def place(i, counts):
-        counts = list(counts)
+    starts = (z.off_local, z.off_first, z.middle, z.middle - 1)
+    for n, start in enumerate(starts):
+        ends[n] = start
+
+    def place(i, c):
         ts = [i * group + u for u in range(group)]
         rows = [tile_row[0, t] for t in ts]
-        spots = [colmap[tile_col[0, t]] for t in ts]
-        sents = [sent[r] for r in rows]
-        entries, places = [], []
-        for t, row, spot, out in zip(ts, rows, spots, sents):
-            live = (t < total).astype(jnp.int32)
-            second = (spot >= z.nb + z.rem_first).astype(jnp.int32)
-            remote = (spot >= z.nb).astype(jnp.int32)
-            kinds = [1 - remote, remote - second, second * out, second * (1 - out)]
-            where = jnp.int32(0)
-            for n, kind in enumerate(kinds):
-                where = where + kind * (z.off[n] + counts[n])
-                counts[n] = counts[n] + kind * live
-            places.append(where)
-            spot = spot - remote * z.nb - second * z.rem_first
-            entries.append(t + (row << BITS) + (spot << (2 * BITS)))
-        for entry, where in zip(entries, places):
-            lists[where] = entry
-        return tuple(counts)
-
-    zero = jnp.int32(0)
-    counts = lax.fori_loop(0, (total + group - 1) // group, place, (zero,) * 4)
-    for n, (off, length) in enumerate(zip(z.off, counts)):
+        codes = [colmap[tile_col[0, t]] for t in ts]
+        others = [unsent[r] for r in rows]
+        for t, row, code, other in zip(ts, rows, codes, others):
+            stage = code & 3
+            kind = stage + ((stage >> 1) & other)
+            step = (t < total).astype(jnp.int32)
+            end = ends[kind]
+            lists[end] = (code - stage) + (row << BITS) + t
+            ends[kind] = end + jnp.where(kind == 3, -step, step)
+        return c
+
+    lax.fori_loop(0, (total + group - 1) // group, place, 0)
+    for n, start in enumerate(starts):
+        end = ends[n]
         for u in range(UNROLL):
-            lists[off + length + u] = z.nb << BITS
-        lists[z.off_len + n] = length
-    for c in copies:
-        c.wait()
+            lists[end + u if n < 3 else end - u] = z.nb << BITS
+        lists[z.off_len + n] = end - start if n < 3 else start - end
+    load.wait()
 
 
 def accumulate(z, lists, which, vals, source, acc, scale=None, begin=0, end=16):
-    off = z.off[which]
-    groups = (lists[z.off_len + which] + UNROLL - 1) // UNROLL
+    if which == 4:
+        length = lists[z.off_len + 2] + lists[z.off_len + 3]
+    else:
+        length = lists[z.off_len + which]
+    groups = (length + UNROLL - 1) // UNROLL
+    if which < 3:
+        off = (z.off_local, z.off_first, z.middle)[which]
+    else:
+        off = z.middle - (groups * UNROLL if which == 3 else lists[z.off_len + 3])
 
     def body(i, c):
         entries = [lists[off + i * UNROLL + u] for u in range(UNROLL)]
@@ -264,13 +268,10 @@
     lax.fori_loop(groups * begin // 16, groups * end // 16, body, 0)
 
 
-def fetch(parts, refs, rem, sems):
-    copies = []
-    for i, ((slot, n), ref) in enumerate(zip(parts, refs)):
-        copies.append(pltpu.make_async_copy(ref.at[pl.ds(0, n)], rem.at[pl.ds(slot, n)], sems.at[i]))
-    for c in copies:
-        c.start()
-    return copies
+def fetch(parts, refs, rem):
+    for (slot, n), ref in zip(parts, refs):
+        for i in range(n):
+            rem[slot + i] = ref[i]
 
 
 def start_kernel(z, lists, vals, field, acc):
@@ -279,16 +280,14 @@
         return c
 
     lax.fori_loop(0, z.nb, body, 0)
-    accumulate(z, lists, 0, vals, field, acc, end=START_SHARE)
 
 
 def edge_kernel(z, parts, step, lists, vals, prev, acc_in, *rest):
     n = len(parts)
     refs, rest = rest[:n], rest[n:]
     acc, rem, hub_out = rest[:3]
-    tails = rest[3:-1]
-    for c in fetch(parts, refs, rem, rest[-1]):
-        c.wait()
+    tails = rest[3:]
+    fetch(parts, refs, rem)
     accumulate(z, lists, 2, vals, rem, acc)
 
     def value(row):
@@ -328,7 +327,7 @@
         return c
 
     lax.fori_loop(0, z.nb, body, 0)
-    accumulate(z, lists, 0, vals, field, acc, step_scale(step), end=FINISH_SHARE)
+    accumulate(z, lists, 0, vals, field, acc, step_scale(step), end=FINISH_SHARE[step])
 
 
 def step_scale(step):
@@ -337,23 +336,19 @@
 
 def local_kernel(z, parts, step, lists, vals, field, acc_in, *rest):
     n = len(parts)
-    refs, (acc, rem, sems) = rest[:n], rest[n:]
-    copies = fetch(parts, refs, rem, sems)
-    share = START_SHARE if step == 0 else FINISH_SHARE
+    refs, (acc, rem) = rest[:n], rest[n:]
+    share = FINISH_SHARE[step]
     accumulate(z, lists, 0, vals, field, acc, step_scale(step), begin=share)
-    for c in copies:
-        c.wait()
+    fetch(parts, refs, rem)
     accumulate(z, lists, 1, vals, rem, acc, step_scale(step))
 
 
 def last_kernel(z, parts, lists, vals, acc_in, *rest):
     n = len(parts)
     refs, rest = rest[:n], rest[n:]
-    acc, out, rem, sems, out_sem = rest
-    for c in fetch(parts, refs, rem, sems):
-        c.wait()
-    accumulate(z, lists, 2, vals, rem, acc, step_scale(ORDER - 1))
-    accumulate(z, lists, 3, vals, rem, acc, step_scale(ORDER - 1))
+    acc, out, rem, out_sem = rest
+    fetch(parts, refs, rem)
+    accumulate(z, lists, 4, vals, rem, acc, step_scale(ORDER - 1))
     c = pltpu.make_async_copy(acc.at[pl.ds(0, z.nb)], out, out_sem)
     c.start()
     c.wait()
@@ -406,31 +401,31 @@
     sent_shapes = [z.block(z.hub, BF16)] + [z.block(len(shifts) * z.tail, BF16) for _, shifts in z.messages]
     hub_ids, send_ids = hbm(hub_ids), hbm(send_ids)
 
-    hub, *tails = pl.pallas_call(
+    field, hub, *tails = pl.pallas_call(
         functools.partial(gather_kernel, z),
-        out_shape=sent_shapes,
+        out_shape=[z.block_vmem(z.nb, BF16)] + sent_shapes,
         in_specs=[ANY_SPEC] * 3,
-        out_specs=[ANY_SPEC] * len(sent_shapes),
+        out_specs=[VMEM_SPEC] + [ANY_SPEC] * len(sent_shapes),
         scratch_shapes=[
             pltpu.SMEM(hub_ids.shape, jnp.int32),
             pltpu.SMEM(send_ids.shape, jnp.int32),
             pltpu.SemaphoreType.DMA((2,)),
             pltpu.SemaphoreType.DMA((z.hub + (z.n_grp - 1) * z.tail,)),
+            pltpu.SemaphoreType.DMA(()),
         ],
         compiler_params=PARAMS,
         name="gather",
     )(hub_ids, send_ids, hbm(field0))
     got, arrays, parts = first_stage(z, hub, tails)
 
-    lists, vals, field = pl.pallas_call(
+    lists, vals = pl.pallas_call(
         functools.partial(bin_kernel, z),
         out_shape=[
             pltpu.SMEM((z.list_len,), jnp.int32),
             pltpu.VMEM(tile_val.shape, BF16),
-            z.block_vmem(z.nb, BF16),
         ],
-        in_specs=[SMEM_SPEC] + [ANY_SPEC] * 6,
-        out_specs=[SMEM_SPEC, VMEM_SPEC, VMEM_SPEC],
+        in_specs=[SMEM_SPEC] + [ANY_SPEC] * 5,
+        out_specs=[SMEM_SPEC, VMEM_SPEC],
         scratch_shapes=[
             pltpu.SMEM(hub_ids.shape, jnp.int32),
             pltpu.SMEM(send_ids.shape, jnp.int32),
@@ -438,13 +433,14 @@
             pltpu.SMEM(tile_col.shape, jnp.int32),
             pltpu.SMEM((z.nb + z.n_hub * z.hub + z.n_grp * z.tail,), jnp.int32),
             pltpu.SMEM((z.nb,), jnp.int32),
+            pltpu.SMEM((4,), jnp.int32),
             pltpu.SemaphoreType.DMA((4,)),
-            pltpu.SemaphoreType.DMA((2,)),
+            pltpu.SemaphoreType.DMA(()),
         ],
         compiler_params=PARAMS,
         cost_estimate=cost(z, 0, 2 * (2 * z.slots * z.blk * z.blk + z.field_bytes)),
         name="binning",
-    )(tile_count, hub_ids, send_ids, hbm(tile_row), hbm(tile_col), hbm(tile_val), hbm(field0))
+    )(tile_count, hub_ids, send_ids, hbm(tile_row), hbm(tile_col), hbm(tile_val))
 
     acc_shape = z.block_vmem(z.nb + 1, F32)
     vals, field = vmem(vals), vmem(field)
@@ -465,14 +461,13 @@
             acc, rem, hub, *tails = pl.pallas_call(
                 functools.partial(edge_kernel, z, late_parts, step),
                 out_shape=[acc_shape, z.block_vmem(z.rem - z.rem_first, BF16)] + sent_shapes,
-                in_specs=[SMEM_SPEC] + [VMEM_SPEC] * 3 + [ANY_SPEC] * len(late_parts),
+                in_specs=[SMEM_SPEC] + [VMEM_SPEC] * (3 + len(late_parts)),
                 out_specs=[VMEM_SPEC] * (2 + len(sent_shapes)),
                 input_output_aliases={3: 0},
-                scratch_shapes=[pltpu.SemaphoreType.DMA((len(late_parts),))],
                 compiler_params=PARAMS,
                 cost_estimate=cost(z, z.slots // 16, 2 * z.rem * z.blk * z.emb),
                 name="edge",
-            )(lists, vals, fields[max(step - 2, 0)], vmem(acc), *late)
+            )(lists, vals, fields[max(step - 2, 0)], vmem(acc), *map(vmem, late))
             got, arrays, parts = first_stage(z, hub, tails)
             acc, new = pl.pallas_call(
                 functools.partial(finish_kernel, z, step),
@@ -485,37 +480,37 @@
                 name="finish",
             )(lists, vals, vmem(rem), *fields, vmem(acc))
             fields.append(vmem(new))
-        got, acc = lax.optimization_barrier((got, acc))
+        if step == 0:
+            got, vals = lax.optimization_barrier((got, vals))
+            vals = vmem(vals)
+        else:
+            got, acc = lax.optimization_barrier((got, acc))
         late, late_parts = second_stage(z, got)
         acc = pl.pallas_call(
             functools.partial(local_kernel, z, parts, step),
             out_shape=acc_shape,
-            in_specs=[SMEM_SPEC] + [VMEM_SPEC] * 3 + [ANY_SPEC] * len(parts),
+            in_specs=[SMEM_SPEC] + [VMEM_SPEC] * (3 + len(parts)),
             out_specs=VMEM_SPEC,
             input_output_aliases={3: 0},
-            scratch_shapes=[
-                pltpu.VMEM((z.rem_first, z.blk, z.emb), BF16),
-                pltpu.SemaphoreType.DMA((len(parts),)),
-            ],
+            scratch_shapes=[pltpu.VMEM((z.rem_first, z.blk, z.emb), BF16)],
             compiler_params=PARAMS,
             cost_estimate=cost(z, z.slots // 2, 0),
             name="local",
-        )(lists, vals, fields[-1], vmem(acc), *arrays)
+        )(lists, vals, fields[-1], vmem(acc), *map(vmem, arrays))
 
     _, out = pl.pallas_call(
         functools.partial(last_kernel, z, late_parts),
         out_shape=[acc_shape, z.block(z.nb, F32)],
-        in_specs=[SMEM_SPEC] + [VMEM_SPEC] * 2 + [ANY_SPEC] * len(late_parts),
+        in_specs=[SMEM_SPEC] + [VMEM_SPEC] * (2 + len(late_parts)),
         out_specs=[VMEM_SPEC, ANY_SPEC],
         input_output_aliases={2: 0},
         scratch_shapes=[
             pltpu.VMEM((z.rem - z.rem_first, z.blk, z.emb), BF16),
-            pltpu.SemaphoreType.DMA((len(late_parts),)),
             pltpu.SemaphoreType.DMA(()),
         ],
         compiler_params=PARAMS,
         name="last",
-    )(lists, vals, vmem(acc), *late)
+    )(lists, vals, vmem(acc), *map(vmem, late))
     return out.reshape(embed.shape[0], z.emb)
 
 

time: 86.7 us -> 83.1 us (0.958)
  Pallas kernels: 32.4 us -> 26 us
  starting transfers between devices: 37.8 us -> 40.2 us
    ppermute x24, starting transfers between devices: 30.1 us -> 32.8 us  [over_hub(): lax.ppermute(x, 'hub', [(i, hub_target(i, d, z.n_hub)) for i in range(z.n...]
    pallas_call x4, Pallas kernels: 12.2 us -> 9.58 us  [shards(): pl.pallas_call(functools.partial(local_kernel, z, parts, step), out_shape...]
    pallas_call x3, Pallas kernels: 3.41 us -> 1.38 us  [shards(): pl.pallas_call(functools.partial(edge_kernel, z, late_parts, step), out_s...]
    pallas_call x1, Pallas kernels: 3.66 us -> 2.36 us  [shards(): pl.pallas_call(functools.partial(last_kernel, z, late_parts), out_shape=[...]
    ppermute x24, waiting for transfers between devices: 15.5 us -> 14.6 us  [over_hub(): lax.ppermute(x, 'hub', [(i, hub_target(i, d, z.n_hub)) for i in range(z.n...]
  transfers between devices with their start and end apart: 36 -> 36, of which waited for: 10 -> 11; matrix products, arithmetic and copies ran while one was open for 0% -> 0% of each run, Pallas kernels for 27% -> 24%
where the time goes in v4:
time: 83.1 us; the launch traced here: 82.9 us
  starting transfers between devices  40.2 us (48%)
  Pallas kernels  26 us (31%)
  waiting for transfers between devices  15.5 us (19%)
  between operations  0.93 us (1%)
    ppermute x24, starting transfers between devices, over_hub(): lax.ppermute(x, 'hub', [(i, hub_target(i, d, z.n_hub)) for i in range(z.n...  32.8 us
    ppermute x24, waiting for transfers between devices, over_hub(): lax.ppermute(x, 'hub', [(i, hub_target(i, d, z.n_hub)) for i in range(z.n...  14.6 us
    pallas_call x4, Pallas kernels, shards(): pl.pallas_call(functools.partial(local_kernel, z, parts, step), out_shape...  9.58 us
    ppermute x12, starting transfers between devices, over_grp(): lax.ppermute(x, 'grp', [(i, grp_target(i, e, z.n_grp)) for i in range(z.n...  7.47 us
    pallas_call x3, Pallas kernels, shards(): pl.pallas_call(functools.partial(finish_kernel, z, step), out_shape=[acc_...  7.11 us
    pallas_call x1, Pallas kernels, shards(): pl.pallas_call(functools.partial(bin_kernel, z), out_shape=[pltpu.SMEM((z...  2.84 us
    pallas_call x1, Pallas kernels, shards(): pl.pallas_call(functools.partial(last_kernel, z, late_parts), out_shape=[...  2.36 us
    pallas_call x1, Pallas kernels, shards(): pl.pallas_call(functools.partial(gather_kernel, z), out_shape=[z.block_vm...  2.12 us
  transfers between devices with their start and end apart: 36, of which 11 were waited for; matrix products, arithmetic and copies ran while one was open for 0% of the time, Pallas kernels for 24%

profile of v4, /device:TPU:0, one launch (start us, length us, event | category | flops | bytes accessed | tf_op | source)
XLA Modules:
  0.0 82.9 jit_solution(2083398724724218552)
XLA Ops:
  0.0 2.1 %gather.1 = (bf16[64,128,128]{2,1,0:T(8,128)(2,1)S(1)}, bf16[4,128,128]{2,1,0:T(8,128)(2,1)S(1)}, bf16[4,128,128]{2,1,0:T(8,128)(2,1)S(1)}, bf16[8,128,128]{2,1,0:T(8,128)(2,1)S(1)}) custom-call(s32[1,4]{1,0:T(1,128)} %hub_in.3, s32[1,4,4]{2,1,0:T(4,128)} %send_in.3, bf16[64,128,128]{2,1,0:T(8,128)(2,1)} %bitcast.2), custom_call_target="tpu_custom_call" | custom-call | tf_op jit(solution)/shard_map/gather/pallas_call | solution.py:404
  2.1 4.1 %collective-permute-start.2 = (bf16[4,128,128]{2,1,0:T(8,128)(2,1)S(1)}, bf16[4,128,128]{2,1,0:T(8,128)(2,1)S(1)}, u32[]{:S(2)}, u32[]{:S(2)}) collective-permute-start(bf16[4,128,128]{2,1,0:T(8,128)(2,1)S(1)} %get-tuple-element.50), channel_id=1, source_target_pairs={{0,4},{1,5},{2,6},{3,7},{4,0},{5,1},{6,2},{7,3},{8,12},{9,13},{10,... | collective-permute-start | bytes 393224 | tf_op jit(solution)/shard_map/ppermute | solution.py:358
  6.2 1.6 %collective-permute-start.1 = (bf16[4,128,128]{2,1,0:T(8,128)(2,1)S(1)}, bf16[4,128,128]{2,1,0:T(8,128)(2,1)S(1)}, u32[]{:S(2)}, u32[]{:S(2)}) collective-permute-start(bf16[4,128,128]{2,1,0:T(8,128)(2,1)S(1)} %get-tuple-element.50), channel_id=1, source_target_pairs={{0,2},{1,3},{2,0},{3,1},{4,6},{5,7},{6,4},{7,5},{8,10},{9,11},{10,... | collective-permute-start | bytes 393224 | tf_op jit(solution)/shard_map/ppermute | solution.py:358
  7.8 1.5 %collective-permute-start = (bf16[4,128,128]{2,1,0:T(8,128)(2,1)S(1)}, bf16[4,128,128]{2,1,0:T(8,128)(2,1)S(1)}, u32[]{:S(2)}, u32[]{:S(2)}) collective-permute-start(bf16[4,128,128]{2,1,0:T(8,128)(2,1)S(1)} %get-tuple-element.50), channel_id=1, source_target_pairs={{0,1},{1,0},{2,3},{3,2},{4,5},{5,4},{6,7},{7,6},{8,9},{9,8},{10,11... | collective-permute-start | bytes 393224 | tf_op jit(solution)/shard_map/ppermute | solution.py:358
  9.3 1.5 %collective-permute-start.4 = (bf16[8,128,128]{2,1,0:T(8,128)(2,1)S(1)}, bf16[8,128,128]{2,1,0:T(8,128)(2,1)S(1)}, u32[]{:S(2)}, u32[]{:S(2)}) collective-permute-start(bf16[8,128,128]{2,1,0:T(8,128)(2,1)S(1)} %get-tuple-element.55), channel_id=1, source_target_pairs={{0,16},{8,24},{16,0},{24,8},{1,17},{9,25},{17,1},{25,9},{2,18},{10... | collective-permute-start | bytes 786440 | tf_op jit(solution)/shard_map/ppermute | solution.py:362
  11.5 2.8 %binning.1 = (s32[852]{0:T(1024)S(4)}, bf16[192,128,128]{2,1,0:T(8,128)(2,1)S(1)}) custom-call(s32[1]{0:T(128)S(6)} %copy.30.tile_count, s32[1,4]{1,0:T(1,128)} %hub_in.3, s32[1,4,4]{2,1,0:T(4,128)} %send_in.3, s32[1,192]{1,0:T(1,128)} %row_in.1, s32[1,192]{1,0:T(1,128)} %col_in.1, bf16[192,128,128]{2,1,0:T(8,128)(2,1)} %vals_in.1), custom_call_target="tpu_custom_call" | custom-call | bytes 16777216 | tf_op jit(solution)/shard_map/binning/pallas_call | solution.py:421
  14.3 0.0 collective-permute-done.2.rest_0_
  14.3 0.0 collective-permute-done.rest_2_
  14.4 0.5 collective-permute-start.7
  14.9 1.0 %collective-permute-start.6 = (bf16[6,128,128]{2,1,0:T(8,128)(2,1)S(1)}, bf16[6,128,128]{2,1,0:T(8,128)(2,1)S(1)}, u32[]{:S(2)}, u32[]{:S(2)}) collective-permute-start(bf16[6,128,128]{2,1,0:T(8,128)(2,1)S(1)} %get-tuple-element.100), channel_id=1, source_target_pairs={{0,1},{1,0},{2,3},{3,2},{4,5},{5,4},{6,7},{7,6},{8,9},{9,8},{10,11... | collective-permute-start | bytes 589832 | tf_op jit(solution)/shard_map/ppermute | solution.py:358
  15.9 0.0 collective-permute-start.3
  15.9 0.6 collective-permute-done.4.rest_4_
  16.5 0.1 collective-permute-start.5
  16.6 1.9 %collective-permute-start.8 = (bf16[4,128,128]{2,1,0:T(8,128)(2,1)S(1)}, bf16[4,128,128]{2,1,0:T(8,128)(2,1)S(1)}, u32[]{:S(2)}, u32[]{:S(2)}) collective-permute-start(bf16[4,128,128]{2,1,0:T(8,128)(2,1)S(1)} %collective-permute-done.2.rest_0_), channel_id=1, source_target_pairs={{0,3},{1,2},{2,1},{3,0},{4,7},{5,6},{6,5},{7,4},{8,11},{9,10},{10,... | collective-permute-start | bytes 393224 | tf_op jit(solution)/shard_map/ppermute | solution.py:358
  18.6 0.6 start.1.acc_in
  19.2 0.0 collective-permute-done.5.rest_5_
  19.2 2.9 %local.4.acc_in = f32[65,128,128]{2,1,0:T(8,128)S(1)} custom-call(s32[852]{0:T(1024)S(4)} %get-tuple-element.49.lists, bf16[192,128,128]{2,1,0:T(8,128)(2,1)S(1)} %get-tuple-element.52.vals, bf16[64,128,128]{2,1,0:T(8,128)(2,1)S(1)} %get-tuple-element.53.field.prev.rest_0_, f32[65,128,128]{2,1,0:T(8,128)S(1)} %start.1.acc_in, ...), custom_call_target="tpu_custom_call", output_to_operand_aliasing={{}: (3, {})} | custom-call | flops 402653184 | bytes 18874368 | tf_op jit(solution)/shard_map/local/pallas_call | solution.py:489
  22.1 1.3 %collective-permute-done.8.rest_2_ = bf16[4,128,128]{2,1,0:T(8,128)(2,1)S(1)} collective-permute-done((bf16[4,128,128]{2,1,0:T(8,128)(2,1)S(1)}, bf16[4,128,128]{2,1,0:T(8,128)(2,1)S(1)}, u32[]{:S(2)}, u32[]{:S(2)}) %collective-permute-start.8) | collective-permute-done | bytes 131104 | tf_op jit(solution)/shard_map/ppermute | solution.py:358
  23.4 0.4 edge.3
  23.9 2.7 %collective-permute-start.11 = (bf16[4,128,128]{2,1,0:T(8,128)(2,1)S(1)}, bf16[4,128,128]{2,1,0:T(8,128)(2,1)S(1)}, u32[]{:S(2)}, u32[]{:S(2)}) collective-permute-start(bf16[4,128,128]{2,1,0:T(8,128)(2,1)S(1)} %get-tuple-element.62), channel_id=1, source_target_pairs={{0,4},{1,5},{2,6},{3,7},{4,0},{5,1},{6,2},{7,3},{8,12},{9,13},{10,... | collective-permute-start | bytes 393224 | tf_op jit(solution)/shard_map/ppermute | solution.py:358
  26.6 1.2 %collective-permute-start.10 = (bf16[4,128,128]{2,1,0:T(8,128)(2,1)S(1)}, bf16[4,128,128]{2,1,0:T(8,128)(2,1)S(1)}, u32[]{:S(2)}, u32[]{:S(2)}) collective-permute-start(bf16[4,128,128]{2,1,0:T(8,128)(2,1)S(1)} %get-tuple-element.62), channel_id=1, source_target_pairs={{0,2},{1,3},{2,0},{3,1},{4,6},{5,7},{6,4},{7,5},{8,10},{9,11},{10,... | collective-permute-start | bytes 393224 | tf_op jit(solution)/shard_map/ppermute | solution.py:358
  27.9 0.6 collective-permute-start.9
  28.5 1.5 %collective-permute-start.13 = (bf16[8,128,128]{2,1,0:T(8,128)(2,1)S(1)}, bf16[8,128,128]{2,1,0:T(8,128)(2,1)S(1)}, u32[]{:S(2)}, u32[]{:S(2)}) collective-permute-start(bf16[8,128,128]{2,1,0:T(8,128)(2,1)S(1)} %get-tuple-element.66), channel_id=1, source_target_pairs={{0,16},{8,24},{16,0},{24,8},{1,17},{9,25},{17,1},{25,9},{2,18},{10... | collective-permute-start | bytes 786440 | tf_op jit(solution)/shard_map/ppermute | solution.py:362
  30.0 2.1 %finish.3 = (f32[65,128,128]{2,1,0:T(8,128)S(1)}, bf16[64,128,128]{2,1,0:T(8,128)(2,1)S(1)}) custom-call(s32[852]{0:T(1024)S(4)} %get-tuple-element.49.lists, bf16[192,128,128]{2,1,0:T(8,128)(2,1)S(1)} %get-tuple-element.52.vals, bf16[16,128,128]{2,1,0:T(8,128)(2,1)S(1)} %get-tuple-element.59.rem, ...), custom_call_target="tpu_custom_call", output_to_operand_aliasing={{0}: (4, {})} | custom-call | flops 201326592 | bytes 19922944 | tf_op jit(solution)/shard_map/finish/pallas_call | solution.py:472
  32.1 0.7 collective-permute-done.11.rest_0_
  32.8 0.5 collective-permute-done.10.rest_1_
  33.3 0.0 collective-permute-done.9.rest_2_
  33.4 0.7 collective-permute-start.16
  34.1 1.2 %collective-permute-start.15 = (bf16[6,128,128]{2,1,0:T(8,128)(2,1)S(1)}, bf16[6,128,128]{2,1,0:T(8,128)(2,1)S(1)}, u32[]{:S(2)}, u32[]{:S(2)}) collective-permute-start(bf16[6,128,128]{2,1,0:T(8,128)(2,1)S(1)} %get-tuple-element.98), channel_id=1, source_target_pairs={{0,1},{1,0},{2,3},{3,2},{4,5},{5,4},{6,7},{7,6},{8,9},{9,8},{10,11... | collective-permute-start | bytes 589832 | tf_op jit(solution)/shard_map/ppermute | solution.py:358
  35.4 0.0 collective-permute-done.13.rest_4_
  35.4 0.6 collective-permute-start.14
  36.0 1.6 %collective-permute-start.17 = (bf16[4,128,128]{2,1,0:T(8,128)(2,1)S(1)}, bf16[4,128,128]{2,1,0:T(8,128)(2,1)S(1)}, u32[]{:S(2)}, u32[]{:S(2)}) collective-permute-start(bf16[4,128,128]{2,1,0:T(8,128)(2,1)S(1)} %collective-permute-done.11.rest_0_), channel_id=1, source_target_pairs={{0,3},{1,2},{2,1},{3,0},{4,7},{5,6},{6,5},{7,4},{8,11},{9,10},{10,... | collective-permute-start | bytes 393224 | tf_op jit(solution)/shard_map/ppermute | solution.py:358
  37.6 0.0 collective-permute-done.12.rest_3_
  37.6 2.0 %local.5.acc_in = f32[65,128,128]{2,1,0:T(8,128)S(1)} custom-call(s32[852]{0:T(1024)S(4)} %get-tuple-element.49.lists, bf16[192,128,128]{2,1,0:T(8,128)(2,1)S(1)} %get-tuple-element.52.vals, bf16[64,128,128]{2,1,0:T(8,128)(2,1)S(1)} %get-tuple-element.61.field.rest_1_.prev, ...), custom_call_target="tpu_custom_call", output_to_operand_aliasing={{}: (3, {})} | custom-call | flops 402653184 | bytes 18874368 | tf_op jit(solution)/shard_map/local/pallas_call | solution.py:489
  39.5 3.2 %collective-permute-done.17.rest_2_ = bf16[4,128,128]{2,1,0:T(8,128)(2,1)S(1)} collective-permute-done((bf16[4,128,128]{2,1,0:T(8,128)(2,1)S(1)}, bf16[4,128,128]{2,1,0:T(8,128)(2,1)S(1)}, u32[]{:S(2)}, u32[]{:S(2)}) %collective-permute-start.17) | collective-permute-done | bytes 131104 | tf_op jit(solution)/shard_map/ppermute | solution.py:358
  42.7 0.5 edge.4
  43.2 2.6 %collective-permute-start.20 = (bf16[4,128,128]{2,1,0:T(8,128)(2,1)S(1)}, bf16[4,128,128]{2,1,0:T(8,128)(2,1)S(1)}, u32[]{:S(2)}, u32[]{:S(2)}) collective-permute-start(bf16[4,128,128]{2,1,0:T(8,128)(2,1)S(1)} %get-tuple-element.73), channel_id=1, source_target_pairs={{0,4},{1,5},{2,6},{3,7},{4,0},{5,1},{6,2},{7,3},{8,12},{9,13},{10,... | collective-permute-start | bytes 393224 | tf_op jit(solution)/shard_map/ppermute | solution.py:358
  45.8 0.4 collective-permute-start.19
  46.2 1.4 %collective-permute-start.18 = (bf16[4,128,128]{2,1,0:T(8,128)(2,1)S(1)}, bf16[4,128,128]{2,1,0:T(8,128)(2,1)S(1)}, u32[]{:S(2)}, u32[]{:S(2)}) collective-permute-start(bf16[4,128,128]{2,1,0:T(8,128)(2,1)S(1)} %get-tuple-element.73), channel_id=1, source_target_pairs={{0,1},{1,0},{2,3},{3,2},{4,5},{5,4},{6,7},{7,6},{8,9},{9,8},{10,11... | collective-permute-start | bytes 393224 | tf_op jit(solution)/shard_map/ppermute | solution.py:358
  47.6 1.5 %collective-permute-start.22 = (bf16[8,128,128]{2,1,0:T(8,128)(2,1)S(1)}, bf16[8,128,128]{2,1,0:T(8,128)(2,1)S(1)}, u32[]{:S(2)}, u32[]{:S(2)}) collective-permute-start(bf16[8,128,128]{2,1,0:T(8,128)(2,1)S(1)} %get-tuple-element.77), channel_id=1, source_target_pairs={{0,16},{8,24},{16,0},{24,8},{1,17},{9,25},{17,1},{25,9},{2,18},{10... | collective-permute-start | bytes 786440 | tf_op jit(solution)/shard_map/ppermute | solution.py:362
  49.1 2.4 %finish.4 = (f32[65,128,128]{2,1,0:T(8,128)S(1)}, bf16[64,128,128]{2,1,0:T(8,128)(2,1)S(1)}) custom-call(s32[852]{0:T(1024)S(4)} %get-tuple-element.49.lists, bf16[192,128,128]{2,1,0:T(8,128)(2,1)S(1)} %get-tuple-element.52.vals, bf16[16,128,128]{2,1,0:T(8,128)(2,1)S(1)} %get-tuple-element.70.rem, ...), custom_call_target="tpu_custom_call", output_to_operand_aliasing={{0}: (5, {})} | custom-call | flops 201326592 | bytes 19922944 | tf_op jit(solution)/shard_map/finish/pallas_call | solution.py:472
  51.5 0.4 collective-permute-done.20.rest_0_
  51.9 0.3 collective-permute-done.19.rest_1_
  52.3 0.6 collective-permute-start.25
  52.9 0.7 collective-permute-start.24
  53.7 0.3 collective-permute-done.22.rest_4_
  53.9 0.3 collective-permute-start.23
  54.3 2.2 %collective-permute-start.26 = (bf16[4,128,128]{2,1,0:T(8,128)(2,1)S(1)}, bf16[4,128,128]{2,1,0:T(8,128)(2,1)S(1)}, u32[]{:S(2)}, u32[]{:S(2)}) collective-permute-start(bf16[4,128,128]{2,1,0:T(8,128)(2,1)S(1)} %collective-permute-done.20.rest_0_), channel_id=1, source_target_pairs={{0,3},{1,2},{2,1},{3,0},{4,7},{5,6},{6,5},{7,4},{8,11},{9,10},{10,... | collective-permute-start | bytes 393224 | tf_op jit(solution)/shard_map/ppermute | solution.py:358
  56.5 1.9 %local.6.acc_in = f32[65,128,128]{2,1,0:T(8,128)S(1)} custom-call(s32[852]{0:T(1024)S(4)} %get-tuple-element.49.lists, bf16[192,128,128]{2,1,0:T(8,128)(2,1)S(1)} %get-tuple-element.52.vals, bf16[64,128,128]{2,1,0:T(8,128)(2,1)S(1)} %get-tuple-element.72.field.rest_2_, f32[65,128,128]{2,1,0:T(8,128)S(1)} %get-tuple-element.75.acc_in, ...), custom_call_target="tpu_custom_call", output_to_operand_aliasing={{}: (3, {})} | custom-call | flops 402653184 | bytes 18874368 | tf_op jit(solution)/shard_map/local/pallas_call | solution.py:489
  58.4 3.7 %collective-permute-done.26.rest_2_ = bf16[4,128,128]{2,1,0:T(8,128)(2,1)S(1)} collective-permute-done((bf16[4,128,128]{2,1,0:T(8,128)(2,1)S(1)}, bf16[4,128,128]{2,1,0:T(8,128)(2,1)S(1)}, u32[]{:S(2)}, u32[]{:S(2)}) %collective-permute-start.26) | collective-permute-done | bytes 131104 | tf_op jit(solution)/shard_map/ppermute | solution.py:358
  62.1 0.5 edge.5
  62.5 0.7 collective-permute-start.29
  63.2 1.2 %collective-permute-start.28 = (bf16[4,128,128]{2,1,0:T(8,128)(2,1)S(1)}, bf16[4,128,128]{2,1,0:T(8,128)(2,1)S(1)}, u32[]{:S(2)}, u32[]{:S(2)}) collective-permute-start(bf16[4,128,128]{2,1,0:T(8,128)(2,1)S(1)} %get-tuple-element.84), channel_id=1, source_target_pairs={{0,2},{1,3},{2,0},{3,1},{4,6},{5,7},{6,4},{7,5},{8,10},{9,11},{10,... | collective-permute-start | bytes 393224 | tf_op jit(solution)/shard_map/ppermute | solution.py:358
  64.4 0.6 collective-permute-start.27
  65.0 1.4 %collective-permute-start.31 = (bf16[8,128,128]{2,1,0:T(8,128)(2,1)S(1)}, bf16[8,128,128]{2,1,0:T(8,128)(2,1)S(1)}, u32[]{:S(2)}, u32[]{:S(2)}) collective-permute-start(bf16[8,128,128]{2,1,0:T(8,128)(2,1)S(1)} %get-tuple-element.88), channel_id=1, source_target_pairs={{0,16},{8,24},{16,0},{24,8},{1,17},{9,25},{17,1},{25,9},{2,18},{10... | collective-permute-start | bytes 786440 | tf_op jit(solution)/shard_map/ppermute | solution.py:362
  66.5 2.5 %finish.5 = (f32[65,128,128]{2,1,0:T(8,128)S(1)}, bf16[64,128,128]{2,1,0:T(8,128)(2,1)S(1)}) custom-call(s32[852]{0:T(1024)S(4)} %get-tuple-element.49.lists, bf16[192,128,128]{2,1,0:T(8,128)(2,1)S(1)} %get-tuple-element.52.vals, bf16[16,128,128]{2,1,0:T(8,128)(2,1)S(1)} %get-tuple-element.81.rem, ...), custom_call_target="tpu_custom_call", output_to_operand_aliasing={{0}: (6, {})} | custom-call | flops 201326592 | bytes 19922944 | tf_op jit(solution)/shard_map/finish/pallas_call | solution.py:472
  69.0 1.5 %collective-permute-done.29.rest_0_ = bf16[4,128,128]{2,1,0:T(8,128)(2,1)S(1)} collective-permute-done((bf16[4,128,128]{2,1,0:T(8,128)(2,1)S(1)}, bf16[4,128,128]{2,1,0:T(8,128)(2,1)S(1)}, u32[]{:S(2)}, u32[]{:S(2)}) %collective-permute-start.29) | collective-permute-done | bytes 131104 | tf_op jit(solution)/shard_map/ppermute | solution.py:358
  70.6 0.1 collective-permute-start.34
  70.8 1.2 %collective-permute-start.33 = (bf16[6,128,128]{2,1,0:T(8,128)(2,1)S(1)}, bf16[6,128,128]{2,1,0:T(8,128)(2,1)S(1)}, u32[]{:S(2)}, u32[]{:S(2)}) collective-permute-start(bf16[6,128,128]{2,1,0:T(8,128)(2,1)S(1)} %get-tuple-element.94), channel_id=1, source_target_pairs={{0,1},{1,0},{2,3},{3,2},{4,5},{5,4},{6,7},{7,6},{8,9},{9,8},{10,11... | collective-permute-start | bytes 589832 | tf_op jit(solution)/shard_map/ppermute | solution.py:358
  72.0 0.6 collective-permute-start.32
  72.6 2.2 %collective-permute-start.35 = (bf16[4,128,128]{2,1,0:T(8,128)(2,1)S(1)}, bf16[4,128,128]{2,1,0:T(8,128)(2,1)S(1)}, u32[]{:S(2)}, u32[]{:S(2)}) collective-permute-start(bf16[4,128,128]{2,1,0:T(8,128)(2,1)S(1)} %collective-permute-done.29.rest_0_), channel_id=1, source_target_pairs={{0,3},{1,2},{2,1},{3,0},{4,7},{5,6},{6,5},{7,4},{8,11},{9,10},{10,... | collective-permute-start | bytes 393224 | tf_op jit(solution)/shard_map/ppermute | solution.py:358
  74.8 2.8 %local.7.acc_in = f32[65,128,128]{2,1,0:T(8,128)S(1)} custom-call(s32[852]{0:T(1024)S(4)} %get-tuple-element.49.lists, bf16[192,128,128]{2,1,0:T(8,128)(2,1)S(1)} %get-tuple-element.52.vals, bf16[64,128,128]{2,1,0:T(8,128)(2,1)S(1)} %get-tuple-element.83.field, f32[65,128,128]{2,1,0:T(8,128)S(1)} %get-tuple-element.86.acc_in, ...), custom_call_target="tpu_custom_call", output_to_operand_aliasing={{}: (3, {})} | custom-call | flops 402653184 | bytes 18874368 | tf_op jit(solution)/shard_map/local/pallas_call | solution.py:489
  77.6 2.8 %collective-permute-done.35.rest_2_ = bf16[4,128,128]{2,1,0:T(8,128)(2,1)S(1)} collective-permute-done((bf16[4,128,128]{2,1,0:T(8,128)(2,1)S(1)}, bf16[4,128,128]{2,1,0:T(8,128)(2,1)S(1)}, u32[]{:S(2)}, u32[]{:S(2)}) %collective-permute-start.35) | collective-permute-done | bytes 131104 | tf_op jit(solution)/shard_map/ppermute | solution.py:358
  80.5 2.4 %last.1 = (f32[65,128,128]{2,1,0:T(8,128)S(1)}, f32[64,128,128]{2,1,0:T(8,128)}) custom-call(s32[852]{0:T(1024)S(4)} %get-tuple-element.49.lists, bf16[192,128,128]{2,1,0:T(8,128)(2,1)S(1)} %get-tuple-element.52.vals, f32[65,128,128]{2,1,0:T(8,128)S(1)} %local.7.acc_in, ...), custom_call_target="tpu_custom_call", output_to_operand_aliasing={{0}: (2, {})} | custom-call | tf_op jit(solution)/shard_map/last/pallas_call | solution.py:501
  (38 shorter events, 0.3 us)
Async XLA Ops:
  2.1 12.2 %collective-permute-start.2 = (bf16[4,128,128]{2,1,0:T(8,128)(2,1)S(1)}, bf16[4,128,128]{2,1,0:T(8,128)(2,1)S(1)}, u32[]{:S(2)}, u32[]{:S(2)}) collective-permute-start(bf16[4,128,128]{2,1,0:T(8,128)(2,1)S(1)} %get-tuple-element.50), channel_id=1, source_target_pairs={{0,4},{1,5},{2,6},{3,7},{4,0},{5,1},{6,2},{7,3},{8,12},{9,13},{10,... | collective-permute-start | bytes 393224 | tf_op jit(solution)/shard_map/ppermute | solution.py:358
  6.2 8.1 %collective-permute-start.1 = (bf16[4,128,128]{2,1,0:T(8,128)(2,1)S(1)}, bf16[4,128,128]{2,1,0:T(8,128)(2,1)S(1)}, u32[]{:S(2)}, u32[]{:S(2)}) collective-permute-start(bf16[4,128,128]{2,1,0:T(8,128)(2,1)S(1)} %get-tuple-element.50), channel_id=1, source_target_pairs={{0,2},{1,3},{2,0},{3,1},{4,6},{5,7},{6,4},{7,5},{8,10},{9,11},{10,... | collective-permute-start | bytes 393224 | tf_op jit(solution)/shard_map/ppermute | solution.py:358
  7.8 6.5 %collective-permute-start = (bf16[4,128,128]{2,1,0:T(8,128)(2,1)S(1)}, bf16[4,128,128]{2,1,0:T(8,128)(2,1)S(1)}, u32[]{:S(2)}, u32[]{:S(2)}) collective-permute-start(bf16[4,128,128]{2,1,0:T(8,128)(2,1)S(1)} %get-tuple-element.50), channel_id=1, source_target_pairs={{0,1},{1,0},{2,3},{3,2},{4,5},{5,4},{6,7},{7,6},{8,9},{9,8},{10,11... | collective-permute-start | bytes 393224 | tf_op jit(solution)/shard_map/ppermute | solution.py:358
  9.3 7.2 %collective-permute-start.4 = (bf16[8,128,128]{2,1,0:T(8,128)(2,1)S(1)}, bf16[8,128,128]{2,1,0:T(8,128)(2,1)S(1)}, u32[]{:S(2)}, u32[]{:S(2)}) collective-permute-start(bf16[8,128,128]{2,1,0:T(8,128)(2,1)S(1)} %get-tuple-element.55), channel_id=1, source_target_pairs={{0,16},{8,24},{16,0},{24,8},{1,17},{9,25},{17,1},{25,9},{2,18},{10... | collective-permute-start | bytes 786440 | tf_op jit(solution)/shard_map/ppermute | solution.py:362
  14.4 9.0 %collective-permute-start.7 = (bf16[6,128,128]{2,1,0:T(8,128)(2,1)S(1)}, bf16[6,128,128]{2,1,0:T(8,128)(2,1)S(1)}, u32[]{:S(2)}, u32[]{:S(2)}) collective-permute-start(bf16[6,128,128]{2,1,0:T(8,128)(2,1)S(1)} %get-tuple-element.99), channel_id=1, source_target_pairs={{0,2},{1,3},{2,0},{3,1},{4,6},{5,7},{6,4},{7,5},{8,10},{9,11},{10,... | collective-permute-start | bytes 589832 | tf_op jit(solution)/shard_map/ppermute | solution.py:358
  14.9 8.5 %collective-permute-start.6 = (bf16[6,128,128]{2,1,0:T(8,128)(2,1)S(1)}, bf16[6,128,128]{2,1,0:T(8,128)(2,1)S(1)}, u32[]{:S(2)}, u32[]{:S(2)}) collective-permute-start(bf16[6,128,128]{2,1,0:T(8,128)(2,1)S(1)} %get-tuple-element.100), channel_id=1, source_target_pairs={{0,1},{1,0},{2,3},{3,2},{4,5},{5,4},{6,7},{7,6},{8,9},{9,8},{10,11... | collective-permute-start | bytes 589832 | tf_op jit(solution)/shard_map/ppermute | solution.py:358
  15.9 3.3 %collective-permute-start.3 = (bf16[4,128,128]{2,1,0:T(8,128)(2,1)S(1)}, bf16[4,128,128]{2,1,0:T(8,128)(2,1)S(1)}, u32[]{:S(2)}, u32[]{:S(2)}) collective-permute-start(bf16[4,128,128]{2,1,0:T(8,128)(2,1)S(1)} %get-tuple-element.54), channel_id=1, source_target_pairs={{0,8},{8,0},{16,24},{24,16},{1,9},{9,1},{17,25},{25,17},{2,10},{10... | collective-permute-start | bytes 393224 | tf_op jit(solution)/shard_map/ppermute | solution.py:362
  16.5 2.7 %collective-permute-start.5 = (bf16[4,128,128]{2,1,0:T(8,128)(2,1)S(1)}, bf16[4,128,128]{2,1,0:T(8,128)(2,1)S(1)}, u32[]{:S(2)}, u32[]{:S(2)}) collective-permute-start(bf16[4,128,128]{2,1,0:T(8,128)(2,1)S(1)} %slice.48), channel_id=1, source_target_pairs={{0,8},{8,0},{16,24},{24,16},{1,9},{9,1},{17,25},{25,17},{2,10},{10... | collective-permute-start | bytes 393224 | tf_op jit(solution)/shard_map/ppermute | solution.py:362
  16.6 6.8 %collective-permute-start.8 = (bf16[4,128,128]{2,1,0:T(8,128)(2,1)S(1)}, bf16[4,128,128]{2,1,0:T(8,128)(2,1)S(1)}, u32[]{:S(2)}, u32[]{:S(2)}) collective-permute-start(bf16[4,128,128]{2,1,0:T(8,128)(2,1)S(1)} %collective-permute-done.2.rest_0_), channel_id=1, source_target_pairs={{0,3},{1,2},{2,1},{3,0},{4,7},{5,6},{6,5},{7,4},{8,11},{9,10},{10,... | collective-permute-start | bytes 393224 | tf_op jit(solution)/shard_map/ppermute | solution.py:358
  23.9 8.9 %collective-permute-start.11 = (bf16[4,128,128]{2,1,0:T(8,128)(2,1)S(1)}, bf16[4,128,128]{2,1,0:T(8,128)(2,1)S(1)}, u32[]{:S(2)}, u32[]{:S(2)}) collective-permute-start(bf16[4,128,128]{2,1,0:T(8,128)(2,1)S(1)} %get-tuple-element.62), channel_id=1, source_target_pairs={{0,4},{1,5},{2,6},{3,7},{4,0},{5,1},{6,2},{7,3},{8,12},{9,13},{10,... | collective-permute-start | bytes 393224 | tf_op jit(solution)/shard_map/ppermute | solution.py:358
  26.6 6.7 %collective-permute-start.10 = (bf16[4,128,128]{2,1,0:T(8,128)(2,1)S(1)}, bf16[4,128,128]{2,1,0:T(8,128)(2,1)S(1)}, u32[]{:S(2)}, u32[]{:S(2)}) collective-permute-start(bf16[4,128,128]{2,1,0:T(8,128)(2,1)S(1)} %get-tuple-element.62), channel_id=1, source_target_pairs={{0,2},{1,3},{2,0},{3,1},{4,6},{5,7},{6,4},{7,5},{8,10},{9,11},{10,... | collective-permute-start | bytes 393224 | tf_op jit(solution)/shard_map/ppermute | solution.py:358
  27.9 5.5 %collective-permute-start.9 = (bf16[4,128,128]{2,1,0:T(8,128)(2,1)S(1)}, bf16[4,128,128]{2,1,0:T(8,128)(2,1)S(1)}, u32[]{:S(2)}, u32[]{:S(2)}) collective-permute-start(bf16[4,128,128]{2,1,0:T(8,128)(2,1)S(1)} %get-tuple-element.62), channel_id=1, source_target_pairs={{0,1},{1,0},{2,3},{3,2},{4,5},{5,4},{6,7},{7,6},{8,9},{9,8},{10,11... | collective-permute-start | bytes 393224 | tf_op jit(solution)/shard_map/ppermute | solution.py:358
  28.5 6.9 %collective-permute-start.13 = (bf16[8,128,128]{2,1,0:T(8,128)(2,1)S(1)}, bf16[8,128,128]{2,1,0:T(8,128)(2,1)S(1)}, u32[]{:S(2)}, u32[]{:S(2)}) collective-permute-start(bf16[8,128,128]{2,1,0:T(8,128)(2,1)S(1)} %get-tuple-element.66), channel_id=1, source_target_pairs={{0,16},{8,24},{16,0},{24,8},{1,17},{9,25},{17,1},{25,9},{2,18},{10... | collective-permute-start | bytes 786440 | tf_op jit(solution)/shard_map/ppermute | solution.py:362
  33.4 9.3 %collective-permute-start.16 = (bf16[6,128,128]{2,1,0:T(8,128)(2,1)S(1)}, bf16[6,128,128]{2,1,0:T(8,128)(2,1)S(1)}, u32[]{:S(2)}, u32[]{:S(2)}) collective-permute-start(bf16[6,128,128]{2,1,0:T(8,128)(2,1)S(1)} %get-tuple-element.97), channel_id=1, source_target_pairs={{0,2},{1,3},{2,0},{3,1},{4,6},{5,7},{6,4},{7,5},{8,10},{9,11},{10,... | collective-permute-start | bytes 589832 | tf_op jit(solution)/shard_map/ppermute | solution.py:358
  34.1 8.6 %collective-permute-start.15 = (bf16[6,128,128]{2,1,0:T(8,128)(2,1)S(1)}, bf16[6,128,128]{2,1,0:T(8,128)(2,1)S(1)}, u32[]{:S(2)}, u32[]{:S(2)}) collective-permute-start(bf16[6,128,128]{2,1,0:T(8,128)(2,1)S(1)} %get-tuple-element.98), channel_id=1, source_target_pairs={{0,1},{1,0},{2,3},{3,2},{4,5},{5,4},{6,7},{7,6},{8,9},{9,8},{10,11... | collective-permute-start | bytes 589832 | tf_op jit(solution)/shard_map/ppermute | solution.py:358
  35.4 2.2 %collective-permute-start.12 = (bf16[4,128,128]{2,1,0:T(8,128)(2,1)S(1)}, bf16[4,128,128]{2,1,0:T(8,128)(2,1)S(1)}, u32[]{:S(2)}, u32[]{:S(2)}) collective-permute-start(bf16[4,128,128]{2,1,0:T(8,128)(2,1)S(1)} %get-tuple-element.65), channel_id=1, source_target_pairs={{0,8},{8,0},{16,24},{24,16},{1,9},{9,1},{17,25},{25,17},{2,10},{10... | collective-permute-start | bytes 393224 | tf_op jit(solution)/shard_map/ppermute | solution.py:362
  35.4 2.2 %collective-permute-start.14 = (bf16[4,128,128]{2,1,0:T(8,128)(2,1)S(1)}, bf16[4,128,128]{2,1,0:T(8,128)(2,1)S(1)}, u32[]{:S(2)}, u32[]{:S(2)}) collective-permute-start(bf16[4,128,128]{2,1,0:T(8,128)(2,1)S(1)} %slice.49), channel_id=1, source_target_pairs={{0,8},{8,0},{16,24},{24,16},{1,9},{9,1},{17,25},{25,17},{2,10},{10... | collective-permute-start | bytes 393224 | tf_op jit(solution)/shard_map/ppermute | solution.py:362
  36.0 6.8 %collective-permute-start.17 = (bf16[4,128,128]{2,1,0:T(8,128)(2,1)S(1)}, bf16[4,128,128]{2,1,0:T(8,128)(2,1)S(1)}, u32[]{:S(2)}, u32[]{:S(2)}) collective-permute-start(bf16[4,128,128]{2,1,0:T(8,128)(2,1)S(1)} %collective-permute-done.11.rest_0_), channel_id=1, source_target_pairs={{0,3},{1,2},{2,1},{3,0},{4,7},{5,6},{6,5},{7,4},{8,11},{9,10},{10,... | collective-permute-start | bytes 393224 | tf_op jit(solution)/shard_map/ppermute | solution.py:358
  43.2 8.7 %collective-permute-start.20 = (bf16[4,128,128]{2,1,0:T(8,128)(2,1)S(1)}, bf16[4,128,128]{2,1,0:T(8,128)(2,1)S(1)}, u32[]{:S(2)}, u32[]{:S(2)}) collective-permute-start(bf16[4,128,128]{2,1,0:T(8,128)(2,1)S(1)} %get-tuple-element.73), channel_id=1, source_target_pairs={{0,4},{1,5},{2,6},{3,7},{4,0},{5,1},{6,2},{7,3},{8,12},{9,13},{10,... | collective-permute-start | bytes 393224 | tf_op jit(solution)/shard_map/ppermute | solution.py:358
  45.8 6.5 %collective-permute-start.19 = (bf16[4,128,128]{2,1,0:T(8,128)(2,1)S(1)}, bf16[4,128,128]{2,1,0:T(8,128)(2,1)S(1)}, u32[]{:S(2)}, u32[]{:S(2)}) collective-permute-start(bf16[4,128,128]{2,1,0:T(8,128)(2,1)S(1)} %get-tuple-element.73), channel_id=1, source_target_pairs={{0,2},{1,3},{2,0},{3,1},{4,6},{5,7},{6,4},{7,5},{8,10},{9,11},{10,... | collective-permute-start | bytes 393224 | tf_op jit(solution)/shard_map/ppermute | solution.py:358
  46.2 6.1 %collective-permute-start.18 = (bf16[4,128,128]{2,1,0:T(8,128)(2,1)S(1)}, bf16[4,128,128]{2,1,0:T(8,128)(2,1)S(1)}, u32[]{:S(2)}, u32[]{:S(2)}) collective-permute-start(bf16[4,128,128]{2,1,0:T(8,128)(2,1)S(1)} %get-tuple-element.73), channel_id=1, source_target_pairs={{0,1},{1,0},{2,3},{3,2},{4,5},{5,4},{6,7},{7,6},{8,9},{9,8},{10,11... | collective-permute-start | bytes 393224 | tf_op jit(solution)/shard_map/ppermute | solution.py:358
  47.6 6.4 %collective-permute-start.22 = (bf16[8,128,128]{2,1,0:T(8,128)(2,1)S(1)}, bf16[8,128,128]{2,1,0:T(8,128)(2,1)S(1)}, u32[]{:S(2)}, u32[]{:S(2)}) collective-permute-start(bf16[8,128,128]{2,1,0:T(8,128)(2,1)S(1)} %get-tuple-element.77), channel_id=1, source_target_pairs={{0,16},{8,24},{16,0},{24,8},{1,17},{9,25},{17,1},{25,9},{2,18},{10... | collective-permute-start | bytes 786440 | tf_op jit(solution)/shard_map/ppermute | solution.py:362
  52.3 9.7 %collective-permute-start.25 = (bf16[6,128,128]{2,1,0:T(8,128)(2,1)S(1)}, bf16[6,128,128]{2,1,0:T(8,128)(2,1)S(1)}, u32[]{:S(2)}, u32[]{:S(2)}) collective-permute-start(bf16[6,128,128]{2,1,0:T(8,128)(2,1)S(1)} %get-tuple-element.95), channel_id=1, source_target_pairs={{0,2},{1,3},{2,0},{3,1},{4,6},{5,7},{6,4},{7,5},{8,10},{9,11},{10,... | collective-permute-start | bytes 589832 | tf_op jit(solution)/shard_map/ppermute | solution.py:358
  52.9 9.1 %collective-permute-start.24 = (bf16[6,128,128]{2,1,0:T(8,128)(2,1)S(1)}, bf16[6,128,128]{2,1,0:T(8,128)(2,1)S(1)}, u32[]{:S(2)}, u32[]{:S(2)}) collective-permute-start(bf16[6,128,128]{2,1,0:T(8,128)(2,1)S(1)} %get-tuple-element.96), channel_id=1, source_target_pairs={{0,1},{1,0},{2,3},{3,2},{4,5},{5,4},{6,7},{7,6},{8,9},{9,8},{10,11... | collective-permute-start | bytes 589832 | tf_op jit(solution)/shard_map/ppermute | solution.py:358
  53.7 2.8 %collective-permute-start.21 = (bf16[4,128,128]{2,1,0:T(8,128)(2,1)S(1)}, bf16[4,128,128]{2,1,0:T(8,128)(2,1)S(1)}, u32[]{:S(2)}, u32[]{:S(2)}) collective-permute-start(bf16[4,128,128]{2,1,0:T(8,128)(2,1)S(1)} %get-tuple-element.76), channel_id=1, source_target_pairs={{0,8},{8,0},{16,24},{24,16},{1,9},{9,1},{17,25},{25,17},{2,10},{10... | collective-permute-start | bytes 393224 | tf_op jit(solution)/shard_map/ppermute | solution.py:362
  53.9 2.5 %collective-permute-start.23 = (bf16[4,128,128]{2,1,0:T(8,128)(2,1)S(1)}, bf16[4,128,128]{2,1,0:T(8,128)(2,1)S(1)}, u32[]{:S(2)}, u32[]{:S(2)}) collective-permute-start(bf16[4,128,128]{2,1,0:T(8,128)(2,1)S(1)} %slice.50), channel_id=1, source_target_pairs={{0,8},{8,0},{16,24},{24,16},{1,9},{9,1},{17,25},{25,17},{2,10},{10... | collective-permute-start | bytes 393224 | tf_op jit(solution)/shard_map/ppermute | solution.py:362
  54.3 7.8 %collective-permute-start.26 = (bf16[4,128,128]{2,1,0:T(8,128)(2,1)S(1)}, bf16[4,128,128]{2,1,0:T(8,128)(2,1)S(1)}, u32[]{:S(2)}, u32[]{:S(2)}) collective-permute-start(bf16[4,128,128]{2,1,0:T(8,128)(2,1)S(1)} %collective-permute-done.20.rest_0_), channel_id=1, source_target_pairs={{0,3},{1,2},{2,1},{3,0},{4,7},{5,6},{6,5},{7,4},{8,11},{9,10},{10,... | collective-permute-start | bytes 393224 | tf_op jit(solution)/shard_map/ppermute | solution.py:358
  62.5 8.0 %collective-permute-start.29 = (bf16[4,128,128]{2,1,0:T(8,128)(2,1)S(1)}, bf16[4,128,128]{2,1,0:T(8,128)(2,1)S(1)}, u32[]{:S(2)}, u32[]{:S(2)}) collective-permute-start(bf16[4,128,128]{2,1,0:T(8,128)(2,1)S(1)} %get-tuple-element.84), channel_id=1, source_target_pairs={{0,4},{1,5},{2,6},{3,7},{4,0},{5,1},{6,2},{7,3},{8,12},{9,13},{10,... | collective-permute-start | bytes 393224 | tf_op jit(solution)/shard_map/ppermute | solution.py:358
  63.2 7.4 %collective-permute-start.28 = (bf16[4,128,128]{2,1,0:T(8,128)(2,1)S(1)}, bf16[4,128,128]{2,1,0:T(8,128)(2,1)S(1)}, u32[]{:S(2)}, u32[]{:S(2)}) collective-permute-start(bf16[4,128,128]{2,1,0:T(8,128)(2,1)S(1)} %get-tuple-element.84), channel_id=1, source_target_pairs={{0,2},{1,3},{2,0},{3,1},{4,6},{5,7},{6,4},{7,5},{8,10},{9,11},{10,... | collective-permute-start | bytes 393224 | tf_op jit(solution)/shard_map/ppermute | solution.py:358
  64.4 6.2 %collective-permute-start.27 = (bf16[4,128,128]{2,1,0:T(8,128)(2,1)S(1)}, bf16[4,128,128]{2,1,0:T(8,128)(2,1)S(1)}, u32[]{:S(2)}, u32[]{:S(2)}) collective-permute-start(bf16[4,128,128]{2,1,0:T(8,128)(2,1)S(1)} %get-tuple-element.84), channel_id=1, source_target_pairs={{0,1},{1,0},{2,3},{3,2},{4,5},{5,4},{6,7},{7,6},{8,9},{9,8},{10,11... | collective-permute-start | bytes 393224 | tf_op jit(solution)/shard_map/ppermute | solution.py:358
  65.0 6.9 %collective-permute-start.31 = (bf16[8,128,128]{2,1,0:T(8,128)(2,1)S(1)}, bf16[8,128,128]{2,1,0:T(8,128)(2,1)S(1)}, u32[]{:S(2)}, u32[]{:S(2)}) collective-permute-start(bf16[8,128,128]{2,1,0:T(8,128)(2,1)S(1)} %get-tuple-element.88), channel_id=1, source_target_pairs={{0,16},{8,24},{16,0},{24,8},{1,17},{9,25},{17,1},{25,9},{2,18},{10... | collective-permute-start | bytes 786440 | tf_op jit(solution)/shard_map/ppermute | solution.py:362
  70.6 9.9 %collective-permute-start.34 = (bf16[6,128,128]{2,1,0:T(8,128)(2,1)S(1)}, bf16[6,128,128]{2,1,0:T(8,128)(2,1)S(1)}, u32[]{:S(2)}, u32[]{:S(2)}) collective-permute-start(bf16[6,128,128]{2,1,0:T(8,128)(2,1)S(1)} %get-tuple-element.93), channel_id=1, source_target_pairs={{0,2},{1,3},{2,0},{3,1},{4,6},{5,7},{6,4},{7,5},{8,10},{9,11},{10,... | collective-permute-start | bytes 589832 | tf_op jit(solution)/shard_map/ppermute | solution.py:358
  70.8 9.7 %collective-permute-start.33 = (bf16[6,128,128]{2,1,0:T(8,128)(2,1)S(1)}, bf16[6,128,128]{2,1,0:T(8,128)(2,1)S(1)}, u32[]{:S(2)}, u32[]{:S(2)}) collective-permute-start(bf16[6,128,128]{2,1,0:T(8,128)(2,1)S(1)} %get-tuple-element.94), channel_id=1, source_target_pairs={{0,1},{1,0},{2,3},{3,2},{4,5},{5,4},{6,7},{7,6},{8,9},{9,8},{10,11... | collective-permute-start | bytes 589832 | tf_op jit(solution)/shard_map/ppermute | solution.py:358
  72.0 2.8 %collective-permute-start.30 = (bf16[4,128,128]{2,1,0:T(8,128)(2,1)S(1)}, bf16[4,128,128]{2,1,0:T(8,128)(2,1)S(1)}, u32[]{:S(2)}, u32[]{:S(2)}) collective-permute-start(bf16[4,128,128]{2,1,0:T(8,128)(2,1)S(1)} %get-tuple-element.87), channel_id=1, source_target_pairs={{0,8},{8,0},{16,24},{24,16},{1,9},{9,1},{17,25},{25,17},{2,10},{10... | collective-permute-start | bytes 393224 | tf_op jit(solution)/shard_map/ppermute | solution.py:362
  72.0 2.8 %collective-permute-start.32 = (bf16[4,128,128]{2,1,0:T(8,128)(2,1)S(1)}, bf16[4,128,128]{2,1,0:T(8,128)(2,1)S(1)}, u32[]{:S(2)}, u32[]{:S(2)}) collective-permute-start(bf16[4,128,128]{2,1,0:T(8,128)(2,1)S(1)} %slice.51), channel_id=1, source_target_pairs={{0,8},{8,0},{16,24},{24,16},{1,9},{9,1},{17,25},{25,17},{2,10},{10... | collective-permute-start | bytes 393224 | tf_op jit(solution)/shard_map/ppermute | solution.py:362
  72.6 7.9 %collective-permute-start.35 = (bf16[4,128,128]{2,1,0:T(8,128)(2,1)S(1)}, bf16[4,128,128]{2,1,0:T(8,128)(2,1)S(1)}, u32[]{:S(2)}, u32[]{:S(2)}) collective-permute-start(bf16[4,128,128]{2,1,0:T(8,128)(2,1)S(1)} %collective-permute-done.29.rest_0_), channel_id=1, source_target_pairs={{0,3},{1,2},{2,1},{3,0},{4,7},{5,6},{6,5},{7,4},{8,11},{9,10},{10,... | collective-permute-start | bytes 393224 | tf_op jit(solution)/shard_map/ppermute | solution.py:358

commit v5 on v4

--- a/solution.py
+++ b/solution.py
@@ -150,10 +150,8 @@
         c.wait()
 
 
-def gather_kernel(z, hub_in, send_in, field, field_out, hub_out, *rest):
-    tails, (hub_ids, send_ids, scalar_sem, sem, field_sem) = rest[:-5], rest[-5:]
-    whole = pltpu.make_async_copy(field, field_out, field_sem)
-    whole.start()
+def gather_kernel(z, hub_in, send_in, field, hub_out, *rest):
+    tails, (hub_ids, send_ids, scalar_sem, sem) = rest[:-4], rest[-4:]
     read_scalars([(hub_in, hub_ids), (send_in, send_ids)], scalar_sem)
     g = lax.axis_index("grp")
     copies = []
@@ -168,15 +166,18 @@
         c.start()
     for c in copies:
         c.wait()
-    whole.wait()
 
 
 def bin_kernel(
-    z, tile_count, hub_in, send_in, row_in, col_in, vals_in, lists, vals, *scratch
+    z, tile_count, hub_in, send_in, row_in, col_in, vals_in, field_in, lists, vals, field, *scratch
 ):
     hub_ids, send_ids, tile_row, tile_col, colmap, unsent, ends, scalar_sem, load_sem = scratch
-    load = pltpu.make_async_copy(vals_in, vals, load_sem)
-    load.start()
+    loads = [
+        pltpu.make_async_copy(vals_in, vals, load_sem.at[0]),
+        pltpu.make_async_copy(field_in, field, load_sem.at[1]),
+    ]
+    for c in loads:
+        c.start()
     read_scalars(
         [(hub_in, hub_ids), (send_in, send_ids), (row_in, tile_row), (col_in, tile_col)],
         scalar_sem,
@@ -240,7 +241,8 @@
         for u in range(UNROLL):
             lists[end + u if n < 3 else end - u] = z.nb << BITS
         lists[z.off_len + n] = end - start if n < 3 else start - end
-    load.wait()
+    for c in loads:
+        c.wait()
 
 
 def accumulate(z, lists, which, vals, source, acc, scale=None, begin=0, end=16):
@@ -401,31 +403,31 @@
     sent_shapes = [z.block(z.hub, BF16)] + [z.block(len(shifts) * z.tail, BF16) for _, shifts in z.messages]
     hub_ids, send_ids = hbm(hub_ids), hbm(send_ids)
 
-    field, hub, *tails = pl.pallas_call(
+    hub, *tails = pl.pallas_call(
         functools.partial(gather_kernel, z),
-        out_shape=[z.block_vmem(z.nb, BF16)] + sent_shapes,
+        out_shape=sent_shapes,
         in_specs=[ANY_SPEC] * 3,
-        out_specs=[VMEM_SPEC] + [ANY_SPEC] * len(sent_shapes),
+        out_specs=[ANY_SPEC] * len(sent_shapes),
         scratch_shapes=[
             pltpu.SMEM(hub_ids.shape, jnp.int32),
             pltpu.SMEM(send_ids.shape, jnp.int32),
             pltpu.SemaphoreType.DMA((2,)),
             pltpu.SemaphoreType.DMA((z.hub + (z.n_grp - 1) * z.tail,)),
-            pltpu.SemaphoreType.DMA(()),
         ],
         compiler_params=PARAMS,
         name="gather",
     )(hub_ids, send_ids, hbm(field0))
     got, arrays, parts = first_stage(z, hub, tails)
 
-    lists, vals = pl.pallas_call(
+    lists, vals, field = pl.pallas_call(
         functools.partial(bin_kernel, z),
         out_shape=[
             pltpu.SMEM((z.list_len,), jnp.int32),
             pltpu.VMEM(tile_val.shape, BF16),
+            z.block_vmem(z.nb, BF16),
         ],
-        in_specs=[SMEM_SPEC] + [ANY_SPEC] * 5,
-        out_specs=[SMEM_SPEC, VMEM_SPEC],
+        in_specs=[SMEM_SPEC] + [ANY_SPEC] * 6,
+        out_specs=[SMEM_SPEC, VMEM_SPEC, VMEM_SPEC],
         scratch_shapes=[
             pltpu.SMEM(hub_ids.shape, jnp.int32),
             pltpu.SMEM(send_ids.shape, jnp.int32),
@@ -435,12 +437,12 @@
             pltpu.SMEM((z.nb,), jnp.int32),
             pltpu.SMEM((4,), jnp.int32),
             pltpu.SemaphoreType.DMA((4,)),
-            pltpu.SemaphoreType.DMA(()),
+            pltpu.SemaphoreType.DMA((2,)),
         ],
         compiler_params=PARAMS,
         cost_estimate=cost(z, 0, 2 * (2 * z.slots * z.blk * z.blk + z.field_bytes)),
         name="binning",
-    )(tile_count, hub_ids, send_ids, hbm(tile_row), hbm(tile_col), hbm(tile_val))
+    )(tile_count, hub_ids, send_ids, hbm(tile_row), hbm(tile_col), hbm(tile_val), hbm(field0))
 
     acc_shape = z.block_vmem(z.nb + 1, F32)
     vals, field = vmem(vals), vmem(field)

time: 83.1 us -> 83.3 us (level)
  starting transfers between devices: 40.2 us -> 38.9 us
  waiting for transfers between devices: 15.5 us -> 16.6 us
    ppermute x24, waiting for transfers between devices: 14.6 us -> 15.7 us  [over_hub(): lax.ppermute(x, 'hub', [(i, hub_target(i, d, z.n_hub)) for i in range(z.n...]
    ppermute x24, starting transfers between devices: 32.8 us -> 31.8 us  [over_hub(): lax.ppermute(x, 'hub', [(i, hub_target(i, d, z.n_hub)) for i in range(z.n...]
  transfers between devices with their start and end apart: 36 -> 36, of which waited for: 11 -> 12; matrix products, arithmetic and copies ran while one was open for 0% -> 0% of each run, Pallas kernels for 24% -> 25%
where the time goes in v5:
time: 83.3 us; the launch traced here: 83 us
  starting transfers between devices  38.9 us (47%)
  Pallas kernels  26.4 us (32%)
  waiting for transfers between devices  16.6 us (20%)
  between operations  0.93 us (1%)
    ppermute x24, starting transfers between devices, over_hub(): lax.ppermute(x, 'hub', [(i, hub_target(i, d, z.n_hub)) for i in range(z.n...  31.8 us
    ppermute x24, waiting for transfers between devices, over_hub(): lax.ppermute(x, 'hub', [(i, hub_target(i, d, z.n_hub)) for i in range(z.n...  15.7 us
    pallas_call x4, Pallas kernels, shards(): pl.pallas_call(functools.partial(local_kernel, z, parts, step), out_shape...  8.93 us
    pallas_call x3, Pallas kernels, shards(): pl.pallas_call(functools.partial(finish_kernel, z, step), out_shape=[acc_...  7.43 us
    ppermute x12, starting transfers between devices, over_grp(): lax.ppermute(x, 'grp', [(i, grp_target(i, e, z.n_grp)) for i in range(z.n...  7.17 us
    pallas_call x1, Pallas kernels, shards(): pl.pallas_call(functools.partial(bin_kernel, z), out_shape=[pltpu.SMEM((z...  3.47 us
    pallas_call x1, Pallas kernels, shards(): pl.pallas_call(functools.partial(last_kernel, z, late_parts), out_shape=[...  2.68 us
    pallas_call x1, Pallas kernels, shards(): pl.pallas_call(functools.partial(gather_kernel, z), out_shape=sent_shapes...  1.86 us
  transfers between devices with their start and end apart: 36, of which 12 were waited for; matrix products, arithmetic and copies ran while one was open for 0% of the time, Pallas kernels for 25%

profile of v5, /device:TPU:0, one launch (start us, length us, event | category | flops | bytes accessed | tf_op | source)
XLA Modules:
  0.0 83.0 jit_solution(1632582392515358607)
XLA Ops:
  0.0 1.9 %gather.1 = (bf16[4,128,128]{2,1,0:T(8,128)(2,1)S(1)}, bf16[4,128,128]{2,1,0:T(8,128)(2,1)S(1)}, bf16[8,128,128]{2,1,0:T(8,128)(2,1)S(1)}) custom-call(s32[1,4]{1,0:T(1,128)} %hub_in.3, s32[1,4,4]{2,1,0:T(4,128)} %send_in.3, bf16[64,128,128]{2,1,0:T(8,128)(2,1)} %bitcast.2), custom_call_target="tpu_custom_call" | custom-call | tf_op jit(solution)/shard_map/gather/pallas_call | solution.py:406
  1.9 4.1 %collective-permute-start.2 = (bf16[4,128,128]{2,1,0:T(8,128)(2,1)S(1)}, bf16[4,128,128]{2,1,0:T(8,128)(2,1)S(1)}, u32[]{:S(2)}, u32[]{:S(2)}) collective-permute-start(bf16[4,128,128]{2,1,0:T(8,128)(2,1)S(1)} %get-tuple-element.50), channel_id=1, source_target_pairs={{0,4},{1,5},{2,6},{3,7},{4,0},{5,1},{6,2},{7,3},{8,12},{9,13},{10,... | collective-permute-start | bytes 393224 | tf_op jit(solution)/shard_map/ppermute | solution.py:360
  6.0 1.6 %collective-permute-start.1 = (bf16[4,128,128]{2,1,0:T(8,128)(2,1)S(1)}, bf16[4,128,128]{2,1,0:T(8,128)(2,1)S(1)}, u32[]{:S(2)}, u32[]{:S(2)}) collective-permute-start(bf16[4,128,128]{2,1,0:T(8,128)(2,1)S(1)} %get-tuple-element.50), channel_id=1, source_target_pairs={{0,2},{1,3},{2,0},{3,1},{4,6},{5,7},{6,4},{7,5},{8,10},{9,11},{10,... | collective-permute-start | bytes 393224 | tf_op jit(solution)/shard_map/ppermute | solution.py:360
  7.5 1.5 %collective-permute-start = (bf16[4,128,128]{2,1,0:T(8,128)(2,1)S(1)}, bf16[4,128,128]{2,1,0:T(8,128)(2,1)S(1)}, u32[]{:S(2)}, u32[]{:S(2)}) collective-permute-start(bf16[4,128,128]{2,1,0:T(8,128)(2,1)S(1)} %get-tuple-element.50), channel_id=1, source_target_pairs={{0,1},{1,0},{2,3},{3,2},{4,5},{5,4},{6,7},{7,6},{8,9},{9,8},{10,11... | collective-permute-start | bytes 393224 | tf_op jit(solution)/shard_map/ppermute | solution.py:360
  9.1 1.5 %collective-permute-start.4 = (bf16[8,128,128]{2,1,0:T(8,128)(2,1)S(1)}, bf16[8,128,128]{2,1,0:T(8,128)(2,1)S(1)}, u32[]{:S(2)}, u32[]{:S(2)}) collective-permute-start(bf16[8,128,128]{2,1,0:T(8,128)(2,1)S(1)} %get-tuple-element.55), channel_id=1, source_target_pairs={{0,16},{8,24},{16,0},{24,8},{1,17},{9,25},{17,1},{25,9},{2,18},{10... | collective-permute-start | bytes 786440 | tf_op jit(solution)/shard_map/ppermute | solution.py:364
  11.3 3.5 %binning.1 = (s32[852]{0:T(1024)S(4)}, bf16[192,128,128]{2,1,0:T(8,128)(2,1)S(1)}, bf16[64,128,128]{2,1,0:T(8,128)(2,1)S(1)}) custom-call(s32[1]{0:T(128)S(6)} %copy.30.tile_count, s32[1,4]{1,0:T(1,128)} %hub_in.3, s32[1,4,4]{2,1,0:T(4,128)} %send_in.3, s32[1,192]{1,0:T(1,128)} %row_in.1, s32[1,192]{1,0:T(1,128)} %col_in.1, bf16[192,128,128]{2,1,0:T(8,128)(2,1)} %vals_in.1, ...), custom_call_target="tpu_custom_call" | custom-call | bytes 16777216 | tf_op jit(solution)/shard_map/binning/pallas_call | solution.py:422
  14.7 0.0 collective-permute-done.1.rest_1_
  14.8 0.0 collective-permute-done.rest_2_
  14.8 0.5 collective-permute-start.7
  15.3 0.5 collective-permute-start.6
  15.8 0.0 collective-permute-start.3
  15.8 0.5 collective-permute-done.4.rest_4_
  16.3 0.1 collective-permute-start.5
  16.4 2.6 %collective-permute-start.8 = (bf16[4,128,128]{2,1,0:T(8,128)(2,1)S(1)}, bf16[4,128,128]{2,1,0:T(8,128)(2,1)S(1)}, u32[]{:S(2)}, u32[]{:S(2)}) collective-permute-start(bf16[4,128,128]{2,1,0:T(8,128)(2,1)S(1)} %collective-permute-done.2.rest_0_), channel_id=1, source_target_pairs={{0,3},{1,2},{2,1},{3,0},{4,7},{5,6},{6,5},{7,4},{8,11},{9,10},{10,... | collective-permute-start | bytes 393224 | tf_op jit(solution)/shard_map/ppermute | solution.py:360
  19.0 0.6 start.1.acc_in
  19.6 0.0 collective-permute-done.5.rest_5_
  19.6 2.6 %local.4.acc_in = f32[65,128,128]{2,1,0:T(8,128)S(1)} custom-call(s32[852]{0:T(1024)S(4)} %get-tuple-element.49.lists, bf16[192,128,128]{2,1,0:T(8,128)(2,1)S(1)} %get-tuple-element.52.vals, bf16[64,128,128]{2,1,0:T(8,128)(2,1)S(1)} %get-tuple-element.53.field.prev.rest_0_, f32[65,128,128]{2,1,0:T(8,128)S(1)} %start.1.acc_in, ...), custom_call_target="tpu_custom_call", output_to_operand_aliasing={{}: (3, {})} | custom-call | flops 402653184 | bytes 18874368 | tf_op jit(solution)/shard_map/local/pallas_call | solution.py:491
  22.2 1.2 %collective-permute-done.8.rest_2_ = bf16[4,128,128]{2,1,0:T(8,128)(2,1)S(1)} collective-permute-done((bf16[4,128,128]{2,1,0:T(8,128)(2,1)S(1)}, bf16[4,128,128]{2,1,0:T(8,128)(2,1)S(1)}, u32[]{:S(2)}, u32[]{:S(2)}) %collective-permute-start.8) | collective-permute-done | bytes 131104 | tf_op jit(solution)/shard_map/ppermute | solution.py:360
  23.4 0.0 collective-permute-done.7.rest_1_
  23.4 0.4 collective-permute-done.6.rest_0_
  23.8 0.4 edge.3
  24.2 2.1 %collective-permute-start.11 = (bf16[4,128,128]{2,1,0:T(8,128)(2,1)S(1)}, bf16[4,128,128]{2,1,0:T(8,128)(2,1)S(1)}, u32[]{:S(2)}, u32[]{:S(2)}) collective-permute-start(bf16[4,128,128]{2,1,0:T(8,128)(2,1)S(1)} %get-tuple-element.62), channel_id=1, source_target_pairs={{0,4},{1,5},{2,6},{3,7},{4,0},{5,1},{6,2},{7,3},{8,12},{9,13},{10,... | collective-permute-start | bytes 393224 | tf_op jit(solution)/shard_map/ppermute | solution.py:360
  26.3 1.2 %collective-permute-start.10 = (bf16[4,128,128]{2,1,0:T(8,128)(2,1)S(1)}, bf16[4,128,128]{2,1,0:T(8,128)(2,1)S(1)}, u32[]{:S(2)}, u32[]{:S(2)}) collective-permute-start(bf16[4,128,128]{2,1,0:T(8,128)(2,1)S(1)} %get-tuple-element.62), channel_id=1, source_target_pairs={{0,2},{1,3},{2,0},{3,1},{4,6},{5,7},{6,4},{7,5},{8,10},{9,11},{10,... | collective-permute-start | bytes 393224 | tf_op jit(solution)/shard_map/ppermute | solution.py:360
  27.6 0.6 collective-permute-start.9
  28.2 1.5 %collective-permute-start.13 = (bf16[8,128,128]{2,1,0:T(8,128)(2,1)S(1)}, bf16[8,128,128]{2,1,0:T(8,128)(2,1)S(1)}, u32[]{:S(2)}, u32[]{:S(2)}) collective-permute-start(bf16[8,128,128]{2,1,0:T(8,128)(2,1)S(1)} %get-tuple-element.66), channel_id=1, source_target_pairs={{0,16},{8,24},{16,0},{24,8},{1,17},{9,25},{17,1},{25,9},{2,18},{10... | collective-permute-start | bytes 786440 | tf_op jit(solution)/shard_map/ppermute | solution.py:364
  29.7 2.1 %finish.3 = (f32[65,128,128]{2,1,0:T(8,128)S(1)}, bf16[64,128,128]{2,1,0:T(8,128)(2,1)S(1)}) custom-call(s32[852]{0:T(1024)S(4)} %get-tuple-element.49.lists, bf16[192,128,128]{2,1,0:T(8,128)(2,1)S(1)} %get-tuple-element.52.vals, bf16[16,128,128]{2,1,0:T(8,128)(2,1)S(1)} %get-tuple-element.59.rem, ...), custom_call_target="tpu_custom_call", output_to_operand_aliasing={{0}: (4, {})} | custom-call | flops 201326592 | bytes 19922944 | tf_op jit(solution)/shard_map/finish/pallas_call | solution.py:474
  31.8 1.0 %collective-permute-done.11.rest_0_ = bf16[4,128,128]{2,1,0:T(8,128)(2,1)S(1)} collective-permute-done((bf16[4,128,128]{2,1,0:T(8,128)(2,1)S(1)}, bf16[4,128,128]{2,1,0:T(8,128)(2,1)S(1)}, u32[]{:S(2)}, u32[]{:S(2)}) %collective-permute-start.11) | collective-permute-done | bytes 131104 | tf_op jit(solution)/shard_map/ppermute | solution.py:360
  32.8 0.5 collective-permute-done.10.rest_1_
  33.3 0.0 collective-permute-done.9.rest_2_
  33.4 0.5 collective-permute-start.16
  33.9 1.2 %collective-permute-start.15 = (bf16[6,128,128]{2,1,0:T(8,128)(2,1)S(1)}, bf16[6,128,128]{2,1,0:T(8,128)(2,1)S(1)}, u32[]{:S(2)}, u32[]{:S(2)}) collective-permute-start(bf16[6,128,128]{2,1,0:T(8,128)(2,1)S(1)} %get-tuple-element.98), channel_id=1, source_target_pairs={{0,1},{1,0},{2,3},{3,2},{4,5},{5,4},{6,7},{7,6},{8,9},{9,8},{10,11... | collective-permute-start | bytes 589832 | tf_op jit(solution)/shard_map/ppermute | solution.py:360
  35.1 0.6 collective-permute-start.14
  35.7 1.8 %collective-permute-start.17 = (bf16[4,128,128]{2,1,0:T(8,128)(2,1)S(1)}, bf16[4,128,128]{2,1,0:T(8,128)(2,1)S(1)}, u32[]{:S(2)}, u32[]{:S(2)}) collective-permute-start(bf16[4,128,128]{2,1,0:T(8,128)(2,1)S(1)} %collective-permute-done.11.rest_0_), channel_id=1, source_target_pairs={{0,3},{1,2},{2,1},{3,0},{4,7},{5,6},{6,5},{7,4},{8,11},{9,10},{10,... | collective-permute-start | bytes 393224 | tf_op jit(solution)/shard_map/ppermute | solution.py:360
  37.5 1.9 %local.5.acc_in = f32[65,128,128]{2,1,0:T(8,128)S(1)} custom-call(s32[852]{0:T(1024)S(4)} %get-tuple-element.49.lists, bf16[192,128,128]{2,1,0:T(8,128)(2,1)S(1)} %get-tuple-element.52.vals, bf16[64,128,128]{2,1,0:T(8,128)(2,1)S(1)} %get-tuple-element.61.field.rest_1_.prev, ...), custom_call_target="tpu_custom_call", output_to_operand_aliasing={{}: (3, {})} | custom-call | flops 402653184 | bytes 18874368 | tf_op jit(solution)/shard_map/local/pallas_call | solution.py:491
  39.5 3.7 %collective-permute-done.17.rest_2_ = bf16[4,128,128]{2,1,0:T(8,128)(2,1)S(1)} collective-permute-done((bf16[4,128,128]{2,1,0:T(8,128)(2,1)S(1)}, bf16[4,128,128]{2,1,0:T(8,128)(2,1)S(1)}, u32[]{:S(2)}, u32[]{:S(2)}) %collective-permute-start.17) | collective-permute-done | bytes 131104 | tf_op jit(solution)/shard_map/ppermute | solution.py:360
  43.2 0.5 edge.4
  43.7 1.9 %collective-permute-start.20 = (bf16[4,128,128]{2,1,0:T(8,128)(2,1)S(1)}, bf16[4,128,128]{2,1,0:T(8,128)(2,1)S(1)}, u32[]{:S(2)}, u32[]{:S(2)}) collective-permute-start(bf16[4,128,128]{2,1,0:T(8,128)(2,1)S(1)} %get-tuple-element.73), channel_id=1, source_target_pairs={{0,4},{1,5},{2,6},{3,7},{4,0},{5,1},{6,2},{7,3},{8,12},{9,13},{10,... | collective-permute-start | bytes 393224 | tf_op jit(solution)/shard_map/ppermute | solution.py:360
  45.6 0.4 collective-permute-start.19
  45.9 1.4 %collective-permute-start.18 = (bf16[4,128,128]{2,1,0:T(8,128)(2,1)S(1)}, bf16[4,128,128]{2,1,0:T(8,128)(2,1)S(1)}, u32[]{:S(2)}, u32[]{:S(2)}) collective-permute-start(bf16[4,128,128]{2,1,0:T(8,128)(2,1)S(1)} %get-tuple-element.73), channel_id=1, source_target_pairs={{0,1},{1,0},{2,3},{3,2},{4,5},{5,4},{6,7},{7,6},{8,9},{9,8},{10,11... | collective-permute-start | bytes 393224 | tf_op jit(solution)/shard_map/ppermute | solution.py:360
  47.3 1.5 %collective-permute-start.22 = (bf16[8,128,128]{2,1,0:T(8,128)(2,1)S(1)}, bf16[8,128,128]{2,1,0:T(8,128)(2,1)S(1)}, u32[]{:S(2)}, u32[]{:S(2)}) collective-permute-start(bf16[8,128,128]{2,1,0:T(8,128)(2,1)S(1)} %get-tuple-element.77), channel_id=1, source_target_pairs={{0,16},{8,24},{16,0},{24,8},{1,17},{9,25},{17,1},{25,9},{2,18},{10... | collective-permute-start | bytes 786440 | tf_op jit(solution)/shard_map/ppermute | solution.py:364
  48.8 2.5 %finish.4 = (f32[65,128,128]{2,1,0:T(8,128)S(1)}, bf16[64,128,128]{2,1,0:T(8,128)(2,1)S(1)}) custom-call(s32[852]{0:T(1024)S(4)} %get-tuple-element.49.lists, bf16[192,128,128]{2,1,0:T(8,128)(2,1)S(1)} %get-tuple-element.52.vals, bf16[16,128,128]{2,1,0:T(8,128)(2,1)S(1)} %get-tuple-element.70.rem, ...), custom_call_target="tpu_custom_call", output_to_operand_aliasing={{0}: (5, {})} | custom-call | flops 201326592 | bytes 19922944 | tf_op jit(solution)/shard_map/finish/pallas_call | solution.py:474
  51.3 0.8 collective-permute-done.20.rest_0_
  52.0 0.1 collective-permute-done.19.rest_1_
  52.2 0.4 collective-permute-start.25
  52.7 1.1 %collective-permute-start.24 = (bf16[6,128,128]{2,1,0:T(8,128)(2,1)S(1)}, bf16[6,128,128]{2,1,0:T(8,128)(2,1)S(1)}, u32[]{:S(2)}, u32[]{:S(2)}) collective-permute-start(bf16[6,128,128]{2,1,0:T(8,128)(2,1)S(1)} %get-tuple-element.96), channel_id=1, source_target_pairs={{0,1},{1,0},{2,3},{3,2},{4,5},{5,4},{6,7},{7,6},{8,9},{9,8},{10,11... | collective-permute-start | bytes 589832 | tf_op jit(solution)/shard_map/ppermute | solution.py:360
  53.8 0.6 collective-permute-start.23
  54.3 2.1 %collective-permute-start.26 = (bf16[4,128,128]{2,1,0:T(8,128)(2,1)S(1)}, bf16[4,128,128]{2,1,0:T(8,128)(2,1)S(1)}, u32[]{:S(2)}, u32[]{:S(2)}) collective-permute-start(bf16[4,128,128]{2,1,0:T(8,128)(2,1)S(1)} %collective-permute-done.20.rest_0_), channel_id=1, source_target_pairs={{0,3},{1,2},{2,1},{3,0},{4,7},{5,6},{6,5},{7,4},{8,11},{9,10},{10,... | collective-permute-start | bytes 393224 | tf_op jit(solution)/shard_map/ppermute | solution.py:360
  56.4 1.9 %local.6.acc_in = f32[65,128,128]{2,1,0:T(8,128)S(1)} custom-call(s32[852]{0:T(1024)S(4)} %get-tuple-element.49.lists, bf16[192,128,128]{2,1,0:T(8,128)(2,1)S(1)} %get-tuple-element.52.vals, bf16[64,128,128]{2,1,0:T(8,128)(2,1)S(1)} %get-tuple-element.72.field.rest_2_, f32[65,128,128]{2,1,0:T(8,128)S(1)} %get-tuple-element.75.acc_in, ...), custom_call_target="tpu_custom_call", output_to_operand_aliasing={{}: (3, {})} | custom-call | flops 402653184 | bytes 18874368 | tf_op jit(solution)/shard_map/local/pallas_call | solution.py:491
  58.3 3.6 %collective-permute-done.26.rest_2_ = bf16[4,128,128]{2,1,0:T(8,128)(2,1)S(1)} collective-permute-done((bf16[4,128,128]{2,1,0:T(8,128)(2,1)S(1)}, bf16[4,128,128]{2,1,0:T(8,128)(2,1)S(1)}, u32[]{:S(2)}, u32[]{:S(2)}) %collective-permute-start.26) | collective-permute-done | bytes 131104 | tf_op jit(solution)/shard_map/ppermute | solution.py:360
  61.9 0.5 edge.5
  62.4 1.1 %collective-permute-start.29 = (bf16[4,128,128]{2,1,0:T(8,128)(2,1)S(1)}, bf16[4,128,128]{2,1,0:T(8,128)(2,1)S(1)}, u32[]{:S(2)}, u32[]{:S(2)}) collective-permute-start(bf16[4,128,128]{2,1,0:T(8,128)(2,1)S(1)} %get-tuple-element.84), channel_id=1, source_target_pairs={{0,4},{1,5},{2,6},{3,7},{4,0},{5,1},{6,2},{7,3},{8,12},{9,13},{10,... | collective-permute-start | bytes 393224 | tf_op jit(solution)/shard_map/ppermute | solution.py:360
  63.5 0.7 collective-permute-start.28
  64.2 1.0 %collective-permute-start.27 = (bf16[4,128,128]{2,1,0:T(8,128)(2,1)S(1)}, bf16[4,128,128]{2,1,0:T(8,128)(2,1)S(1)}, u32[]{:S(2)}, u32[]{:S(2)}) collective-permute-start(bf16[4,128,128]{2,1,0:T(8,128)(2,1)S(1)} %get-tuple-element.84), channel_id=1, source_target_pairs={{0,1},{1,0},{2,3},{3,2},{4,5},{5,4},{6,7},{7,6},{8,9},{9,8},{10,11... | collective-permute-start | bytes 393224 | tf_op jit(solution)/shard_map/ppermute | solution.py:360
  65.1 1.2 %collective-permute-start.31 = (bf16[8,128,128]{2,1,0:T(8,128)(2,1)S(1)}, bf16[8,128,128]{2,1,0:T(8,128)(2,1)S(1)}, u32[]{:S(2)}, u32[]{:S(2)}) collective-permute-start(bf16[8,128,128]{2,1,0:T(8,128)(2,1)S(1)} %get-tuple-element.88), channel_id=1, source_target_pairs={{0,16},{8,24},{16,0},{24,8},{1,17},{9,25},{17,1},{25,9},{2,18},{10... | collective-permute-start | bytes 786440 | tf_op jit(solution)/shard_map/ppermute | solution.py:364
  66.3 2.9 %finish.5 = (f32[65,128,128]{2,1,0:T(8,128)S(1)}, bf16[64,128,128]{2,1,0:T(8,128)(2,1)S(1)}) custom-call(s32[852]{0:T(1024)S(4)} %get-tuple-element.49.lists, bf16[192,128,128]{2,1,0:T(8,128)(2,1)S(1)} %get-tuple-element.52.vals, bf16[16,128,128]{2,1,0:T(8,128)(2,1)S(1)} %get-tuple-element.81.rem, ...), custom_call_target="tpu_custom_call", output_to_operand_aliasing={{0}: (6, {})} | custom-call | flops 201326592 | bytes 19922944 | tf_op jit(solution)/shard_map/finish/pallas_call | solution.py:474
  69.2 1.5 %collective-permute-done.29.rest_0_ = bf16[4,128,128]{2,1,0:T(8,128)(2,1)S(1)} collective-permute-done((bf16[4,128,128]{2,1,0:T(8,128)(2,1)S(1)}, bf16[4,128,128]{2,1,0:T(8,128)(2,1)S(1)}, u32[]{:S(2)}, u32[]{:S(2)}) %collective-permute-start.29) | collective-permute-done | bytes 131104 | tf_op jit(solution)/shard_map/ppermute | solution.py:360
  70.7 0.2 collective-permute-start.34
  70.8 0.9 %collective-permute-start.33 = (bf16[6,128,128]{2,1,0:T(8,128)(2,1)S(1)}, bf16[6,128,128]{2,1,0:T(8,128)(2,1)S(1)}, u32[]{:S(2)}, u32[]{:S(2)}) collective-permute-start(bf16[6,128,128]{2,1,0:T(8,128)(2,1)S(1)} %get-tuple-element.94), channel_id=1, source_target_pairs={{0,1},{1,0},{2,3},{3,2},{4,5},{5,4},{6,7},{7,6},{8,9},{9,8},{10,11... | collective-permute-start | bytes 589832 | tf_op jit(solution)/shard_map/ppermute | solution.py:360
  71.8 0.4 collective-permute-done.31.rest_4_
  72.2 0.2 collective-permute-start.32
  72.4 2.5 %collective-permute-start.35 = (bf16[4,128,128]{2,1,0:T(8,128)(2,1)S(1)}, bf16[4,128,128]{2,1,0:T(8,128)(2,1)S(1)}, u32[]{:S(2)}, u32[]{:S(2)}) collective-permute-start(bf16[4,128,128]{2,1,0:T(8,128)(2,1)S(1)} %collective-permute-done.29.rest_0_), channel_id=1, source_target_pairs={{0,3},{1,2},{2,1},{3,0},{4,7},{5,6},{6,5},{7,4},{8,11},{9,10},{10,... | collective-permute-start | bytes 393224 | tf_op jit(solution)/shard_map/ppermute | solution.py:360
  74.8 2.5 %local.7.acc_in = f32[65,128,128]{2,1,0:T(8,128)S(1)} custom-call(s32[852]{0:T(1024)S(4)} %get-tuple-element.49.lists, bf16[192,128,128]{2,1,0:T(8,128)(2,1)S(1)} %get-tuple-element.52.vals, bf16[64,128,128]{2,1,0:T(8,128)(2,1)S(1)} %get-tuple-element.83.field, f32[65,128,128]{2,1,0:T(8,128)S(1)} %get-tuple-element.86.acc_in, ...), custom_call_target="tpu_custom_call", output_to_operand_aliasing={{}: (3, {})} | custom-call | flops 402653184 | bytes 18874368 | tf_op jit(solution)/shard_map/local/pallas_call | solution.py:491
  77.4 3.0 %collective-permute-done.35.rest_2_ = bf16[4,128,128]{2,1,0:T(8,128)(2,1)S(1)} collective-permute-done((bf16[4,128,128]{2,1,0:T(8,128)(2,1)S(1)}, bf16[4,128,128]{2,1,0:T(8,128)(2,1)S(1)}, u32[]{:S(2)}, u32[]{:S(2)}) %collective-permute-start.35) | collective-permute-done | bytes 131104 | tf_op jit(solution)/shard_map/ppermute | solution.py:360
  80.4 2.7 %last.1 = (f32[65,128,128]{2,1,0:T(8,128)S(1)}, f32[64,128,128]{2,1,0:T(8,128)}) custom-call(s32[852]{0:T(1024)S(4)} %get-tuple-element.49.lists, bf16[192,128,128]{2,1,0:T(8,128)(2,1)S(1)} %get-tuple-element.52.vals, f32[65,128,128]{2,1,0:T(8,128)S(1)} %local.7.acc_in, ...), custom_call_target="tpu_custom_call", output_to_operand_aliasing={{0}: (2, {})} | custom-call | tf_op jit(solution)/shard_map/last/pallas_call | solution.py:503
  (38 shorter events, 0.3 us)
Async XLA Ops:
  1.9 12.9 %collective-permute-start.2 = (bf16[4,128,128]{2,1,0:T(8,128)(2,1)S(1)}, bf16[4,128,128]{2,1,0:T(8,128)(2,1)S(1)}, u32[]{:S(2)}, u32[]{:S(2)}) collective-permute-start(bf16[4,128,128]{2,1,0:T(8,128)(2,1)S(1)} %get-tuple-element.50), channel_id=1, source_target_pairs={{0,4},{1,5},{2,6},{3,7},{4,0},{5,1},{6,2},{7,3},{8,12},{9,13},{10,... | collective-permute-start | bytes 393224 | tf_op jit(solution)/shard_map/ppermute | solution.py:360
  6.0 8.8 %collective-permute-start.1 = (bf16[4,128,128]{2,1,0:T(8,128)(2,1)S(1)}, bf16[4,128,128]{2,1,0:T(8,128)(2,1)S(1)}, u32[]{:S(2)}, u32[]{:S(2)}) collective-permute-start(bf16[4,128,128]{2,1,0:T(8,128)(2,1)S(1)} %get-tuple-element.50), channel_id=1, source_target_pairs={{0,2},{1,3},{2,0},{3,1},{4,6},{5,7},{6,4},{7,5},{8,10},{9,11},{10,... | collective-permute-start | bytes 393224 | tf_op jit(solution)/shard_map/ppermute | solution.py:360
  7.5 7.2 %collective-permute-start = (bf16[4,128,128]{2,1,0:T(8,128)(2,1)S(1)}, bf16[4,128,128]{2,1,0:T(8,128)(2,1)S(1)}, u32[]{:S(2)}, u32[]{:S(2)}) collective-permute-start(bf16[4,128,128]{2,1,0:T(8,128)(2,1)S(1)} %get-tuple-element.50), channel_id=1, source_target_pairs={{0,1},{1,0},{2,3},{3,2},{4,5},{5,4},{6,7},{7,6},{8,9},{9,8},{10,11... | collective-permute-start | bytes 393224 | tf_op jit(solution)/shard_map/ppermute | solution.py:360
  9.1 7.2 %collective-permute-start.4 = (bf16[8,128,128]{2,1,0:T(8,128)(2,1)S(1)}, bf16[8,128,128]{2,1,0:T(8,128)(2,1)S(1)}, u32[]{:S(2)}, u32[]{:S(2)}) collective-permute-start(bf16[8,128,128]{2,1,0:T(8,128)(2,1)S(1)} %get-tuple-element.55), channel_id=1, source_target_pairs={{0,16},{8,24},{16,0},{24,8},{1,17},{9,25},{17,1},{25,9},{2,18},{10... | collective-permute-start | bytes 786440 | tf_op jit(solution)/shard_map/ppermute | solution.py:364
  14.8 8.6 %collective-permute-start.7 = (bf16[6,128,128]{2,1,0:T(8,128)(2,1)S(1)}, bf16[6,128,128]{2,1,0:T(8,128)(2,1)S(1)}, u32[]{:S(2)}, u32[]{:S(2)}) collective-permute-start(bf16[6,128,128]{2,1,0:T(8,128)(2,1)S(1)} %get-tuple-element.99), channel_id=1, source_target_pairs={{0,2},{1,3},{2,0},{3,1},{4,6},{5,7},{6,4},{7,5},{8,10},{9,11},{10,... | collective-permute-start | bytes 589832 | tf_op jit(solution)/shard_map/ppermute | solution.py:360
  15.3 8.5 %collective-permute-start.6 = (bf16[6,128,128]{2,1,0:T(8,128)(2,1)S(1)}, bf16[6,128,128]{2,1,0:T(8,128)(2,1)S(1)}, u32[]{:S(2)}, u32[]{:S(2)}) collective-permute-start(bf16[6,128,128]{2,1,0:T(8,128)(2,1)S(1)} %get-tuple-element.100), channel_id=1, source_target_pairs={{0,1},{1,0},{2,3},{3,2},{4,5},{5,4},{6,7},{7,6},{8,9},{9,8},{10,11... | collective-permute-start | bytes 589832 | tf_op jit(solution)/shard_map/ppermute | solution.py:360
  15.8 3.8 %collective-permute-start.3 = (bf16[4,128,128]{2,1,0:T(8,128)(2,1)S(1)}, bf16[4,128,128]{2,1,0:T(8,128)(2,1)S(1)}, u32[]{:S(2)}, u32[]{:S(2)}) collective-permute-start(bf16[4,128,128]{2,1,0:T(8,128)(2,1)S(1)} %get-tuple-element.54), channel_id=1, source_target_pairs={{0,8},{8,0},{16,24},{24,16},{1,9},{9,1},{17,25},{25,17},{2,10},{10... | collective-permute-start | bytes 393224 | tf_op jit(solution)/shard_map/ppermute | solution.py:364
  16.3 3.3 %collective-permute-start.5 = (bf16[4,128,128]{2,1,0:T(8,128)(2,1)S(1)}, bf16[4,128,128]{2,1,0:T(8,128)(2,1)S(1)}, u32[]{:S(2)}, u32[]{:S(2)}) collective-permute-start(bf16[4,128,128]{2,1,0:T(8,128)(2,1)S(1)} %slice.48), channel_id=1, source_target_pairs={{0,8},{8,0},{16,24},{24,16},{1,9},{9,1},{17,25},{25,17},{2,10},{10... | collective-permute-start | bytes 393224 | tf_op jit(solution)/shard_map/ppermute | solution.py:364
  16.4 7.0 %collective-permute-start.8 = (bf16[4,128,128]{2,1,0:T(8,128)(2,1)S(1)}, bf16[4,128,128]{2,1,0:T(8,128)(2,1)S(1)}, u32[]{:S(2)}, u32[]{:S(2)}) collective-permute-start(bf16[4,128,128]{2,1,0:T(8,128)(2,1)S(1)} %collective-permute-done.2.rest_0_), channel_id=1, source_target_pairs={{0,3},{1,2},{2,1},{3,0},{4,7},{5,6},{6,5},{7,4},{8,11},{9,10},{10,... | collective-permute-start | bytes 393224 | tf_op jit(solution)/shard_map/ppermute | solution.py:360
  24.2 8.6 %collective-permute-start.11 = (bf16[4,128,128]{2,1,0:T(8,128)(2,1)S(1)}, bf16[4,128,128]{2,1,0:T(8,128)(2,1)S(1)}, u32[]{:S(2)}, u32[]{:S(2)}) collective-permute-start(bf16[4,128,128]{2,1,0:T(8,128)(2,1)S(1)} %get-tuple-element.62), channel_id=1, source_target_pairs={{0,4},{1,5},{2,6},{3,7},{4,0},{5,1},{6,2},{7,3},{8,12},{9,13},{10,... | collective-permute-start | bytes 393224 | tf_op jit(solution)/shard_map/ppermute | solution.py:360
  26.3 7.0 %collective-permute-start.10 = (bf16[4,128,128]{2,1,0:T(8,128)(2,1)S(1)}, bf16[4,128,128]{2,1,0:T(8,128)(2,1)S(1)}, u32[]{:S(2)}, u32[]{:S(2)}) collective-permute-start(bf16[4,128,128]{2,1,0:T(8,128)(2,1)S(1)} %get-tuple-element.62), channel_id=1, source_target_pairs={{0,2},{1,3},{2,0},{3,1},{4,6},{5,7},{6,4},{7,5},{8,10},{9,11},{10,... | collective-permute-start | bytes 393224 | tf_op jit(solution)/shard_map/ppermute | solution.py:360
  27.6 5.7 %collective-permute-start.9 = (bf16[4,128,128]{2,1,0:T(8,128)(2,1)S(1)}, bf16[4,128,128]{2,1,0:T(8,128)(2,1)S(1)}, u32[]{:S(2)}, u32[]{:S(2)}) collective-permute-start(bf16[4,128,128]{2,1,0:T(8,128)(2,1)S(1)} %get-tuple-element.62), channel_id=1, source_target_pairs={{0,1},{1,0},{2,3},{3,2},{4,5},{5,4},{6,7},{7,6},{8,9},{9,8},{10,11... | collective-permute-start | bytes 393224 | tf_op jit(solution)/shard_map/ppermute | solution.py:360
  28.2 6.9 %collective-permute-start.13 = (bf16[8,128,128]{2,1,0:T(8,128)(2,1)S(1)}, bf16[8,128,128]{2,1,0:T(8,128)(2,1)S(1)}, u32[]{:S(2)}, u32[]{:S(2)}) collective-permute-start(bf16[8,128,128]{2,1,0:T(8,128)(2,1)S(1)} %get-tuple-element.66), channel_id=1, source_target_pairs={{0,16},{8,24},{16,0},{24,8},{1,17},{9,25},{17,1},{25,9},{2,18},{10... | collective-permute-start | bytes 786440 | tf_op jit(solution)/shard_map/ppermute | solution.py:364
  33.4 9.8 %collective-permute-start.16 = (bf16[6,128,128]{2,1,0:T(8,128)(2,1)S(1)}, bf16[6,128,128]{2,1,0:T(8,128)(2,1)S(1)}, u32[]{:S(2)}, u32[]{:S(2)}) collective-permute-start(bf16[6,128,128]{2,1,0:T(8,128)(2,1)S(1)} %get-tuple-element.97), channel_id=1, source_target_pairs={{0,2},{1,3},{2,0},{3,1},{4,6},{5,7},{6,4},{7,5},{8,10},{9,11},{10,... | collective-permute-start | bytes 589832 | tf_op jit(solution)/shard_map/ppermute | solution.py:360
  33.9 9.3 %collective-permute-start.15 = (bf16[6,128,128]{2,1,0:T(8,128)(2,1)S(1)}, bf16[6,128,128]{2,1,0:T(8,128)(2,1)S(1)}, u32[]{:S(2)}, u32[]{:S(2)}) collective-permute-start(bf16[6,128,128]{2,1,0:T(8,128)(2,1)S(1)} %get-tuple-element.98), channel_id=1, source_target_pairs={{0,1},{1,0},{2,3},{3,2},{4,5},{5,4},{6,7},{7,6},{8,9},{9,8},{10,11... | collective-permute-start | bytes 589832 | tf_op jit(solution)/shard_map/ppermute | solution.py:360
  35.1 2.4 %collective-permute-start.12 = (bf16[4,128,128]{2,1,0:T(8,128)(2,1)S(1)}, bf16[4,128,128]{2,1,0:T(8,128)(2,1)S(1)}, u32[]{:S(2)}, u32[]{:S(2)}) collective-permute-start(bf16[4,128,128]{2,1,0:T(8,128)(2,1)S(1)} %get-tuple-element.65), channel_id=1, source_target_pairs={{0,8},{8,0},{16,24},{24,16},{1,9},{9,1},{17,25},{25,17},{2,10},{10... | collective-permute-start | bytes 393224 | tf_op jit(solution)/shard_map/ppermute | solution.py:364
  35.1 2.4 %collective-permute-start.14 = (bf16[4,128,128]{2,1,0:T(8,128)(2,1)S(1)}, bf16[4,128,128]{2,1,0:T(8,128)(2,1)S(1)}, u32[]{:S(2)}, u32[]{:S(2)}) collective-permute-start(bf16[4,128,128]{2,1,0:T(8,128)(2,1)S(1)} %slice.49), channel_id=1, source_target_pairs={{0,8},{8,0},{16,24},{24,16},{1,9},{9,1},{17,25},{25,17},{2,10},{10... | collective-permute-start | bytes 393224 | tf_op jit(solution)/shard_map/ppermute | solution.py:364
  35.7 7.5 %collective-permute-start.17 = (bf16[4,128,128]{2,1,0:T(8,128)(2,1)S(1)}, bf16[4,128,128]{2,1,0:T(8,128)(2,1)S(1)}, u32[]{:S(2)}, u32[]{:S(2)}) collective-permute-start(bf16[4,128,128]{2,1,0:T(8,128)(2,1)S(1)} %collective-permute-done.11.rest_0_), channel_id=1, source_target_pairs={{0,3},{1,2},{2,1},{3,0},{4,7},{5,6},{6,5},{7,4},{8,11},{9,10},{10,... | collective-permute-start | bytes 393224 | tf_op jit(solution)/shard_map/ppermute | solution.py:360
  43.7 8.4 %collective-permute-start.20 = (bf16[4,128,128]{2,1,0:T(8,128)(2,1)S(1)}, bf16[4,128,128]{2,1,0:T(8,128)(2,1)S(1)}, u32[]{:S(2)}, u32[]{:S(2)}) collective-permute-start(bf16[4,128,128]{2,1,0:T(8,128)(2,1)S(1)} %get-tuple-element.73), channel_id=1, source_target_pairs={{0,4},{1,5},{2,6},{3,7},{4,0},{5,1},{6,2},{7,3},{8,12},{9,13},{10,... | collective-permute-start | bytes 393224 | tf_op jit(solution)/shard_map/ppermute | solution.py:360
  45.6 6.6 %collective-permute-start.19 = (bf16[4,128,128]{2,1,0:T(8,128)(2,1)S(1)}, bf16[4,128,128]{2,1,0:T(8,128)(2,1)S(1)}, u32[]{:S(2)}, u32[]{:S(2)}) collective-permute-start(bf16[4,128,128]{2,1,0:T(8,128)(2,1)S(1)} %get-tuple-element.73), channel_id=1, source_target_pairs={{0,2},{1,3},{2,0},{3,1},{4,6},{5,7},{6,4},{7,5},{8,10},{9,11},{10,... | collective-permute-start | bytes 393224 | tf_op jit(solution)/shard_map/ppermute | solution.py:360
  45.9 6.3 %collective-permute-start.18 = (bf16[4,128,128]{2,1,0:T(8,128)(2,1)S(1)}, bf16[4,128,128]{2,1,0:T(8,128)(2,1)S(1)}, u32[]{:S(2)}, u32[]{:S(2)}) collective-permute-start(bf16[4,128,128]{2,1,0:T(8,128)(2,1)S(1)} %get-tuple-element.73), channel_id=1, source_target_pairs={{0,1},{1,0},{2,3},{3,2},{4,5},{5,4},{6,7},{7,6},{8,9},{9,8},{10,11... | collective-permute-start | bytes 393224 | tf_op jit(solution)/shard_map/ppermute | solution.py:360
  47.3 6.4 %collective-permute-start.22 = (bf16[8,128,128]{2,1,0:T(8,128)(2,1)S(1)}, bf16[8,128,128]{2,1,0:T(8,128)(2,1)S(1)}, u32[]{:S(2)}, u32[]{:S(2)}) collective-permute-start(bf16[8,128,128]{2,1,0:T(8,128)(2,1)S(1)} %get-tuple-element.77), channel_id=1, source_target_pairs={{0,16},{8,24},{16,0},{24,8},{1,17},{9,25},{17,1},{25,9},{2,18},{10... | collective-permute-start | bytes 786440 | tf_op jit(solution)/shard_map/ppermute | solution.py:364
  52.2 9.7 %collective-permute-start.25 = (bf16[6,128,128]{2,1,0:T(8,128)(2,1)S(1)}, bf16[6,128,128]{2,1,0:T(8,128)(2,1)S(1)}, u32[]{:S(2)}, u32[]{:S(2)}) collective-permute-start(bf16[6,128,128]{2,1,0:T(8,128)(2,1)S(1)} %get-tuple-element.95), channel_id=1, source_target_pairs={{0,2},{1,3},{2,0},{3,1},{4,6},{5,7},{6,4},{7,5},{8,10},{9,11},{10,... | collective-permute-start | bytes 589832 | tf_op jit(solution)/shard_map/ppermute | solution.py:360
  52.7 9.3 %collective-permute-start.24 = (bf16[6,128,128]{2,1,0:T(8,128)(2,1)S(1)}, bf16[6,128,128]{2,1,0:T(8,128)(2,1)S(1)}, u32[]{:S(2)}, u32[]{:S(2)}) collective-permute-start(bf16[6,128,128]{2,1,0:T(8,128)(2,1)S(1)} %get-tuple-element.96), channel_id=1, source_target_pairs={{0,1},{1,0},{2,3},{3,2},{4,5},{5,4},{6,7},{7,6},{8,9},{9,8},{10,11... | collective-permute-start | bytes 589832 | tf_op jit(solution)/shard_map/ppermute | solution.py:360
  53.7 2.7 %collective-permute-start.21 = (bf16[4,128,128]{2,1,0:T(8,128)(2,1)S(1)}, bf16[4,128,128]{2,1,0:T(8,128)(2,1)S(1)}, u32[]{:S(2)}, u32[]{:S(2)}) collective-permute-start(bf16[4,128,128]{2,1,0:T(8,128)(2,1)S(1)} %get-tuple-element.76), channel_id=1, source_target_pairs={{0,8},{8,0},{16,24},{24,16},{1,9},{9,1},{17,25},{25,17},{2,10},{10... | collective-permute-start | bytes 393224 | tf_op jit(solution)/shard_map/ppermute | solution.py:364
  53.8 2.6 %collective-permute-start.23 = (bf16[4,128,128]{2,1,0:T(8,128)(2,1)S(1)}, bf16[4,128,128]{2,1,0:T(8,128)(2,1)S(1)}, u32[]{:S(2)}, u32[]{:S(2)}) collective-permute-start(bf16[4,128,128]{2,1,0:T(8,128)(2,1)S(1)} %slice.50), channel_id=1, source_target_pairs={{0,8},{8,0},{16,24},{24,16},{1,9},{9,1},{17,25},{25,17},{2,10},{10... | collective-permute-start | bytes 393224 | tf_op jit(solution)/shard_map/ppermute | solution.py:364
  54.3 7.6 %collective-permute-start.26 = (bf16[4,128,128]{2,1,0:T(8,128)(2,1)S(1)}, bf16[4,128,128]{2,1,0:T(8,128)(2,1)S(1)}, u32[]{:S(2)}, u32[]{:S(2)}) collective-permute-start(bf16[4,128,128]{2,1,0:T(8,128)(2,1)S(1)} %collective-permute-done.20.rest_0_), channel_id=1, source_target_pairs={{0,3},{1,2},{2,1},{3,0},{4,7},{5,6},{6,5},{7,4},{8,11},{9,10},{10,... | collective-permute-start | bytes 393224 | tf_op jit(solution)/shard_map/ppermute | solution.py:360
  62.4 8.2 %collective-permute-start.29 = (bf16[4,128,128]{2,1,0:T(8,128)(2,1)S(1)}, bf16[4,128,128]{2,1,0:T(8,128)(2,1)S(1)}, u32[]{:S(2)}, u32[]{:S(2)}) collective-permute-start(bf16[4,128,128]{2,1,0:T(8,128)(2,1)S(1)} %get-tuple-element.84), channel_id=1, source_target_pairs={{0,4},{1,5},{2,6},{3,7},{4,0},{5,1},{6,2},{7,3},{8,12},{9,13},{10,... | collective-permute-start | bytes 393224 | tf_op jit(solution)/shard_map/ppermute | solution.py:360
  63.5 7.1 %collective-permute-start.28 = (bf16[4,128,128]{2,1,0:T(8,128)(2,1)S(1)}, bf16[4,128,128]{2,1,0:T(8,128)(2,1)S(1)}, u32[]{:S(2)}, u32[]{:S(2)}) collective-permute-start(bf16[4,128,128]{2,1,0:T(8,128)(2,1)S(1)} %get-tuple-element.84), channel_id=1, source_target_pairs={{0,2},{1,3},{2,0},{3,1},{4,6},{5,7},{6,4},{7,5},{8,10},{9,11},{10,... | collective-permute-start | bytes 393224 | tf_op jit(solution)/shard_map/ppermute | solution.py:360
  64.2 6.5 %collective-permute-start.27 = (bf16[4,128,128]{2,1,0:T(8,128)(2,1)S(1)}, bf16[4,128,128]{2,1,0:T(8,128)(2,1)S(1)}, u32[]{:S(2)}, u32[]{:S(2)}) collective-permute-start(bf16[4,128,128]{2,1,0:T(8,128)(2,1)S(1)} %get-tuple-element.84), channel_id=1, source_target_pairs={{0,1},{1,0},{2,3},{3,2},{4,5},{5,4},{6,7},{7,6},{8,9},{9,8},{10,11... | collective-permute-start | bytes 393224 | tf_op jit(solution)/shard_map/ppermute | solution.py:360
  65.1 7.1 %collective-permute-start.31 = (bf16[8,128,128]{2,1,0:T(8,128)(2,1)S(1)}, bf16[8,128,128]{2,1,0:T(8,128)(2,1)S(1)}, u32[]{:S(2)}, u32[]{:S(2)}) collective-permute-start(bf16[8,128,128]{2,1,0:T(8,128)(2,1)S(1)} %get-tuple-element.88), channel_id=1, source_target_pairs={{0,16},{8,24},{16,0},{24,8},{1,17},{9,25},{17,1},{25,9},{2,18},{10... | collective-permute-start | bytes 786440 | tf_op jit(solution)/shard_map/ppermute | solution.py:364
  70.7 9.7 %collective-permute-start.34 = (bf16[6,128,128]{2,1,0:T(8,128)(2,1)S(1)}, bf16[6,128,128]{2,1,0:T(8,128)(2,1)S(1)}, u32[]{:S(2)}, u32[]{:S(2)}) collective-permute-start(bf16[6,128,128]{2,1,0:T(8,128)(2,1)S(1)} %get-tuple-element.93), channel_id=1, source_target_pairs={{0,2},{1,3},{2,0},{3,1},{4,6},{5,7},{6,4},{7,5},{8,10},{9,11},{10,... | collective-permute-start | bytes 589832 | tf_op jit(solution)/shard_map/ppermute | solution.py:360
  70.8 9.5 %collective-permute-start.33 = (bf16[6,128,128]{2,1,0:T(8,128)(2,1)S(1)}, bf16[6,128,128]{2,1,0:T(8,128)(2,1)S(1)}, u32[]{:S(2)}, u32[]{:S(2)}) collective-permute-start(bf16[6,128,128]{2,1,0:T(8,128)(2,1)S(1)} %get-tuple-element.94), channel_id=1, source_target_pairs={{0,1},{1,0},{2,3},{3,2},{4,5},{5,4},{6,7},{7,6},{8,9},{9,8},{10,11... | collective-permute-start | bytes 589832 | tf_op jit(solution)/shard_map/ppermute | solution.py:360
  71.8 3.1 %collective-permute-start.30 = (bf16[4,128,128]{2,1,0:T(8,128)(2,1)S(1)}, bf16[4,128,128]{2,1,0:T(8,128)(2,1)S(1)}, u32[]{:S(2)}, u32[]{:S(2)}) collective-permute-start(bf16[4,128,128]{2,1,0:T(8,128)(2,1)S(1)} %get-tuple-element.87), channel_id=1, source_target_pairs={{0,8},{8,0},{16,24},{24,16},{1,9},{9,1},{17,25},{25,17},{2,10},{10... | collective-permute-start | bytes 393224 | tf_op jit(solution)/shard_map/ppermute | solution.py:364
  72.2 2.7 %collective-permute-start.32 = (bf16[4,128,128]{2,1,0:T(8,128)(2,1)S(1)}, bf16[4,128,128]{2,1,0:T(8,128)(2,1)S(1)}, u32[]{:S(2)}, u32[]{:S(2)}) collective-permute-start(bf16[4,128,128]{2,1,0:T(8,128)(2,1)S(1)} %slice.51), channel_id=1, source_target_pairs={{0,8},{8,0},{16,24},{24,16},{1,9},{9,1},{17,25},{25,17},{2,10},{10... | collective-permute-start | bytes 393224 | tf_op jit(solution)/shard_map/ppermute | solution.py:364
  72.4 8.0 %collective-permute-start.35 = (bf16[4,128,128]{2,1,0:T(8,128)(2,1)S(1)}, bf16[4,128,128]{2,1,0:T(8,128)(2,1)S(1)}, u32[]{:S(2)}, u32[]{:S(2)}) collective-permute-start(bf16[4,128,128]{2,1,0:T(8,128)(2,1)S(1)} %collective-permute-done.29.rest_0_), channel_id=1, source_target_pairs={{0,3},{1,2},{2,1},{3,0},{4,7},{5,6},{6,5},{7,4},{8,11},{9,10},{10,... | collective-permute-start | bytes 393224 | tf_op jit(solution)/shard_map/ppermute | solution.py:360
